TPU v7x, 32 devices: a whole 2x2x4 slice. The times are simulated.
32 devices in a mesh: segment: 2 (over y), blk: 16 (over z, x, core).
Axes of the slice: x: 2, y: 2, z: 4, core: 2. Of those that a mesh axis runs over, the one named last changes fastest.
Arguments:
- inputs: bfloat16 [2, 128, 128, 256], P(None, 'blk'), may hold values from -6 to 6
- first_right: bfloat16 [4, 128, 128, 128], P('segment', 'blk'), may hold values from -0.5 to 0.5
- first_left: bfloat16 [4, 128, 128, 128], P('segment', 'blk'), may hold values from -0.5 to 0.5
- second_right: bfloat16 [4, 128, 128, 128], P('segment', 'blk'), may hold values from -0.5 to 0.5
- second_left: bfloat16 [4, 128, 128, 128], P('segment', 'blk'), may hold values from -0.5 to 0.5
- cotangent: bfloat16 [2, 128, 128, 256], P(None, 'blk'), may hold values from -6 to 6
- sections: int32 [2], replicated, may hold values from 1 to 2, as said below
Outputs:
- grad_first_right: float32 [4, 128, 128, 128], P('segment', 'blk')
- grad_first_left: float32 [4, 128, 128, 128], P('segment', 'blk')
- grad_second_right: float32 [4, 128, 128, 128], P('segment', 'blk')
- grad_second_left: float32 [4, 128, 128, 128], P('segment', 'blk')
Inputs may be any that keep to these rules, and one draw needn't show every extreme that they name: Segment s runs its first sections[s] layer slots; at least one segment runs all 2 and at least one runs a single one.
All inputs are finite; a program needn't handle non-finite values.
Results may differ from a plain program's by a relative error of at most 0.019.
Values may be sent and summed in bfloat16 or wider, within the bound.
No kernel may reach another device: no remote copies, remote signals or barrier semaphores. Data moves between devices by JAX's collectives and lax.ppermute only.
A program may use at most 64 MiB of HBM per device.

v0:
```python
import jax
import jax.numpy as jnp
from jax import lax
from jax.sharding import PartitionSpec as P


def shifted(value, axis, steps):
    count = lax.axis_size(axis)
    leading, last = (max(0, -steps), min(count, count - steps))
    return lax.ppermute(value, axis, [(source, source + steps) for source in range(leading, last)])


def factor(weight, values):
    return jnp.einsum("bij,bit->bjt", weight, values, preferred_element_type=jnp.float32)


def monarch_forward(right, left, values):
    mixed = factor(right, values).astype(jnp.bfloat16)
    permuted = jnp.swapaxes(
        lax.all_to_all(mixed, "blk", split_axis=1, concat_axis=0, tiled=True), 0, 1
    )
    outer = jnp.einsum("jbk,jbt->jkt", left, permuted, preferred_element_type=jnp.float32).astype(
        jnp.bfloat16
    )
    returned = lax.all_to_all(outer, "blk", split_axis=1, concat_axis=0, tiled=True)
    return (permuted, jnp.swapaxes(returned, 0, 1))


def monarch_backward(right, left, values, permuted, grad_out):
    grad_c = jnp.swapaxes(
        lax.all_to_all(grad_out, "blk", split_axis=1, concat_axis=0, tiled=True), 0, 1
    )
    grad_p = jnp.einsum("jbk,jkt->jbt", left, grad_c, preferred_element_type=jnp.float32).astype(
        jnp.bfloat16
    )
    returned = lax.all_to_all(grad_p, "blk", split_axis=1, concat_axis=0, tiled=True)
    grad_c, grad_a = (grad_c, jnp.swapaxes(returned, 0, 1))
    grad_left = jnp.einsum("jbt,jkt->jbk", permuted, grad_c, preferred_element_type=jnp.float32)
    grad_right = jnp.einsum("bit,bjt->bij", values, grad_a, preferred_element_type=jnp.float32)
    grad_in = jnp.einsum("bij,bjt->bit", right, grad_a, preferred_element_type=jnp.float32)
    return (grad_in, grad_right, grad_left)


def layer_forward(weights, state):
    p_one, upper = monarch_forward(weights[0], weights[1], state)
    hidden = jax.nn.gelu(upper.astype(jnp.float32)).astype(jnp.bfloat16)
    p_two, branch = monarch_forward(weights[2], weights[3], hidden)
    result = (state.astype(jnp.float32) + branch.astype(jnp.float32)).astype(jnp.bfloat16)
    return (result, (state, p_one, upper, p_two))


def layer_backward(weights, kept, grad):
    state_in, p_one, upper, p_two = kept
    upper_f = upper.astype(jnp.float32)
    hidden = jax.nn.gelu(upper_f).astype(jnp.bfloat16)
    grad_h, g_r2, g_l2 = monarch_backward(weights[2], weights[3], hidden, p_two, grad)
    grad_u = jax.vjp(jax.nn.gelu, upper_f)[1](grad_h)[0].astype(jnp.bfloat16)
    grad_x, g_r1, g_l1 = monarch_backward(weights[0], weights[1], state_in, p_one, grad_u)
    new_grad = (grad.astype(jnp.float32) + grad_x).astype(jnp.bfloat16)
    return (new_grad, (g_r1, g_l1, g_r2, g_l2))


def store(buffer, value, micro, slot, valid):
    old = buffer[micro, slot]
    return buffer.at[micro, slot].set(jnp.where(valid, value, old))


def shards(inputs, first_right, first_left, second_right, second_left, cotangent, sections):
    segments = lax.axis_size("segment")
    segment = lax.axis_index("segment")
    micros = inputs.shape[0]
    slots = first_right.shape[0]
    ticks = micros + segments - 1
    count = jnp.sum(jnp.where(jnp.arange(segments) == segment, sections, 0))
    all_weights = (first_right, first_left, second_right, second_left)
    shard = inputs.shape[1:]
    kinds = 4
    buffers = tuple((jnp.zeros((micros, slots) + shard, jnp.bfloat16) for index in range(kinds)))

    def forward_tick(tick, carry):
        received, saved = carry
        micro = tick - segment
        valid = (micro >= 0) & (micro < micros)
        clipped = jnp.clip(micro, 0, micros - 1)
        first = lax.dynamic_index_in_dim(inputs, clipped, 0, keepdims=False)
        current = jnp.where(segment == 0, first, received)
        saved = list(saved)
        for slot in range(slots):
            weights = tuple((w[slot] for w in all_weights))
            result, kept = layer_forward(weights, current)
            for index in range(kinds):
                saved[index] = store(saved[index], kept[index], clipped, slot, valid)
            current = jnp.where(slot < count, result, current)
        received = shifted(current, "segment", 1)
        return (received, tuple(saved))

    start = jnp.zeros(shard, jnp.bfloat16)
    ignored, buffers = lax.fori_loop(0, ticks, forward_tick, (start, buffers))
    totals = tuple((jnp.zeros(first_right.shape, jnp.float32) for index in range(4)))

    def backward_tick(tick, carry):
        received, sums = carry
        micro = tick - (segments - 1 - segment)
        valid = (micro >= 0) & (micro < micros)
        clipped = jnp.clip(micro, 0, micros - 1)
        last = lax.dynamic_index_in_dim(cotangent, clipped, 0, keepdims=False)
        current = jnp.where(segment == segments - 1, last, received)
        sums = list(sums)
        for slot in reversed(range(slots)):
            weights = tuple((w[slot] for w in all_weights))
            kept = tuple((buffers[index][clipped, slot] for index in range(4)))
            new_grad, parts = layer_backward(weights, kept, current)
            active = slot < count
            taken = valid & active
            for index in range(4):
                sums[index] = sums[index].at[slot].add(jnp.where(taken, parts[index], 0.0))
            current = jnp.where(active, new_grad, current)
        received = shifted(current, "segment", -1)
        return (received, tuple(sums))

    ignored, totals = lax.fori_loop(0, ticks, backward_tick, (start, totals))
    return (totals[0], totals[1], totals[2], totals[3])


def solution(mesh):
    in_specs = (
        P(None, "blk", None, None),
        P("segment", "blk", None, None),
        P("segment", "blk", None, None),
        P("segment", "blk", None, None),
        P("segment", "blk", None, None),
        P(None, "blk", None, None),
        P(),
    )
    out_specs = (
        P("segment", "blk", None, None),
        P("segment", "blk", None, None),
        P("segment", "blk", None, None),
        P("segment", "blk", None, None),
    )
    return jax.shard_map(shards, mesh=mesh, in_specs=in_specs, out_specs=out_specs, check_vma=False)
```

profile of v0, /device:TPU:0, one launch (start us, length us, event | category | flops | bytes accessed | tf_op | source)
XLA Modules:
  0.0 1220.4 jit_solution(2317167860093061009)
XLA Ops:
  10.6 602.4 %while.63 = (s32[]{:T(128)}, bf16[8,128,256]{1,2,0:T(8,128)(2,1)S(1)}, bf16[2,2,8,128,256]{3,4,2,1,0:T(8,128)(2,1)}, bf16[2,2,8,128,256]{3,4,2,1,0:T(8,128)(2,1)...) while((s32[]{:T(128)}, ...), condition=%wide.region_4.5_spmd, body=%wide.region_1.4_spmd.sunk | while | flops 551288896 | bytes 99624712 | solution.py:98
  17.3 21.6 %all_to_all.692 = bf16[8,128,256]{2,0,1:T(8,128)(2,1)S(1)} all-to-all(bf16[8,128,256]{2,0,1:T(8,128)(2,1)S(1)} %copy.307), channel_id=1, replica_groups=mesh['segment'=2,'blk'=16] {'blk'}, dimensions={1} | all-to-all | bytes 1048576 | tf_op jit(solution)/shard_map/while/body/eval_jaxpr/all_to_all | solution.py:20
  62.1 18.4 %all_to_all.694 = bf16[8,128,256]{2,0,1:T(8,128)(2,1)S(1)} all-to-all(bf16[8,128,256]{2,0,1:T(8,128)(2,1)S(1)} %copy.313), channel_id=1, replica_groups=mesh['segment'=2,'blk'=16] {'blk'}, dimensions={1} | all-to-all | bytes 1048576 | tf_op jit(solution)/shard_map/while/body/eval_jaxpr/all_to_all | solution.py:20
  107.5 18.4 %all_to_all.695 = bf16[8,128,256]{2,0,1:T(8,128)(2,1)S(1)} all-to-all(bf16[8,128,256]{2,0,1:T(8,128)(2,1)S(1)} %copy.319), channel_id=1, replica_groups=mesh['segment'=2,'blk'=16] {'blk'}, dimensions={1} | all-to-all | bytes 1048576 | tf_op jit(solution)/shard_map/while/body/eval_jaxpr/all_to_all | solution.py:20
  128.1 18.4 %all_to_all.696 = bf16[8,128,256]{2,0,1:T(8,128)(2,1)S(1)} all-to-all(bf16[8,128,256]{2,0,1:T(8,128)(2,1)S(1)} %copy.322), channel_id=1, replica_groups=mesh['segment'=2,'blk'=16] {'blk'}, dimensions={1} | all-to-all | bytes 1048576 | tf_op jit(solution)/shard_map/while/body/eval_jaxpr/all_to_all | solution.py:25
  219.5 18.6 %all_to_all.692 = bf16[8,128,256]{2,0,1:T(8,128)(2,1)S(1)} all-to-all(bf16[8,128,256]{2,0,1:T(8,128)(2,1)S(1)} %copy.307), channel_id=1, replica_groups=mesh['segment'=2,'blk'=16] {'blk'}, dimensions={1} | all-to-all | bytes 1048576 | tf_op jit(solution)/shard_map/while/body/eval_jaxpr/all_to_all | solution.py:20
  240.3 18.4 %all_to_all.693 = bf16[8,128,256]{2,0,1:T(8,128)(2,1)S(1)} all-to-all(bf16[8,128,256]{2,0,1:T(8,128)(2,1)S(1)} %copy.310), channel_id=1, replica_groups=mesh['segment'=2,'blk'=16] {'blk'}, dimensions={1} | all-to-all | bytes 1048576 | tf_op jit(solution)/shard_map/while/body/eval_jaxpr/all_to_all | solution.py:25
  306.6 18.4 %all_to_all.695 = bf16[8,128,256]{2,0,1:T(8,128)(2,1)S(1)} all-to-all(bf16[8,128,256]{2,0,1:T(8,128)(2,1)S(1)} %copy.319), channel_id=1, replica_groups=mesh['segment'=2,'blk'=16] {'blk'}, dimensions={1} | all-to-all | bytes 1048576 | tf_op jit(solution)/shard_map/while/body/eval_jaxpr/all_to_all | solution.py:20
  419.6 18.6 %all_to_all.692 = bf16[8,128,256]{2,0,1:T(8,128)(2,1)S(1)} all-to-all(bf16[8,128,256]{2,0,1:T(8,128)(2,1)S(1)} %copy.307), channel_id=1, replica_groups=mesh['segment'=2,'blk'=16] {'blk'}, dimensions={1} | all-to-all | bytes 1048576 | tf_op jit(solution)/shard_map/while/body/eval_jaxpr/all_to_all | solution.py:20
  506.7 18.4 %all_to_all.695 = bf16[8,128,256]{2,0,1:T(8,128)(2,1)S(1)} all-to-all(bf16[8,128,256]{2,0,1:T(8,128)(2,1)S(1)} %copy.319), channel_id=1, replica_groups=mesh['segment'=2,'blk'=16] {'blk'}, dimensions={1} | all-to-all | bytes 1048576 | tf_op jit(solution)/shard_map/while/body/eval_jaxpr/all_to_all | solution.py:20
  629.1 591.3 %while.64 = (s32[]{:T(128)}, bf16[8,128,256]{1,2,0:T(8,128)(2,1)}, f32[2,8,128,128]{3,2,1,0:T(8,128)}, f32[2,8,128,128]{3,2,1,0:T(8,128)}, f32[2,8,128,128]{3,2,...) while((s32[]{:T(128)}, bf16[8,128,256]{1,2,0:T(8,128)(2,1)}, ...), condition=%wide.region_6.7_spmd, body=%wide.region_5.6_spmd.sunk | while | flops 1095499776 | bytes 109577424 | solution.py:121
  632.0 18.6 %all_to_all.697 = bf16[8,128,256]{2,0,1:T(8,128)(2,1)S(1)} all-to-all(bf16[8,128,256]{2,0,1:T(8,128)(2,1)S(1)} %copy.340), channel_id=1, replica_groups=mesh['segment'=2,'blk'=16] {'blk'}, dimensions={1} | all-to-all | bytes 1048576 | tf_op jit(solution)/shard_map/while/body/eval_jaxpr/all_to_all | solution.py:31
  652.7 18.4 %all_to_all.698 = bf16[8,128,256]{2,0,1:T(8,128)(2,1)S(1)} all-to-all(bf16[8,128,256]{2,0,1:T(8,128)(2,1)S(1)} %copy.343), channel_id=1, replica_groups=mesh['segment'=2,'blk'=16] {'blk'}, dimensions={1} | all-to-all | bytes 1048576 | tf_op jit(solution)/shard_map/while/body/eval_jaxpr/all_to_all | solution.py:36
  718.0 18.4 %all_to_all.701 = bf16[8,128,256]{2,0,1:T(8,128)(2,1)S(1)} all-to-all(bf16[8,128,256]{2,0,1:T(8,128)(2,1)S(1)} %copy.352), channel_id=1, replica_groups=mesh['segment'=2,'blk'=16] {'blk'}, dimensions={1} | all-to-all | bytes 1048576 | tf_op jit(solution)/shard_map/while/body/eval_jaxpr/all_to_all | solution.py:31
  829.0 18.6 %all_to_all.697 = bf16[8,128,256]{2,0,1:T(8,128)(2,1)S(1)} all-to-all(bf16[8,128,256]{2,0,1:T(8,128)(2,1)S(1)} %copy.340), channel_id=1, replica_groups=mesh['segment'=2,'blk'=16] {'blk'}, dimensions={1} | all-to-all | bytes 1048576 | tf_op jit(solution)/shard_map/while/body/eval_jaxpr/all_to_all | solution.py:31
  849.9 18.4 %all_to_all.698 = bf16[8,128,256]{2,0,1:T(8,128)(2,1)S(1)} all-to-all(bf16[8,128,256]{2,0,1:T(8,128)(2,1)S(1)} %copy.343), channel_id=1, replica_groups=mesh['segment'=2,'blk'=16] {'blk'}, dimensions={1} | all-to-all | bytes 1048576 | tf_op jit(solution)/shard_map/while/body/eval_jaxpr/all_to_all | solution.py:36
  871.2 18.4 %all_to_all.699 = bf16[8,128,256]{2,0,1:T(8,128)(2,1)S(1)} all-to-all(bf16[8,128,256]{2,0,1:T(8,128)(2,1)S(1)} %copy.346), channel_id=1, replica_groups=mesh['segment'=2,'blk'=16] {'blk'}, dimensions={1} | all-to-all | bytes 1048576 | tf_op jit(solution)/shard_map/while/body/eval_jaxpr/all_to_all | solution.py:31
  891.8 18.4 %all_to_all.700 = bf16[8,128,256]{2,0,1:T(8,128)(2,1)S(1)} all-to-all(bf16[8,128,256]{2,0,1:T(8,128)(2,1)S(1)} %copy.349), channel_id=1, replica_groups=mesh['segment'=2,'blk'=16] {'blk'}, dimensions={1} | all-to-all | bytes 1048576 | tf_op jit(solution)/shard_map/while/body/eval_jaxpr/all_to_all | solution.py:36
  938.4 18.4 %all_to_all.702 = bf16[8,128,256]{2,0,1:T(8,128)(2,1)S(1)} all-to-all(bf16[8,128,256]{2,0,1:T(8,128)(2,1)S(1)} %copy.355), channel_id=1, replica_groups=mesh['segment'=2,'blk'=16] {'blk'}, dimensions={1} | all-to-all | bytes 1048576 | tf_op jit(solution)/shard_map/while/body/eval_jaxpr/all_to_all | solution.py:36
  1026.1 18.6 %all_to_all.697 = bf16[8,128,256]{2,0,1:T(8,128)(2,1)S(1)} all-to-all(bf16[8,128,256]{2,0,1:T(8,128)(2,1)S(1)} %copy.340), channel_id=1, replica_groups=mesh['segment'=2,'blk'=16] {'blk'}, dimensions={1} | all-to-all | bytes 1048576 | tf_op jit(solution)/shard_map/while/body/eval_jaxpr/all_to_all | solution.py:31
  1047.0 18.4 %all_to_all.698 = bf16[8,128,256]{2,0,1:T(8,128)(2,1)S(1)} all-to-all(bf16[8,128,256]{2,0,1:T(8,128)(2,1)S(1)} %copy.343), channel_id=1, replica_groups=mesh['segment'=2,'blk'=16] {'blk'}, dimensions={1} | all-to-all | bytes 1048576 | tf_op jit(solution)/shard_map/while/body/eval_jaxpr/all_to_all | solution.py:36
  1068.3 18.4 %all_to_all.699 = bf16[8,128,256]{2,0,1:T(8,128)(2,1)S(1)} all-to-all(bf16[8,128,256]{2,0,1:T(8,128)(2,1)S(1)} %copy.346), channel_id=1, replica_groups=mesh['segment'=2,'blk'=16] {'blk'}, dimensions={1} | all-to-all | bytes 1048576 | tf_op jit(solution)/shard_map/while/body/eval_jaxpr/all_to_all | solution.py:31
  1088.9 18.4 %all_to_all.700 = bf16[8,128,256]{2,0,1:T(8,128)(2,1)S(1)} all-to-all(bf16[8,128,256]{2,0,1:T(8,128)(2,1)S(1)} %copy.349), channel_id=1, replica_groups=mesh['segment'=2,'blk'=16] {'blk'}, dimensions={1} | all-to-all | bytes 1048576 | tf_op jit(solution)/shard_map/while/body/eval_jaxpr/all_to_all | solution.py:36
  1135.6 18.4 %all_to_all.702 = bf16[8,128,256]{2,0,1:T(8,128)(2,1)S(1)} all-to-all(bf16[8,128,256]{2,0,1:T(8,128)(2,1)S(1)} %copy.355), channel_id=1, replica_groups=mesh['segment'=2,'blk'=16] {'blk'}, dimensions={1} | all-to-all | bytes 1048576 | tf_op jit(solution)/shard_map/while/body/eval_jaxpr/all_to_all | solution.py:36
  (479 shorter events, 808.0 us)
Async XLA Ops:
  83.5 18.6 %all-to-all-start.3 = ((bf16[8,128,256]{2,0,1:T(8,128)(2,1)}), bf16[8,128,256]{2,0,1:T(8,128)(2,1)S(1)}, u32[]{:S(2)}, u32[]{:S(2)}) async-start(bf16[8,128,256]{2,0,1:T(8,128)(2,1)} %copy.316), calls=%async_computation.3 | async-start | bytes 1048576 | tf_op jit(solution)/shard_map/while/body/eval_jaxpr/all_to_all | solution.py:25
  149.8 18.7 %all-to-all-start.6 = ((bf16[8,128,256]{2,0,1:T(8,128)(2,1)}), bf16[8,128,256]{2,0,1:T(8,128)(2,1)}, u32[]{:S(2)}, u32[]{:S(2)}) async-start(bf16[8,128,256]{2,0,1:T(8,128)(2,1)} %copy.325), calls=%async_computation.6 | async-start | bytes 1048576 | tf_op jit(solution)/shard_map/while/body/eval_jaxpr/all_to_all | solution.py:20
  175.3 18.7 %all-to-all-start.7 = ((bf16[8,128,256]{2,0,1:T(8,128)(2,1)}), bf16[8,128,256]{2,0,1:T(8,128)(2,1)}, u32[]{:S(2)}, u32[]{:S(2)}) async-start(bf16[8,128,256]{2,0,1:T(8,128)(2,1)} %copy.328), calls=%async_computation.7 | async-start | bytes 1048576 | tf_op jit(solution)/shard_map/while/body/eval_jaxpr/all_to_all | solution.py:25
  198.1 14.8 %collective-permute-start = (bf16[8,128,256]{1,2,0:T(8,128)(2,1)S(1)}, bf16[8,128,256]{1,2,0:T(8,128)(2,1)S(1)}, u32[]{:S(2)}, u32[]{:S(2)}) collective-permute-start(bf16[8,128,256]{1,2,0:T(8,128)(2,1)S(1)} %fusion.315), channel_id=1, source_target_pairs={{0,16},{1,17},{2,18},{3,19},{4,20},{5,21},{6,22},{7,23},{8,24},{9,... | collective-permute-start | bytes 1572872 | tf_op jit(solution)/shard_map/while/body/eval_jaxpr/ppermute | solution.py:10
  282.6 18.6 %all-to-all-start.3 = ((bf16[8,128,256]{2,0,1:T(8,128)(2,1)}), bf16[8,128,256]{2,0,1:T(8,128)(2,1)S(1)}, u32[]{:S(2)}, u32[]{:S(2)}) async-start(bf16[8,128,256]{2,0,1:T(8,128)(2,1)} %copy.316), calls=%async_computation.3 | async-start | bytes 1048576 | tf_op jit(solution)/shard_map/while/body/eval_jaxpr/all_to_all | solution.py:25
  349.0 18.7 %all-to-all-start.6 = ((bf16[8,128,256]{2,0,1:T(8,128)(2,1)}), bf16[8,128,256]{2,0,1:T(8,128)(2,1)}, u32[]{:S(2)}, u32[]{:S(2)}) async-start(bf16[8,128,256]{2,0,1:T(8,128)(2,1)} %copy.325), calls=%async_computation.6 | async-start | bytes 1048576 | tf_op jit(solution)/shard_map/while/body/eval_jaxpr/all_to_all | solution.py:20
  374.5 18.7 %all-to-all-start.7 = ((bf16[8,128,256]{2,0,1:T(8,128)(2,1)}), bf16[8,128,256]{2,0,1:T(8,128)(2,1)}, u32[]{:S(2)}, u32[]{:S(2)}) async-start(bf16[8,128,256]{2,0,1:T(8,128)(2,1)} %copy.328), calls=%async_computation.7 | async-start | bytes 1048576 | tf_op jit(solution)/shard_map/while/body/eval_jaxpr/all_to_all | solution.py:25
  397.2 15.7 %collective-permute-start = (bf16[8,128,256]{1,2,0:T(8,128)(2,1)S(1)}, bf16[8,128,256]{1,2,0:T(8,128)(2,1)S(1)}, u32[]{:S(2)}, u32[]{:S(2)}) collective-permute-start(bf16[8,128,256]{1,2,0:T(8,128)(2,1)S(1)} %fusion.315), channel_id=1, source_target_pairs={{0,16},{1,17},{2,18},{3,19},{4,20},{5,21},{6,22},{7,23},{8,24},{9,... | collective-permute-start | bytes 1572872 | tf_op jit(solution)/shard_map/while/body/eval_jaxpr/ppermute | solution.py:10
  482.7 18.6 %all-to-all-start.3 = ((bf16[8,128,256]{2,0,1:T(8,128)(2,1)}), bf16[8,128,256]{2,0,1:T(8,128)(2,1)S(1)}, u32[]{:S(2)}, u32[]{:S(2)}) async-start(bf16[8,128,256]{2,0,1:T(8,128)(2,1)} %copy.316), calls=%async_computation.3 | async-start | bytes 1048576 | tf_op jit(solution)/shard_map/while/body/eval_jaxpr/all_to_all | solution.py:25
  549.1 18.7 %all-to-all-start.6 = ((bf16[8,128,256]{2,0,1:T(8,128)(2,1)}), bf16[8,128,256]{2,0,1:T(8,128)(2,1)}, u32[]{:S(2)}, u32[]{:S(2)}) async-start(bf16[8,128,256]{2,0,1:T(8,128)(2,1)} %copy.325), calls=%async_computation.6 | async-start | bytes 1048576 | tf_op jit(solution)/shard_map/while/body/eval_jaxpr/all_to_all | solution.py:20
  574.6 18.7 %all-to-all-start.7 = ((bf16[8,128,256]{2,0,1:T(8,128)(2,1)}), bf16[8,128,256]{2,0,1:T(8,128)(2,1)}, u32[]{:S(2)}, u32[]{:S(2)}) async-start(bf16[8,128,256]{2,0,1:T(8,128)(2,1)} %copy.328), calls=%async_computation.7 | async-start | bytes 1048576 | tf_op jit(solution)/shard_map/while/body/eval_jaxpr/all_to_all | solution.py:25
  597.3 15.7 %collective-permute-start = (bf16[8,128,256]{1,2,0:T(8,128)(2,1)S(1)}, bf16[8,128,256]{1,2,0:T(8,128)(2,1)S(1)}, u32[]{:S(2)}, u32[]{:S(2)}) collective-permute-start(bf16[8,128,256]{1,2,0:T(8,128)(2,1)S(1)} %fusion.315), channel_id=1, source_target_pairs={{0,16},{1,17},{2,18},{3,19},{4,20},{5,21},{6,22},{7,23},{8,24},{9,... | collective-permute-start | bytes 1572872 | tf_op jit(solution)/shard_map/while/body/eval_jaxpr/ppermute | solution.py:10
  716.5 21.2 %copy-start.1 = (bf16[2,8,128,128]{3,2,1,0:T(8,128)(2,1)S(1)}, bf16[2,8,128,128]{3,2,1,0:T(8,128)(2,1)}, u32[]{:S(2)}) copy-start(bf16[2,8,128,128]{3,2,1,0:T(8,128)(2,1)} %get-tuple-element.1662) | copy-start | bytes 1572868 | tf_op jit(solution)/shard_map/while
  766.2 18.7 %all-to-all-start.14 = ((bf16[8,128,256]{2,0,1:T(8,128)(2,1)}), bf16[8,128,256]{2,0,1:T(8,128)(2,1)}, u32[]{:S(2)}, u32[]{:S(2)}) async-start(bf16[8,128,256]{2,0,1:T(8,128)(2,1)} %copy.358), calls=%async_computation.14 | async-start | bytes 1048576 | tf_op jit(solution)/shard_map/while/body/eval_jaxpr/all_to_all | solution.py:31
  789.8 18.5 %all-to-all-start.15 = ((bf16[8,128,256]{2,0,1:T(8,128)(2,1)}), bf16[8,128,256]{2,0,1:T(8,128)(2,1)S(1)}, u32[]{:S(2)}, u32[]{:S(2)}) async-start(bf16[8,128,256]{2,0,1:T(8,128)(2,1)} %copy.361), calls=%async_computation.15 | async-start | bytes 1048576 | tf_op jit(solution)/shard_map/while/body/eval_jaxpr/all_to_all | solution.py:36
  810.3 15.8 %collective-permute-start.1 = (bf16[8,128,256]{1,2,0:T(8,128)(2,1)S(1)}, bf16[8,128,256]{1,2,0:T(8,128)(2,1)}, u32[]{:S(2)}, u32[]{:S(2)}) collective-permute-start(bf16[8,128,256]{1,2,0:T(8,128)(2,1)S(1)} %fusion.361), channel_id=1, source_target_pairs={{16,0},{17,1},{18,2},{19,3},{20,4},{21,5},{22,6},{23,7},{24,8},{25... | collective-permute-start | bytes 1572872 | tf_op jit(solution)/shard_map/while/body/eval_jaxpr/ppermute | solution.py:10
  913.7 21.2 %copy-start.1 = (bf16[2,8,128,128]{3,2,1,0:T(8,128)(2,1)S(1)}, bf16[2,8,128,128]{3,2,1,0:T(8,128)(2,1)}, u32[]{:S(2)}) copy-start(bf16[2,8,128,128]{3,2,1,0:T(8,128)(2,1)} %get-tuple-element.1662) | copy-start | bytes 1572868 | tf_op jit(solution)/shard_map/while
  963.3 18.7 %all-to-all-start.14 = ((bf16[8,128,256]{2,0,1:T(8,128)(2,1)}), bf16[8,128,256]{2,0,1:T(8,128)(2,1)}, u32[]{:S(2)}, u32[]{:S(2)}) async-start(bf16[8,128,256]{2,0,1:T(8,128)(2,1)} %copy.358), calls=%async_computation.14 | async-start | bytes 1048576 | tf_op jit(solution)/shard_map/while/body/eval_jaxpr/all_to_all | solution.py:31
  987.0 18.5 %all-to-all-start.15 = ((bf16[8,128,256]{2,0,1:T(8,128)(2,1)}), bf16[8,128,256]{2,0,1:T(8,128)(2,1)S(1)}, u32[]{:S(2)}, u32[]{:S(2)}) async-start(bf16[8,128,256]{2,0,1:T(8,128)(2,1)} %copy.361), calls=%async_computation.15 | async-start | bytes 1048576 | tf_op jit(solution)/shard_map/while/body/eval_jaxpr/all_to_all | solution.py:36
  1007.4 15.8 %collective-permute-start.1 = (bf16[8,128,256]{1,2,0:T(8,128)(2,1)S(1)}, bf16[8,128,256]{1,2,0:T(8,128)(2,1)}, u32[]{:S(2)}, u32[]{:S(2)}) collective-permute-start(bf16[8,128,256]{1,2,0:T(8,128)(2,1)S(1)} %fusion.361), channel_id=1, source_target_pairs={{16,0},{17,1},{18,2},{19,3},{20,4},{21,5},{22,6},{23,7},{24,8},{25... | collective-permute-start | bytes 1572872 | tf_op jit(solution)/shard_map/while/body/eval_jaxpr/ppermute | solution.py:10
  1110.8 21.2 %copy-start.1 = (bf16[2,8,128,128]{3,2,1,0:T(8,128)(2,1)S(1)}, bf16[2,8,128,128]{3,2,1,0:T(8,128)(2,1)}, u32[]{:S(2)}) copy-start(bf16[2,8,128,128]{3,2,1,0:T(8,128)(2,1)} %get-tuple-element.1662) | copy-start | bytes 1572868 | tf_op jit(solution)/shard_map/while
  1160.4 18.7 %all-to-all-start.14 = ((bf16[8,128,256]{2,0,1:T(8,128)(2,1)}), bf16[8,128,256]{2,0,1:T(8,128)(2,1)}, u32[]{:S(2)}, u32[]{:S(2)}) async-start(bf16[8,128,256]{2,0,1:T(8,128)(2,1)} %copy.358), calls=%async_computation.14 | async-start | bytes 1048576 | tf_op jit(solution)/shard_map/while/body/eval_jaxpr/all_to_all | solution.py:31
  1184.1 18.5 %all-to-all-start.15 = ((bf16[8,128,256]{2,0,1:T(8,128)(2,1)}), bf16[8,128,256]{2,0,1:T(8,128)(2,1)S(1)}, u32[]{:S(2)}, u32[]{:S(2)}) async-start(bf16[8,128,256]{2,0,1:T(8,128)(2,1)} %copy.361), calls=%async_computation.15 | async-start | bytes 1048576 | tf_op jit(solution)/shard_map/while/body/eval_jaxpr/all_to_all | solution.py:36
  1204.5 15.8 %collective-permute-start.1 = (bf16[8,128,256]{1,2,0:T(8,128)(2,1)S(1)}, bf16[8,128,256]{1,2,0:T(8,128)(2,1)}, u32[]{:S(2)}, u32[]{:S(2)}) collective-permute-start(bf16[8,128,256]{1,2,0:T(8,128)(2,1)S(1)} %fusion.361), channel_id=1, source_target_pairs={{16,0},{17,1},{18,2},{19,3},{20,4},{21,5},{22,6},{23,7},{24,8},{25... | collective-permute-start | bytes 1572872 | tf_op jit(solution)/shard_map/while/body/eval_jaxpr/ppermute | solution.py:10
  (56 other events, 304.9 us)
where the time goes:
time: 1230 us; the launch traced here: 1220 us
  blocking collectives  611 us (50%)
  waiting for transfers between devices  180 us (15%)
  local copies, waits for them, and re-layouts  168 us (14%)
  matrix products  121 us (10%)
  starting transfers between devices  78.8 us (6%)
  other arithmetic  57.6 us (5%)
    all_to_all x9, blocking collectives, monarch_forward(): lax.all_to_all(mixed, 'blk', split_axis=1, concat_axis=0, tiled=True)  169 us
    all_to_all x9, blocking collectives, monarch_backward(): lax.all_to_all(grad_out, 'blk', split_axis=1, concat_axis=0, tiled=True)  166 us
    all_to_all x9, blocking collectives, monarch_backward(): lax.all_to_all(grad_p, 'blk', split_axis=1, concat_axis=0, tiled=True)  165 us
    all_to_all x6, blocking collectives, monarch_forward(): lax.all_to_all(outer, 'blk', split_axis=1, concat_axis=0, tiled=True)  110 us
    ppermute x6, waiting for transfers between devices, shifted(): lax.ppermute(value, axis, [(source, source + steps) for source in range(l...  58.4 us
    all_to_all x6, waiting for transfers between devices, monarch_forward(): lax.all_to_all(outer, 'blk', split_axis=1, concat_axis=0, tiled=True)  54.5 us
    scatter x24, other arithmetic, store(): return buffer.at[micro, slot].set(jnp.where(valid, value, old))  46.8 us
    dynamic_slice x21, local copies, waits for them, and re-layouts, store(): old = buffer[micro, slot]  33 us
  transfers between devices with their start and end apart: 21, of which 21 were waited for; matrix products, arithmetic and copies ran while one was open for 9% of the time, Pallas kernels for 0%

commit v1 on v0

v1 whole, which is shorter than its diff:
```python
import functools
import math

import jax
import jax.numpy as jnp
from jax import lax
from jax.experimental import pallas as pl
from jax.experimental.pallas import tpu as pltpu
from jax.sharding import PartitionSpec as P

F32 = jnp.float32
BF16 = jnp.bfloat16
ROOT = math.sqrt(2.0 / math.pi)


def gelu(u):
    return 0.5 * u * (1.0 + jnp.tanh(ROOT * (u + 0.044715 * (u * u * u))))


def gelu_slope(u):
    square = u * u
    th = jnp.tanh(ROOT * (u + 0.044715 * (u * square)))
    inner = ROOT * (1.0 + 3 * 0.044715 * square)
    return 0.5 * (1.0 + th) + 0.5 * u * (1.0 - th * th) * inner


class Plan:
    def __init__(self, segments, devices, micros, blocks, tokens):
        self.segments = segments
        self.halves = 2 if micros * tokens >= 256 * segments and devices % 2 == 0 else 1
        self.group = devices // self.halves
        self.own = blocks // devices
        self.held = self.own * self.halves
        self.size = blocks
        self.tokens = micros * tokens // (segments * self.halves)
        self.kernels = segments == 2 and self.own % 8 == 0 and self.held % 16 == 0
        self.kernels = self.kernels and self.tokens % 128 == 0
        self.groups = None
        if self.halves > 1:
            self.groups = [
                [half * self.group + rank for rank in range(self.group)]
                for half in range(self.halves)
            ]

    def packed_shape(self):
        return (self.group, self.held, self.held, self.tokens)

    def natural_shape(self):
        return (self.held, self.size, self.tokens)

    def pack(self, values):
        split = values.reshape(self.held, self.halves, self.group, self.own, self.tokens)
        return split.transpose(2, 1, 3, 0, 4).reshape(self.packed_shape())

    def unpack(self, packed):
        split = packed.reshape(self.group, self.held, self.halves, self.own, self.tokens)
        return split.transpose(1, 2, 0, 3, 4).reshape(self.natural_shape())

    def exchange(self, packed):
        return lax.all_to_all(packed, "blk", 0, 0, axis_index_groups=self.groups, tiled=True)

    def swap_halves(self, value):
        devices = self.group * self.halves
        return lax.ppermute(
            value, "blk", [(at, (at + self.group) % devices) for at in range(devices)]
        )


def matmul(a, b, over_a, over_b):
    return lax.dot_general(a, b, (((over_a,), (over_b,)), ((), ())), preferred_element_type=F32)


def read_natural(plan, ref, block):
    values = ref[:, block].astype(F32)
    rows = [
        values[rank, half * plan.own : (half + 1) * plan.own]
        for half in range(plan.halves)
        for rank in range(plan.group)
    ]
    return jnp.concatenate(rows, axis=0)


def write_packed(plan, scratch, out):
    step = plan.group * plan.own * plan.held
    for half in range(plan.halves):
        rows = scratch[half * step : (half + 1) * step, :].astype(BF16)
        out[:, half * plan.own : (half + 1) * plan.own] = rows.reshape(
            plan.group, plan.own, plan.held, plan.tokens
        )


def scatter(plan, scratch, block, values):
    scratch[pl.ds(block, plan.size, stride=plan.held), :] = values


def call(plan, body, ins, outs, scratch, flops):
    shapes = [jax.ShapeDtypeStruct(shape, dtype) for shape, dtype in outs]
    volume = sum(math.prod(i.shape) * i.dtype.itemsize for i in ins)
    volume += sum(math.prod(s.shape) * s.dtype.itemsize for s in shapes)
    vmem = pl.BlockSpec(memory_space=pltpu.VMEM)
    return pl.pallas_call(
        functools.partial(body, plan),
        out_shape=shapes,
        in_specs=[vmem] * len(ins),
        out_specs=[vmem] * len(shapes),
        scratch_shapes=[pltpu.VMEM((plan.size * plan.held, plan.tokens), F32)] if scratch else [],
        compiler_params=pltpu.CompilerParams(vmem_limit_bytes=32 * 1024 * 1024),
        cost_estimate=pl.CostEstimate(flops=flops, bytes_accessed=volume, transcendentals=0),
    )(*ins)


def first_body(plan, state, weight, out, scratch):
    for block in range(plan.held):
        scatter(plan, scratch, block, matmul(weight[block], state[block], 0, 0))
    write_packed(plan, scratch, out)


def residual_body(plan, state, branch, weight, out, result, scratch):
    for block in range(plan.held):
        total = state[block].astype(F32) + read_natural(plan, branch, block)
        total = total.astype(BF16)
        result[block] = total
        scatter(plan, scratch, block, matmul(weight[block], total, 0, 0))
    write_packed(plan, scratch, out)


def left_body(plan, values, weight, out, kept, scratch):
    for block in range(plan.held):
        natural = read_natural(plan, values, block).astype(BF16)
        kept[block] = natural
        scatter(plan, scratch, block, matmul(weight[block], natural, 0, 0))
    write_packed(plan, scratch, out)


def gelu_body(plan, values, weight, out, upper, hidden, scratch):
    for block in range(plan.held):
        natural = read_natural(plan, values, block)
        upper[block] = natural.astype(BF16)
        active = gelu(natural).astype(BF16)
        hidden[block] = active
        scatter(plan, scratch, block, matmul(weight[block], active, 0, 0))
    write_packed(plan, scratch, out)


def pack_body(plan, values, out, scratch):
    for block in range(plan.held):
        scatter(plan, scratch, block, values[block].astype(F32))
    write_packed(plan, scratch, out)


def back_left_body(plan, grad, kept, weight, out, grad_weight, scratch):
    for block in range(plan.held):
        natural = read_natural(plan, grad, block).astype(BF16)
        scatter(plan, scratch, block, matmul(weight[block], natural, 1, 0))
        grad_weight[block] = matmul(kept[block], natural, 1, 1).astype(BF16)
    write_packed(plan, scratch, out)


def back_gelu_body(plan, grad, hidden, upper, weight, out, grad_weight, scratch):
    for block in range(plan.held):
        natural = read_natural(plan, grad, block).astype(BF16)
        grad_hidden = matmul(weight[block], natural, 1, 0)
        scatter(plan, scratch, block, grad_hidden * gelu_slope(upper[block].astype(F32)))
        grad_weight[block] = matmul(hidden[block], natural, 1, 1).astype(BF16)
    write_packed(plan, scratch, out)


def back_right_body(plan, grad, state, above, weight, out, result, grad_weight, scratch):
    for block in range(plan.held):
        natural = read_natural(plan, grad, block).astype(BF16)
        total = matmul(weight[block], natural, 1, 0) + above[block].astype(F32)
        result[block] = total.astype(BF16)
        scatter(plan, scratch, block, total)
        grad_weight[block] = matmul(state[block], natural, 1, 1).astype(BF16)
    write_packed(plan, scratch, out)


def outer_body(plan, grad, state, grad_weight):
    for block in range(plan.held):
        natural = read_natural(plan, grad, block).astype(BF16)
        grad_weight[block] = matmul(state[block], natural, 1, 1).astype(BF16)


def unpack_body(plan, values, out):
    for block in range(plan.held):
        out[block] = read_natural(plan, values, block).astype(BF16)


def apply(weight, values):
    return jnp.einsum("bij,bit->bjt", weight, values, preferred_element_type=F32)


def apply_back(weight, values):
    return jnp.einsum("bij,bjt->bit", weight, values, preferred_element_type=F32)


def outer(values, grad):
    return jnp.einsum("bit,bjt->bij", values, grad, preferred_element_type=F32).astype(BF16)


class Steps:
    def __init__(self, plan):
        self.plan = plan
        self.packed = (plan.packed_shape(), BF16)
        self.natural = (plan.natural_shape(), BF16)
        self.square = ((plan.held, plan.size, plan.size), BF16)
        self.flops = 2 * plan.held * plan.size * plan.size * plan.tokens

    def run(self, body, ins, outs, scratch=True, products=1):
        return call(self.plan, body, ins, outs, scratch, products * self.flops)

    def first(self, state, weight):
        if self.plan.kernels:
            return self.run(first_body, (state, weight), [self.packed])[0]
        return self.plan.pack(apply(weight, state).astype(BF16))

    def residual(self, state, branch, weight, active):
        if self.plan.kernels:
            return self.run(residual_body, (state, branch, weight), [self.packed, self.natural])
        total = (state.astype(F32) + self.plan.unpack(branch).astype(F32)).astype(BF16)
        total = jnp.where(active, total, state)
        return self.plan.pack(apply(weight, total).astype(BF16)), total

    def left(self, values, weight):
        if self.plan.kernels:
            return self.run(left_body, (values, weight), [self.packed, self.natural])
        natural = self.plan.unpack(values)
        return self.plan.pack(apply(weight, natural).astype(BF16)), natural

    def gelu(self, values, weight):
        if self.plan.kernels:
            outs = [self.packed, self.natural, self.natural]
            return self.run(gelu_body, (values, weight), outs)
        upper = self.plan.unpack(values)
        hidden = gelu(upper.astype(F32)).astype(BF16)
        return self.plan.pack(apply(weight, hidden).astype(BF16)), upper, hidden

    def pack(self, values):
        if self.plan.kernels:
            return self.run(pack_body, (values,), [self.packed], products=0)[0]
        return self.plan.pack(values)

    def unpack(self, values):
        if self.plan.kernels:
            return self.run(unpack_body, (values,), [self.natural], False, 0)[0]
        return self.plan.unpack(values)

    def back_left(self, grad, kept, weight):
        if self.plan.kernels:
            outs = [self.packed, self.square]
            return self.run(back_left_body, (grad, kept, weight), outs, products=2)
        natural = self.plan.unpack(grad)
        back = apply_back(weight, natural).astype(BF16)
        return self.plan.pack(back), outer(kept, natural)

    def back_gelu(self, grad, hidden, upper, weight):
        if self.plan.kernels:
            outs = [self.packed, self.square]
            return self.run(back_gelu_body, (grad, hidden, upper, weight), outs, products=2)
        natural = self.plan.unpack(grad)
        back = apply_back(weight, natural) * gelu_slope(upper.astype(F32))
        return self.plan.pack(back.astype(BF16)), outer(hidden, natural)

    def back_right(self, grad, state, above, weight, active):
        if self.plan.kernels:
            outs = [self.packed, self.natural, self.square]
            return self.run(back_right_body, (grad, state, above, weight), outs, products=2)
        natural = self.plan.unpack(grad)
        total = (apply_back(weight, natural) + above.astype(F32)).astype(BF16)
        total = jnp.where(active, total, above)
        return self.plan.pack(total), total, outer(state, natural)

    def outer(self, grad, state):
        if self.plan.kernels:
            return self.run(outer_body, (grad, state), [self.square], False)[0]
        return outer(state, self.plan.unpack(grad))


def spread(plan, factor, owner, half):
    mine = lax.axis_index("segment")
    if plan.segments == 2:
        other = lax.ppermute(factor, "segment", [(0, 1), (1, 0)])
        factor = jnp.where(owner == mine, factor, other)
    else:
        every = lax.all_gather(factor, "segment", axis=0)
        factor = lax.dynamic_index_in_dim(every, owner, 0, keepdims=False)
    if plan.halves == 1:
        return factor
    other = plan.swap_halves(factor)
    lower = jnp.where(half == 0, factor, other)
    upper = jnp.where(half == 0, other, factor)
    return jnp.concatenate([lower, upper], axis=1)


def collect(plan, parts, half):
    if plan.halves == 1:
        total = parts.astype(F32)
    else:
        lower, upper = parts[:, : plan.own], parts[:, plan.own :]
        kept = jnp.where(half == 0, lower, upper)
        other = plan.swap_halves(jnp.where(half == 0, upper, lower))
        total = kept.astype(F32) + other.astype(F32)
    if plan.segments == 2:
        other = lax.ppermute(total.astype(BF16), "segment", [(0, 1), (1, 0)])
        return total + other.astype(F32)
    return lax.psum(total, "segment")


def token_chunk(plan, values, half):
    mine = lax.axis_index("segment")
    per_micro = values.shape[-1] // plan.tokens

    def chunk(at):
        at = mine * plan.halves + at
        micro = lax.dynamic_index_in_dim(values, at // per_micro, 0, keepdims=False)
        start = (at % per_micro) * plan.tokens
        return lax.dynamic_slice_in_dim(micro, start, plan.tokens, 2)

    if plan.halves == 1:
        return chunk(0)
    kept, other = chunk(half), plan.swap_halves(chunk(1 - half))
    lower = jnp.where(half == 0, kept, other)
    upper = jnp.where(half == 0, other, kept)
    return jnp.concatenate([lower, upper], axis=0)


def shards(inputs, first_right, first_left, second_right, second_left, cotangent, sections):
    segments = lax.axis_size("segment")
    segment = lax.axis_index("segment")
    devices = lax.axis_size("blk")
    slots = first_right.shape[0]
    plan = Plan(segments, devices, inputs.shape[0], inputs.shape[2], inputs.shape[3])
    steps = Steps(plan)
    half = lax.axis_index("blk") // plan.group
    factors = (first_right, first_left, second_right, second_left)

    count = segments * slots - 1
    ends = jnp.cumsum(sections)
    layers = []
    for index in range(count):
        owner = jnp.minimum(jnp.sum((index >= ends).astype(jnp.int32)), segments - 1)
        slot = jnp.clip(index - (ends[owner] - sections[owner]), 0, slots - 1)
        layers.append((owner, slot, index < ends[-1]))

    weights = []
    for index, (owner, slot, active) in enumerate(layers):
        picked = [lax.dynamic_index_in_dim(f, slot, 0, keepdims=True) for f in factors]
        if index == 0:
            first = spread(plan, picked[0], owner, half)
            rest = spread(plan, jnp.concatenate(picked[1:], axis=0), owner, half)
            weights.append((first[0], rest[0], rest[1], rest[2]))
        else:
            every = spread(plan, jnp.concatenate(picked, axis=0), owner, half)
            weights.append((every[0], every[1], every[2], every[3]))

    state = token_chunk(plan, inputs, half)
    grad = token_chunk(plan, cotangent, half)

    saved = []
    branch = None
    for index in range(count):
        w = weights[index]
        if index == 0:
            sent = steps.first(state, w[0])
        else:
            sent, state = steps.residual(state, branch, w[0], layers[index - 1][2])
        sent, inner_one = steps.left(plan.exchange(sent), w[1])
        sent, upper, hidden = steps.gelu(plan.exchange(sent), w[2])
        if index < count - 1:
            sent, inner_two = steps.left(plan.exchange(sent), w[3])
            branch = plan.exchange(sent)
        else:
            inner_two = steps.unpack(plan.exchange(sent))
        saved.append((state, inner_one, upper, hidden, inner_two))

    totals = [None] * count
    sent = steps.pack(grad)
    for index in reversed(range(count)):
        w = weights[index]
        state, inner_one, upper, hidden, inner_two = saved[index]
        sent, grad_l2 = steps.back_left(plan.exchange(sent), inner_two, w[3])
        sent, grad_r2 = steps.back_gelu(plan.exchange(sent), hidden, upper, w[2])
        sent, grad_l1 = steps.back_left(plan.exchange(sent), inner_one, w[1])
        if index > 0:
            sent, grad, grad_r1 = steps.back_right(
                plan.exchange(sent), state, grad, w[0], layers[index][2]
            )
            every = collect(plan, jnp.stack([grad_r1, grad_l1, grad_r2, grad_l2]), half)
            totals[index] = (every[0], every[1], every[2], every[3])
        else:
            late = collect(plan, jnp.stack([grad_l1, grad_r2, grad_l2]), half)
            grad_r1 = steps.outer(plan.exchange(sent), state)
            last = collect(plan, grad_r1[None], half)
            totals[index] = (last[0], late[0], late[1], late[2])

    outs = []
    for at in range(4):
        rows = []
        for place in range(slots):
            total = jnp.zeros(first_right.shape[1:], F32)
            for index, (owner, slot, active) in enumerate(layers):
                here = active & (owner == segment) & (slot == place)
                total = jnp.where(here, totals[index][at], total)
            rows.append(total)
        outs.append(jnp.stack(rows))
    return tuple(outs)


def solution(mesh):
    whole = P("segment", "blk", None, None)
    tokens = P(None, "blk", None, None)
    in_specs = (tokens, whole, whole, whole, whole, tokens, P())
    return jax.shard_map(
        shards, mesh=mesh, in_specs=in_specs, out_specs=(whole,) * 4, check_vma=False
    )
```

time: 1230 us -> 603 us (0.49)
  blocking collectives: 611 us -> 150 us
  local copies, waits for them, and re-layouts: 168 us -> 29 us
  matrix products: 121 us -> 0 us
  waiting for transfers between devices: 180 us -> 240 us
  Pallas kernels: 0 us -> 29.6 us
    all_to_all x33 -> x13, blocking collectives: 611 us -> 150 us  [exchange(): lax.all_to_all(packed, 'blk', 0, 0, axis_index_groups=self.groups, tiled=...]
    ppermute x6 -> x18, waiting for transfers between devices: 58.4 us -> 209 us  [the longest x10 173 us: swap_halves(): lax.ppermute(value, 'blk', [(at, (at + self.group) % devices) for at in r...]
    dot_general x72 -> x0, matrix products: 121 us -> none  [the longest x12 25.6 us: monarch_backward(): jnp.einsum('bij,bjt->bit', right, grad_a, preferred_element_type=jnp.floa...]
    all_to_all x15 -> x10, waiting for transfers between devices: 122 us -> 30.5 us  [exchange(): lax.all_to_all(packed, 'blk', 0, 0, axis_index_groups=self.groups, tiled=...]
    convert_element_type x54 -> x0, local copies, waits for them, and re-layouts: 50.8 us -> none  [the longest x12 12.8 us: monarch_forward(): jnp.einsum('jbk,jbt->jkt', left, permuted, preferred_element_type=jnp.flo...]
    scatter x24 -> x0, other arithmetic: 46.8 us -> none  [store(): return buffer.at[micro, slot].set(jnp.where(valid, value, old))]
    all_to_all x84 -> x0, local copies, waits for them, and re-layouts: 43.6 us -> none  [the longest x24 15.1 us: monarch_forward(): lax.all_to_all(mixed, 'blk', split_axis=1, concat_axis=0, tiled=True)]
    dynamic_slice x33 -> x7, local copies, waits for them, and re-layouts: 41.1 us -> 6.68 us  [the longest x4 3.08 us: shards(): lax.dynamic_index_in_dim(f, slot, 0, keepdims=True)]
  transfers between devices with their start and end apart: 21 -> 28, of which waited for: 21 -> 21; matrix products, arithmetic and copies ran while one was open for 9% -> 8% of each run, Pallas kernels for 0% -> 2%
where the time goes in v1:
time: 603 us; the launch traced here: 601 us
  waiting for transfers between devices  240 us (40%)
  blocking collectives  150 us (25%)
  starting transfers between devices  90.5 us (15%)
  other arithmetic  52.9 us (9%)
  Pallas kernels  29.6 us (5%)
  local copies, waits for them, and re-layouts  29 us (5%)
  between operations  8.95 us (1%)
    ppermute x10, waiting for transfers between devices, swap_halves(): lax.ppermute(value, 'blk', [(at, (at + self.group) % devices) for at in r...  173 us
    all_to_all x13, blocking collectives, exchange(): lax.all_to_all(packed, 'blk', 0, 0, axis_index_groups=self.groups, tiled=...  150 us
    all_to_all x10, starting transfers between devices, exchange(): lax.all_to_all(packed, 'blk', 0, 0, axis_index_groups=self.groups, tiled=...  61.8 us
    all_to_all x10, waiting for transfers between devices, exchange(): lax.all_to_all(packed, 'blk', 0, 0, axis_index_groups=self.groups, tiled=...  30.5 us
    pallas_call x25, Pallas kernels, call(): pl.pallas_call(functools.partial(body, plan), out_shape=shapes, in_specs=...  29.6 us
    ppermute x4, waiting for transfers between devices, collect(): other = lax.ppermute(total.astype(BF16), 'segment', [(0, 1), (1, 0)])  22.1 us
    unnamed x148, local copies, waits for them, and re-layouts  21.8 us
    ppermute x10, starting transfers between devices, swap_halves(): lax.ppermute(value, 'blk', [(at, (at + self.group) % devices) for at in r...  20.5 us
  transfers between devices with their start and end apart: 28, of which 21 were waited for; matrix products, arithmetic and copies ran while one was open for 8% of the time, Pallas kernels for 2%

profile of v1, /device:TPU:0, one launch (start us, length us, event | category | flops | bytes accessed | tf_op | source)
XLA Modules:
  0.0 600.9 jit_solution(1118475663200616597)
XLA Ops:
  26.6 13.0 %collective-permute-done.1 = bf16[8,128,128]{2,1,0:T(8,128)(2,1)S(1)} collective-permute-done((bf16[8,128,128]{2,1,0:T(8,128)(2,1)S(1)}, bf16[8,128,128]{2,1,0:T(8,128)(2,1)S(1)}, u32[]{:S(2)}, u32[]{:S(2)}) %collective-permute-start.1) | collective-permute-done | bytes 262176 | tf_op jit(solution)/shard_map/ppermute | solution.py:64
  46.2 19.3 %all-to-all-start.1 = ((bf16[8,16,16,128]{3,2,1,0:T(8,128)(2,1)}), bf16[8,16,16,128]{3,2,1,0:T(8,128)(2,1)S(1)}, u32[]{:S(2)}, u32[]{:S(2)}) async-start(bf16[8,16,16,128]{3,2,1,0:T(8,128)(2,1)} %shard_map.103), calls=%async_computation.1 | async-start | bytes 1048576 | tf_op jit(solution)/shard_map/all_to_all | solution.py:60
  107.2 8.7 %collective-permute-done.6 = bf16[4,8,128,128]{3,2,1,0:T(8,128)(2,1)} collective-permute-done((bf16[4,8,128,128]{3,2,1,0:T(8,128)(2,1)}, bf16[4,8,128,128]{3,2,1,0:T(8,128)(2,1)}, u32[]{:S(2)}, u32[]{:S(2)}) %collective-permute-start.6) | collective-permute-done | bytes 1048608 | tf_op jit(solution)/shard_map/ppermute | solution.py:282
  136.7 31.8 %collective-permute-done.9 = bf16[4,8,128,128]{3,2,1,0:T(8,128)(2,1)} collective-permute-done((bf16[4,8,128,128]{3,2,1,0:T(8,128)(2,1)}, bf16[4,8,128,128]{3,2,1,0:T(8,128)(2,1)}, u32[]{:S(2)}, u32[]{:S(2)}) %collective-permute-start.9) | collective-permute-done | bytes 1048608 | tf_op jit(solution)/shard_map/ppermute | solution.py:64
  168.5 21.6 %collective-permute-done.7 = bf16[4,8,128,128]{3,2,1,0:T(8,128)(2,1)} collective-permute-done((bf16[4,8,128,128]{3,2,1,0:T(8,128)(2,1)}, bf16[4,8,128,128]{3,2,1,0:T(8,128)(2,1)}, u32[]{:S(2)}, u32[]{:S(2)}) %collective-permute-start.7) | collective-permute-done | bytes 1048608 | tf_op jit(solution)/shard_map/ppermute | solution.py:64
  198.8 11.4 %all_to_all.115.values = bf16[8,16,16,128]{3,2,1,0:T(8,128)(2,1)S(1)} all-to-all(bf16[8,16,16,128]{3,2,1,0:T(8,128)(2,1)S(1)} %get-tuple-element.54), channel_id=1, replica_groups={{0,1,2,3,4,5,6,7},{8,9,10,11,12,13,14,15},{16,17,18,19,20,21,22,23},{24..., dimensions={0} | all-to-all | bytes 1048576 | tf_op jit(solution)/shard_map/all_to_all | solution.py:60
  211.5 11.5 %all_to_all.116.values = bf16[8,16,16,128]{3,2,1,0:T(8,128)(2,1)S(1)} all-to-all(bf16[8,16,16,128]{3,2,1,0:T(8,128)(2,1)S(1)} %get-tuple-element.55), channel_id=1, replica_groups={{0,1,2,3,4,5,6,7},{8,9,10,11,12,13,14,15},{16,17,18,19,20,21,22,23},{24..., dimensions={0} | all-to-all | bytes 1048576 | tf_op jit(solution)/shard_map/all_to_all | solution.py:60
  223.9 11.5 %all_to_all.117.values = bf16[8,16,16,128]{3,2,1,0:T(8,128)(2,1)S(1)} all-to-all(bf16[8,16,16,128]{3,2,1,0:T(8,128)(2,1)S(1)} %get-tuple-element.56), channel_id=1, replica_groups={{0,1,2,3,4,5,6,7},{8,9,10,11,12,13,14,15},{16,17,18,19,20,21,22,23},{24..., dimensions={0} | all-to-all | bytes 1048576 | tf_op jit(solution)/shard_map/all_to_all | solution.py:60
  254.4 11.5 %all_to_all.118.values = bf16[8,16,16,128]{3,2,1,0:T(8,128)(2,1)S(1)} all-to-all(bf16[8,16,16,128]{3,2,1,0:T(8,128)(2,1)S(1)} %get-tuple-element.58), channel_id=1, replica_groups={{0,1,2,3,4,5,6,7},{8,9,10,11,12,13,14,15},{16,17,18,19,20,21,22,23},{24..., dimensions={0} | all-to-all | bytes 1048576 | tf_op jit(solution)/shard_map/all_to_all | solution.py:60
  267.3 11.5 %all_to_all.119.values = bf16[8,16,16,128]{3,2,1,0:T(8,128)(2,1)S(1)} all-to-all(bf16[8,16,16,128]{3,2,1,0:T(8,128)(2,1)S(1)} %get-tuple-element.59), channel_id=1, replica_groups={{0,1,2,3,4,5,6,7},{8,9,10,11,12,13,14,15},{16,17,18,19,20,21,22,23},{24..., dimensions={0} | all-to-all | bytes 1048576 | tf_op jit(solution)/shard_map/all_to_all | solution.py:60
  290.8 7.6 %collective-permute-done = bf16[8,128,128]{2,1,0:T(8,128)(2,1)S(1)} collective-permute-done((bf16[8,128,128]{2,1,0:T(8,128)(2,1)S(1)}, bf16[8,128,128]{2,1,0:T(8,128)(2,1)S(1)}, u32[]{:S(2)}, u32[]{:S(2)}) %collective-permute-start) | collective-permute-done | bytes 262176 | tf_op jit(solution)/shard_map/ppermute | solution.py:64
  301.1 7.9 %all-to-all-start = ((bf16[8,16,16,128]{3,2,1,0:T(8,128)(2,1)}), bf16[8,16,16,128]{3,2,1,0:T(8,128)(2,1)}, u32[]{:S(2)}, u32[]{:S(2)}) async-start(bf16[8,16,16,128]{3,2,1,0:T(8,128)(2,1)} %copy-done.17), calls=%async_computation | async-start | bytes 1048576 | tf_op jit(solution)/shard_map/all_to_all | solution.py:60
  322.1 11.6 %all_to_all.120.grad = bf16[8,16,16,128]{3,2,1,0:T(8,128)(2,1)S(1)} all-to-all(bf16[8,16,16,128]{3,2,1,0:T(8,128)(2,1)S(1)} %get-tuple-element.61), channel_id=1, replica_groups={{0,1,2,3,4,5,6,7},{8,9,10,11,12,13,14,15},{16,17,18,19,20,21,22,23},{24..., dimensions={0} | all-to-all | bytes 1048576 | tf_op jit(solution)/shard_map/all_to_all | solution.py:60
  334.9 11.6 %all_to_all.121.grad = bf16[8,16,16,128]{3,2,1,0:T(8,128)(2,1)S(1)} all-to-all(bf16[8,16,16,128]{3,2,1,0:T(8,128)(2,1)S(1)} %get-tuple-element.64), channel_id=1, replica_groups={{0,1,2,3,4,5,6,7},{8,9,10,11,12,13,14,15},{16,17,18,19,20,21,22,23},{24..., dimensions={0} | all-to-all | bytes 1048576 | tf_op jit(solution)/shard_map/all_to_all | solution.py:60
  348.1 11.6 %all_to_all.122.grad = bf16[8,16,16,128]{3,2,1,0:T(8,128)(2,1)S(1)} all-to-all(bf16[8,16,16,128]{3,2,1,0:T(8,128)(2,1)S(1)} %get-tuple-element.66), channel_id=1, replica_groups={{0,1,2,3,4,5,6,7},{8,9,10,11,12,13,14,15},{16,17,18,19,20,21,22,23},{24..., dimensions={0} | all-to-all | bytes 1048576 | tf_op jit(solution)/shard_map/all_to_all | solution.py:60
  361.4 11.6 %all_to_all.123.grad = bf16[8,16,16,128]{3,2,1,0:T(8,128)(2,1)S(1)} all-to-all(bf16[8,16,16,128]{3,2,1,0:T(8,128)(2,1)S(1)} %get-tuple-element.72), channel_id=1, replica_groups={{0,1,2,3,4,5,6,7},{8,9,10,11,12,13,14,15},{16,17,18,19,20,21,22,23},{24..., dimensions={0} | all-to-all | bytes 1048576 | tf_op jit(solution)/shard_map/all_to_all | solution.py:60
  373.7 11.6 %all_to_all.124.grad = bf16[8,16,16,128]{3,2,1,0:T(8,128)(2,1)S(1)} all-to-all(bf16[8,16,16,128]{3,2,1,0:T(8,128)(2,1)S(1)} %get-tuple-element.74), channel_id=1, replica_groups={{0,1,2,3,4,5,6,7},{8,9,10,11,12,13,14,15},{16,17,18,19,20,21,22,23},{24..., dimensions={0} | all-to-all | bytes 1048576 | tf_op jit(solution)/shard_map/all_to_all | solution.py:60
  386.5 11.6 %all_to_all.125.grad = bf16[8,16,16,128]{3,2,1,0:T(8,128)(2,1)S(1)} all-to-all(bf16[8,16,16,128]{3,2,1,0:T(8,128)(2,1)S(1)} %get-tuple-element.77), channel_id=1, replica_groups={{0,1,2,3,4,5,6,7},{8,9,10,11,12,13,14,15},{16,17,18,19,20,21,22,23},{24..., dimensions={0} | all-to-all | bytes 1048576 | tf_op jit(solution)/shard_map/all_to_all | solution.py:60
  399.7 11.6 %all_to_all.126.grad = bf16[8,16,16,128]{3,2,1,0:T(8,128)(2,1)S(1)} all-to-all(bf16[8,16,16,128]{3,2,1,0:T(8,128)(2,1)S(1)} %get-tuple-element.79), channel_id=1, replica_groups={{0,1,2,3,4,5,6,7},{8,9,10,11,12,13,14,15},{16,17,18,19,20,21,22,23},{24..., dimensions={0} | all-to-all | bytes 1048576 | tf_op jit(solution)/shard_map/all_to_all | solution.py:60
  412.9 11.6 %all_to_all.127.grad = bf16[8,16,16,128]{3,2,1,0:T(8,128)(2,1)S(1)} all-to-all(bf16[8,16,16,128]{3,2,1,0:T(8,128)(2,1)S(1)} %get-tuple-element.85), channel_id=1, replica_groups={{0,1,2,3,4,5,6,7},{8,9,10,11,12,13,14,15},{16,17,18,19,20,21,22,23},{24..., dimensions={0} | all-to-all | bytes 1048576 | tf_op jit(solution)/shard_map/all_to_all | solution.py:60
  452.1 53.9 %collective-permute-done.10 = bf16[4,8,128,128]{3,2,1,0:T(8,128)(2,1)} collective-permute-done((bf16[4,8,128,128]{3,2,1,0:T(8,128)(2,1)}, bf16[4,8,128,128]{3,2,1,0:T(8,128)(2,1)}, u32[]{:S(2)}, u32[]{:S(2)}) %collective-permute-start.10) | collective-permute-done | bytes 1048608 | tf_op jit(solution)/shard_map/ppermute | solution.py:64
  519.4 26.0 %collective-permute-done.12 = bf16[4,8,128,128]{3,2,1,0:T(8,128)(2,1)} collective-permute-done((bf16[4,8,128,128]{3,2,1,0:T(8,128)(2,1)}, bf16[4,8,128,128]{3,2,1,0:T(8,128)(2,1)}, u32[]{:S(2)}, u32[]{:S(2)}) %collective-permute-start.12) | collective-permute-done | bytes 1048608 | tf_op jit(solution)/shard_map/ppermute | solution.py:64
  565.5 9.8 %collective-permute-done.13 = bf16[4,8,128,128]{3,2,1,0:T(8,128)(2,1)} collective-permute-done((bf16[4,8,128,128]{3,2,1,0:T(8,128)(2,1)}, bf16[4,8,128,128]{3,2,1,0:T(8,128)(2,1)}, u32[]{:S(2)}, u32[]{:S(2)}) %collective-permute-start.13) | collective-permute-done | bytes 1048608 | tf_op jit(solution)/shard_map/ppermute | solution.py:304
  581.4 10.7 %collective-permute-done.17 = bf16[3,8,128,128]{3,2,1,0:T(8,128)(2,1)} collective-permute-done((bf16[3,8,128,128]{3,2,1,0:T(8,128)(2,1)}, bf16[3,8,128,128]{3,2,1,0:T(8,128)(2,1)}, u32[]{:S(2)}, u32[]{:S(2)}) %collective-permute-start.17) | collective-permute-done | bytes 786464 | tf_op jit(solution)/shard_map/ppermute | solution.py:304
  (266 shorter events, 231.5 us)
Async XLA Ops:
  17.1 23.8 %collective-permute-start.4 = (bf16[3,8,128,128]{3,2,1,0:T(8,128)(2,1)}, bf16[3,8,128,128]{3,2,1,0:T(8,128)(2,1)}, u32[]{:S(2)}, u32[]{:S(2)}) collective-permute-start(bf16[3,8,128,128]{3,2,1,0:T(8,128)(2,1)} %pad_maximum_fusion.9), channel_id=1, source_target_pairs={{0,16},{16,0},{1,17},{17,1},{2,18},{18,2},{3,19},{19,3},{4,20},{20... | collective-permute-start | bytes 2359304 | tf_op jit(solution)/shard_map/ppermute | solution.py:282
  18.2 21.4 %collective-permute-start.1 = (bf16[8,128,128]{2,1,0:T(8,128)(2,1)S(1)}, bf16[8,128,128]{2,1,0:T(8,128)(2,1)S(1)}, u32[]{:S(2)}, u32[]{:S(2)}) collective-permute-start(bf16[8,128,128]{2,1,0:T(8,128)(2,1)S(1)} %dynamic-slice_bitcast_fusion), channel_id=1, source_target_pairs={{0,8},{1,9},{2,10},{3,11},{4,12},{5,13},{6,14},{7,15},{8,0},{9,1},... | collective-permute-start | bytes 786440 | tf_op jit(solution)/shard_map/ppermute | solution.py:64
  23.4 21.3 %collective-permute-start.3 = (bf16[1,8,128,128]{3,2,1,0:T(8,128)(2,1)S(1)}, bf16[1,8,128,128]{3,2,1,0:T(8,128)(2,1)S(1)}, u32[]{:S(2)}, u32[]{:S(2)}) collective-permute-start(bf16[1,8,128,128]{3,2,1,0:T(8,128)(2,1)S(1)} %broadcast_select_fusion.15), channel_id=1, source_target_pairs={{0,8},{1,9},{2,10},{3,11},{4,12},{5,13},{6,14},{7,15},{8,0},{9,1},... | collective-permute-start | bytes 786440 | tf_op jit(solution)/shard_map/ppermute | solution.py:64
  42.0 36.0 %collective-permute-start.5 = (bf16[3,8,128,128]{3,2,1,0:T(8,128)(2,1)}, bf16[3,8,128,128]{3,2,1,0:T(8,128)(2,1)}, u32[]{:S(2)}, u32[]{:S(2)}) collective-permute-start(bf16[3,8,128,128]{3,2,1,0:T(8,128)(2,1)} %broadcast_select_fusion.10), channel_id=1, source_target_pairs={{0,8},{1,9},{2,10},{3,11},{4,12},{5,13},{6,14},{7,15},{8,0},{9,1},... | collective-permute-start | bytes 2359304 | tf_op jit(solution)/shard_map/ppermute | solution.py:64
  46.2 37.2 %all-to-all-start.1 = ((bf16[8,16,16,128]{3,2,1,0:T(8,128)(2,1)}), bf16[8,16,16,128]{3,2,1,0:T(8,128)(2,1)S(1)}, u32[]{:S(2)}, u32[]{:S(2)}) async-start(bf16[8,16,16,128]{3,2,1,0:T(8,128)(2,1)} %shard_map.103), calls=%async_computation.1 | async-start | bytes 1048576 | tf_op jit(solution)/shard_map/all_to_all | solution.py:60
  67.6 26.3 %collective-permute-start.8 = (bf16[4,8,128,128]{3,2,1,0:T(8,128)(2,1)}, bf16[4,8,128,128]{3,2,1,0:T(8,128)(2,1)}, u32[]{:S(2)}, u32[]{:S(2)}) collective-permute-start(bf16[4,8,128,128]{3,2,1,0:T(8,128)(2,1)} %pad_maximum_fusion.4), channel_id=1, source_target_pairs={{0,16},{16,0},{1,17},{17,1},{2,18},{18,2},{3,19},{19,3},{4,20},{20... | collective-permute-start | bytes 3145736 | tf_op jit(solution)/shard_map/ppermute | solution.py:282
  70.1 45.8 %collective-permute-start.6 = (bf16[4,8,128,128]{3,2,1,0:T(8,128)(2,1)}, bf16[4,8,128,128]{3,2,1,0:T(8,128)(2,1)}, u32[]{:S(2)}, u32[]{:S(2)}) collective-permute-start(bf16[4,8,128,128]{3,2,1,0:T(8,128)(2,1)} %pad_maximum_fusion.3), channel_id=1, source_target_pairs={{0,16},{16,0},{1,17},{17,1},{2,18},{18,2},{3,19},{19,3},{4,20},{20... | collective-permute-start | bytes 3145736 | tf_op jit(solution)/shard_map/ppermute | solution.py:282
  96.3 72.1 %collective-permute-start.9 = (bf16[4,8,128,128]{3,2,1,0:T(8,128)(2,1)}, bf16[4,8,128,128]{3,2,1,0:T(8,128)(2,1)}, u32[]{:S(2)}, u32[]{:S(2)}) collective-permute-start(bf16[4,8,128,128]{3,2,1,0:T(8,128)(2,1)} %broadcast_select_fusion), channel_id=1, source_target_pairs={{0,8},{1,9},{2,10},{3,11},{4,12},{5,13},{6,14},{7,15},{8,0},{9,1},... | collective-permute-start | bytes 3145736 | tf_op jit(solution)/shard_map/ppermute | solution.py:64
  103.0 26.3 %all-to-all-start.3 = ((bf16[8,16,16,128]{3,2,1,0:T(8,128)(2,1)}), bf16[8,16,16,128]{3,2,1,0:T(8,128)(2,1)S(1)}, u32[]{:S(2)}, u32[]{:S(2)}) async-start(bf16[8,16,16,128]{3,2,1,0:T(8,128)(2,1)} %get-tuple-element.51), calls=%async_computation.3 | async-start | bytes 1048576 | tf_op jit(solution)/shard_map/all_to_all | solution.py:60
  118.5 71.6 %collective-permute-start.7 = (bf16[4,8,128,128]{3,2,1,0:T(8,128)(2,1)}, bf16[4,8,128,128]{3,2,1,0:T(8,128)(2,1)}, u32[]{:S(2)}, u32[]{:S(2)}) collective-permute-start(bf16[4,8,128,128]{3,2,1,0:T(8,128)(2,1)} %broadcast_select_fusion.1), channel_id=1, source_target_pairs={{0,8},{1,9},{2,10},{3,11},{4,12},{5,13},{6,14},{7,15},{8,0},{9,1},... | collective-permute-start | bytes 3145736 | tf_op jit(solution)/shard_map/ppermute | solution.py:64
  131.5 63.5 %all-to-all-start.4 = ((bf16[8,16,16,128]{3,2,1,0:T(8,128)(2,1)}), bf16[8,16,16,128]{3,2,1,0:T(8,128)(2,1)}, u32[]{:S(2)}, u32[]{:S(2)}) async-start(bf16[8,16,16,128]{3,2,1,0:T(8,128)(2,1)} %get-tuple-element.52), calls=%async_computation.4 | async-start | bytes 1048576 | tf_op jit(solution)/shard_map/all_to_all | solution.py:60
  282.0 19.2 %all-to-all-start.11 = ((bf16[8,16,16,128]{3,2,1,0:T(8,128)(2,1)}), bf16[8,16,16,128]{3,2,1,0:T(8,128)(2,1)}, u32[]{:S(2)}, u32[]{:S(2)}) async-start(bf16[8,16,16,128]{3,2,1,0:T(8,128)(2,1)} %get-tuple-element.60), calls=%async_computation.11 | async-start | bytes 1048576 | tf_op jit(solution)/shard_map/all_to_all | solution.py:60
  301.1 16.9 %all-to-all-start = ((bf16[8,16,16,128]{3,2,1,0:T(8,128)(2,1)}), bf16[8,16,16,128]{3,2,1,0:T(8,128)(2,1)}, u32[]{:S(2)}, u32[]{:S(2)}) async-start(bf16[8,16,16,128]{3,2,1,0:T(8,128)(2,1)} %copy-done.17), calls=%async_computation | async-start | bytes 1048576 | tf_op jit(solution)/shard_map/all_to_all | solution.py:60
  426.8 15.9 %all-to-all-start.20 = ((bf16[8,16,16,128]{3,2,1,0:T(8,128)(2,1)}), bf16[8,16,16,128]{3,2,1,0:T(8,128)(2,1)S(1)}, u32[]{:S(2)}, u32[]{:S(2)}) async-start(bf16[8,16,16,128]{3,2,1,0:T(8,128)(2,1)} %get-tuple-element.87), calls=%async_computation.20 | async-start | bytes 1048576 | tf_op jit(solution)/shard_map/all_to_all | solution.py:60
  433.5 72.6 %collective-permute-start.10 = (bf16[4,8,128,128]{3,2,1,0:T(8,128)(2,1)}, bf16[4,8,128,128]{3,2,1,0:T(8,128)(2,1)}, u32[]{:S(2)}, u32[]{:S(2)}) collective-permute-start(bf16[4,8,128,128]{3,2,1,0:T(8,128)(2,1)} %broadcast_select_fusion.4), channel_id=1, source_target_pairs={{0,8},{1,9},{2,10},{3,11},{4,12},{5,13},{6,14},{7,15},{8,0},{9,1},... | collective-permute-start | bytes 3145736 | tf_op jit(solution)/shard_map/ppermute | solution.py:64
  445.4 63.9 %all-to-all-start.21 = ((bf16[8,16,16,128]{3,2,1,0:T(8,128)(2,1)}), bf16[8,16,16,128]{3,2,1,0:T(8,128)(2,1)S(1)}, u32[]{:S(2)}, u32[]{:S(2)}) async-start(bf16[8,16,16,128]{3,2,1,0:T(8,128)(2,1)} %get-tuple-element.90), calls=%async_computation.21 | async-start | bytes 1048576 | tf_op jit(solution)/shard_map/all_to_all | solution.py:60
  452.1 93.3 %collective-permute-start.12 = (bf16[4,8,128,128]{3,2,1,0:T(8,128)(2,1)}, bf16[4,8,128,128]{3,2,1,0:T(8,128)(2,1)}, u32[]{:S(2)}, u32[]{:S(2)}) collective-permute-start(bf16[4,8,128,128]{3,2,1,0:T(8,128)(2,1)} %broadcast_select_fusion.2), channel_id=1, source_target_pairs={{0,8},{1,9},{2,10},{3,11},{4,12},{5,13},{6,14},{7,15},{8,0},{9,1},... | collective-permute-start | bytes 3145736 | tf_op jit(solution)/shard_map/ppermute | solution.py:64
  508.7 42.4 %collective-permute-start.11 = (bf16[4,8,128,128]{3,2,1,0:T(8,128)(2,1)}, bf16[4,8,128,128]{3,2,1,0:T(8,128)(2,1)}, u32[]{:S(2)}, u32[]{:S(2)}) collective-permute-start(bf16[4,8,128,128]{3,2,1,0:T(8,128)(2,1)} %fusion), channel_id=1, source_target_pairs={{0,16},{16,0},{1,17},{17,1},{2,18},{18,2},{3,19},{19,3},{4,20},{20... | collective-permute-start | bytes 3145736 | tf_op jit(solution)/shard_map/ppermute | solution.py:304
  513.2 48.8 %collective-permute-start.16 = (bf16[3,8,128,128]{3,2,1,0:T(8,128)(2,1)}, bf16[3,8,128,128]{3,2,1,0:T(8,128)(2,1)}, u32[]{:S(2)}, u32[]{:S(2)}) collective-permute-start(bf16[3,8,128,128]{3,2,1,0:T(8,128)(2,1)} %broadcast_select_fusion.11), channel_id=1, source_target_pairs={{0,8},{1,9},{2,10},{3,11},{4,12},{5,13},{6,14},{7,15},{8,0},{9,1},... | collective-permute-start | bytes 2359304 | tf_op jit(solution)/shard_map/ppermute | solution.py:64
  513.2 51.7 %all-to-all-start.22 = ((bf16[8,16,16,128]{3,2,1,0:T(8,128)(2,1)}), bf16[8,16,16,128]{3,2,1,0:T(8,128)(2,1)S(1)}, u32[]{:S(2)}, u32[]{:S(2)}) async-start(bf16[8,16,16,128]{3,2,1,0:T(8,128)(2,1)} %get-tuple-element.92), calls=%async_computation.22 | async-start | bytes 1048576 | tf_op jit(solution)/shard_map/all_to_all | solution.py:60
  548.8 26.4 %collective-permute-start.13 = (bf16[4,8,128,128]{3,2,1,0:T(8,128)(2,1)}, bf16[4,8,128,128]{3,2,1,0:T(8,128)(2,1)}, u32[]{:S(2)}, u32[]{:S(2)}) collective-permute-start(bf16[4,8,128,128]{3,2,1,0:T(8,128)(2,1)} %fusion.1), channel_id=1, source_target_pairs={{0,16},{16,0},{1,17},{17,1},{2,18},{18,2},{3,19},{19,3},{4,20},{20... | collective-permute-start | bytes 3145736 | tf_op jit(solution)/shard_map/ppermute | solution.py:304
  564.3 27.8 %collective-permute-start.17 = (bf16[3,8,128,128]{3,2,1,0:T(8,128)(2,1)}, bf16[3,8,128,128]{3,2,1,0:T(8,128)(2,1)}, u32[]{:S(2)}, u32[]{:S(2)}) collective-permute-start(bf16[3,8,128,128]{3,2,1,0:T(8,128)(2,1)} %fusion.2), channel_id=1, source_target_pairs={{0,16},{16,0},{1,17},{17,1},{2,18},{18,2},{3,19},{19,3},{4,20},{20... | collective-permute-start | bytes 2359304 | tf_op jit(solution)/shard_map/ppermute | solution.py:304
  565.4 14.3 %collective-permute-start.14 = (bf16[1,8,128,128]{3,2,1,0:T(8,128)(2,1)S(1)}, bf16[1,8,128,128]{3,2,1,0:T(8,128)(2,1)S(1)}, u32[]{:S(2)}, u32[]{:S(2)}) collective-permute-start(bf16[1,8,128,128]{3,2,1,0:T(8,128)(2,1)S(1)} %broadcast_select_fusion.16), channel_id=1, source_target_pairs={{0,8},{1,9},{2,10},{3,11},{4,12},{5,13},{6,14},{7,15},{8,0},{9,1},... | collective-permute-start | bytes 786440 | tf_op jit(solution)/shard_map/ppermute | solution.py:64
  579.9 16.2 %collective-permute-start.15 = (bf16[1,8,128,128]{3,2,1,0:T(8,128)(2,1)S(1)}, bf16[1,8,128,128]{3,2,1,0:T(8,128)(2,1)S(1)}, u32[]{:S(2)}, u32[]{:S(2)}) collective-permute-start(bf16[1,8,128,128]{3,2,1,0:T(8,128)(2,1)S(1)} %get-tuple-element.99), channel_id=1, source_target_pairs={{0,16},{16,0},{1,17},{17,1},{2,18},{18,2},{3,19},{19,3},{4,20},{20... | collective-permute-start | bytes 786440 | tf_op jit(solution)/shard_map/ppermute | solution.py:304
  (78 other events, 1331.0 us)

commit v2 on v1

v2 whole, which is shorter than its diff:
```python
import functools
import math

import jax
import jax.numpy as jnp
from jax import lax
from jax.experimental import pallas as pl
from jax.experimental.pallas import tpu as pltpu
from jax.sharding import PartitionSpec as P

F32 = jnp.float32
BF16 = jnp.bfloat16
ROOT = math.sqrt(2.0 / math.pi)


def gelu(u):
    return 0.5 * u * (1.0 + jnp.tanh(ROOT * (u + 0.044715 * (u * u * u))))


def gelu_slope(u):
    square = u * u
    th = jnp.tanh(ROOT * (u + 0.044715 * (u * square)))
    inner = ROOT * (1.0 + 3 * 0.044715 * square)
    return 0.5 * (1.0 + th) + 0.5 * u * (1.0 - th * th) * inner


class Plan:
    def __init__(self, segments, devices, micros, blocks, tokens):
        self.segments = segments
        self.devices = devices
        self.halves = 2 if micros * tokens >= 256 * segments and devices % 2 == 0 else 1
        self.group = devices // self.halves
        self.own = blocks // devices
        self.held = self.own * self.halves
        self.size = blocks
        self.tokens = micros * tokens // (segments * self.halves)
        self.kernels = segments == 2 and micros == 2 and self.halves == 2
        self.kernels = self.kernels and self.own == 8 and self.tokens % 128 == 0
        self.groups = None
        if self.halves > 1:
            self.groups = [
                [half * self.group + rank for rank in range(self.group)]
                for half in range(self.halves)
            ]

    def packed_shape(self):
        return (self.group, self.held, self.held, self.tokens)

    def natural_shape(self):
        return (self.held, self.size, self.tokens)

    def pack(self, values):
        split = values.reshape(self.held, self.halves, self.group, self.own, self.tokens)
        return split.transpose(2, 1, 3, 0, 4).reshape(self.packed_shape())

    def unpack(self, packed):
        split = packed.reshape(self.group, self.held, self.halves, self.own, self.tokens)
        return split.transpose(1, 2, 0, 3, 4).reshape(self.natural_shape())

    def exchange(self, packed):
        return lax.all_to_all(packed, "blk", 0, 0, axis_index_groups=self.groups, tiled=True)

    def swap_halves(self, value):
        return lax.ppermute(
            value, "blk", [(at, (at + self.group) % self.devices) for at in range(self.devices)]
        )


def matmul(a, b, over_a, over_b):
    return lax.dot_general(a, b, (((over_a,), (over_b,)), ((), ())), preferred_element_type=F32)


def each_block(plan, half):
    for turn in range(2):
        base = (half[0] if turn == 0 else 1 - half[0]) * plan.own
        for at in range(plan.own):
            yield turn, at, turn * plan.own + at, base + at


def read_natural(plan, ref, block):
    values = ref[:, block].astype(F32)
    rows = [
        values[rank, half * plan.own : (half + 1) * plan.own]
        for half in range(plan.halves)
        for rank in range(plan.group)
    ]
    return jnp.concatenate(rows, axis=0)


def write_packed(plan, scratch, out):
    step = plan.group * plan.own * plan.held
    for half in range(plan.halves):
        rows = scratch[half * step : (half + 1) * step, :].astype(BF16)
        out[:, half * plan.own : (half + 1) * plan.own] = rows.reshape(
            plan.group, plan.own, plan.held, plan.tokens
        )


def scatter(plan, scratch, block, values):
    scratch[pl.ds(block, plan.size, stride=plan.held), :] = values


def start_body(plan, state, weight, out, scratch):
    for block in range(plan.own):
        values = matmul(weight[block], state[block], 0, 0)
        for part in range(plan.halves):
            chunk = values[:, part * plan.tokens : (part + 1) * plan.tokens]
            scratch[part, pl.ds(block, plan.size, stride=plan.own), :] = chunk
    step = plan.own * plan.own
    for part in range(plan.halves):
        for half in range(plan.halves):
            for rank in range(plan.group):
                at = (half * plan.group + rank) * step
                rows = scratch[part, at : at + step, :].astype(BF16)
                out[part * plan.group + rank, half * step : (half + 1) * step] = rows


def wide_left_body(plan, half, values, own, other, out, kept, scratch):
    for turn in range(2):
        base = (half[0] if turn == 0 else 1 - half[0]) * plan.own * plan.own
        weight = own if turn == 0 else other
        for pair in range(plan.own // 2):
            start = pl.multiple_of(base + pair * 2 * plan.own, 2 * plan.own)
            rows = values[:, pl.ds(start, 2 * plan.own), :].astype(F32)
            for odd in range(2):
                at = 2 * pair + odd
                natural = rows[:, odd * plan.own : (odd + 1) * plan.own]
                natural = natural.reshape(plan.size, plan.tokens).astype(BF16)
                kept[turn * plan.own + at] = natural
                block = (half[0] if turn == 0 else 1 - half[0]) * plan.own + at
                scatter(plan, scratch, block, matmul(weight[at], natural, 0, 0))
    write_packed(plan, scratch, out)


def residual_body(plan, half, state, branch, own, other, out, result, scratch):
    for turn, at, place, block in each_block(plan, half):
        total = state[place].astype(F32) + read_natural(plan, branch, block)
        total = total.astype(BF16)
        result[place] = total
        scatter(plan, scratch, block, matmul((own, other)[turn][at], total, 0, 0))
    write_packed(plan, scratch, out)


def left_body(plan, half, values, own, other, out, kept, scratch):
    for turn, at, place, block in each_block(plan, half):
        natural = read_natural(plan, values, block).astype(BF16)
        kept[place] = natural
        scatter(plan, scratch, block, matmul((own, other)[turn][at], natural, 0, 0))
    write_packed(plan, scratch, out)


def gelu_body(plan, half, values, own, other, out, upper, hidden, scratch):
    for turn, at, place, block in each_block(plan, half):
        natural = read_natural(plan, values, block)
        upper[place] = natural.astype(BF16)
        active = gelu(natural).astype(BF16)
        hidden[place] = active
        scatter(plan, scratch, block, matmul((own, other)[turn][at], active, 0, 0))
    write_packed(plan, scratch, out)


def pack_body(plan, half, values, out, scratch):
    for turn, at, place, block in each_block(plan, half):
        scatter(plan, scratch, block, values[place].astype(F32))
    write_packed(plan, scratch, out)


def unpack_body(plan, half, values, out):
    for turn, at, place, block in each_block(plan, half):
        out[place] = read_natural(plan, values, block).astype(BF16)


def put_grad(grads, turn, at, values):
    grads[turn][at] = values.astype(grads[turn].dtype)


def back_left_body(plan, half, grad, kept, own, other, out, stay, leave, scratch):
    for turn, at, place, block in each_block(plan, half):
        natural = read_natural(plan, grad, block).astype(BF16)
        scatter(plan, scratch, block, matmul((own, other)[turn][at], natural, 1, 0))
        put_grad((stay, leave), turn, at, matmul(kept[place], natural, 1, 1))
    write_packed(plan, scratch, out)


def last_left_body(plan, half, grad, kept, own, other, out, stay, leave, scratch):
    for turn, at, place, block in each_block(plan, half):
        natural = read_natural(plan, grad, block).astype(BF16)
        scatter(plan, scratch, block, matmul((own, other)[turn][at], natural, 1, 0))
        put_grad((stay, leave), turn, at, matmul(kept[place], natural, 1, 1))
    out[...] = scratch[...].astype(BF16).reshape(plan.devices, plan.size, plan.tokens)


def back_gelu_body(plan, half, grad, hidden, upper, own, other, out, stay, leave, scratch):
    for turn, at, place, block in each_block(plan, half):
        natural = read_natural(plan, grad, block).astype(BF16)
        grad_hidden = matmul((own, other)[turn][at], natural, 1, 0)
        scatter(plan, scratch, block, grad_hidden * gelu_slope(upper[place].astype(F32)))
        put_grad((stay, leave), turn, at, matmul(hidden[place], natural, 1, 1))
    write_packed(plan, scratch, out)


def back_right_body(
    plan, half, grad, state, above, own, other, out, result, stay, leave, scratch
):
    for turn, at, place, block in each_block(plan, half):
        natural = read_natural(plan, grad, block).astype(BF16)
        total = matmul((own, other)[turn][at], natural, 1, 0) + above[place].astype(F32)
        result[place] = total.astype(BF16)
        scatter(plan, scratch, block, total)
        put_grad((stay, leave), turn, at, matmul(state[place], natural, 1, 1))
    write_packed(plan, scratch, out)


def end_body(plan, grad, state, stay, leave):
    for block in range(plan.own):
        total = jnp.zeros((plan.size, plan.size), F32)
        for part in range(plan.halves):
            rows = slice(block * plan.held, (block + 1) * plan.held)
            sources = slice(part * plan.group, (part + 1) * plan.group)
            values = grad[sources, rows].astype(F32)
            natural = jnp.concatenate(
                [
                    values[rank, half * plan.own : (half + 1) * plan.own]
                    for half in range(plan.halves)
                    for rank in range(plan.group)
                ],
                axis=0,
            ).astype(BF16)
            tokens = slice(part * plan.tokens, (part + 1) * plan.tokens)
            total = total + matmul(state[block, :, tokens], natural, 1, 1)
        stay[block] = total
        leave[block] = total.astype(BF16)


class Kernels:
    def __init__(self, plan, half):
        self.plan = plan
        self.half = half
        self.packed = (plan.packed_shape(), BF16)
        self.wide = ((plan.devices, plan.size, plan.tokens), BF16)
        self.natural = (plan.natural_shape(), BF16)
        square = (plan.own, plan.size, plan.size)
        self.grads = [(square, F32), (square, BF16)]
        self.rows = (plan.size * plan.held, plan.tokens)

    def run(self, body, ins, outs, scratch=None, products=1, after=(), half=True):
        plan = self.plan
        shapes = [jax.ShapeDtypeStruct(shape, dtype) for shape, dtype in outs]
        volume = sum(math.prod(i.shape) * i.dtype.itemsize for i in ins)
        volume += sum(math.prod(s.shape) * s.dtype.itemsize for s in shapes)
        flops = products * 2 * plan.held * plan.size * plan.size * plan.tokens
        vmem = pl.BlockSpec(memory_space=pltpu.VMEM)
        specs = [vmem] * len(ins)
        if half:
            ins = (self.half,) + tuple(ins)
            specs = [pl.BlockSpec(memory_space=pltpu.SMEM)] + specs
        first, count = len(ins), len(after)

        def kernel(*refs):
            body(plan, *refs[:first], *refs[first + count :])

        return pl.pallas_call(
            kernel,
            out_shape=shapes,
            in_specs=specs + [pl.BlockSpec(memory_space=pl.ANY)] * count,
            out_specs=[vmem] * len(shapes),
            scratch_shapes=[pltpu.VMEM(scratch, F32)] if scratch else [],
            compiler_params=pltpu.CompilerParams(vmem_limit_bytes=32 * 1024 * 1024),
            cost_estimate=pl.CostEstimate(flops=flops, bytes_accessed=volume, transcendentals=0),
            name=body.__name__,
        )(*ins, *after)


def swap_segments(value):
    return lax.ppermute(value, "segment", [(0, 1), (1, 0)])


def two_segments(plan, inputs, factors, cotangent, sections):
    segment = lax.axis_index("segment")
    half = lax.axis_index("blk") // plan.group
    kernels = Kernels(plan, half.astype(jnp.int32).reshape(1))
    run, packed, natural, grads = kernels.run, kernels.packed, kernels.natural, kernels.grads
    rows = kernels.rows
    count = 3

    owners = [jnp.int32(0), 2 - sections[0], jnp.int32(1)]
    places = [jnp.int32(0), sections[0] - 1, sections[1] - 1]

    def pick(index, factor, received):
        slot = places[index]
        mine = factor[0] if index == 0 else jnp.where(slot == 0, factor[0], factor[1])
        theirs = received[0] if index == 0 else jnp.where(slot == 0, received[0], received[1])
        return jnp.where(owners[index] == segment, mine, theirs)

    micro = lax.dynamic_index_in_dim(inputs, segment, 0, keepdims=False)
    above = lax.dynamic_index_in_dim(cotangent, segment, 0, keepdims=False)

    def own_and_other(values):
        lower, upper = values[:, :, : plan.tokens], values[:, :, plan.tokens :]
        kept = jnp.where(half == 0, lower, upper)
        leave = jnp.where(half == 0, upper, lower)
        return jnp.concatenate([kept, plan.swap_halves(leave)], axis=0)

    first = lax.ppermute(factors[0][0], "segment", [(0, 1)])
    first = jnp.where(segment == 0, factors[0][0], first)
    received = [None] * 4
    for at in (1, 2, 3, 0):
        received[at] = swap_segments(factors[at])
    weights = []
    for index in range(count):
        layer = []
        for at in range(4):
            if index == 0 and at == 0:
                layer.append((first, None))
                continue
            own = pick(index, factors[at], received[at])
            layer.append((own, plan.swap_halves(own)))
        weights.append(layer)

    sent = run(
        start_body,
        (micro, first),
        [kernels.wide],
        (plan.halves, plan.size * plan.own, plan.tokens),
        half=False,
    )[0]
    sent = lax.all_to_all(sent, "blk", 0, 0, tiled=True)
    state = own_and_other(micro)
    grad = own_and_other(above)

    saved = []
    branch = None
    for index in range(count):
        w = weights[index]
        if index == 0:
            body, values = wide_left_body, sent
        else:
            ins = (state, branch) + w[0]
            sent, state = run(residual_body, ins, [packed, natural], rows)
            body, values = left_body, plan.exchange(sent)
        sent, inner_one = run(body, (values,) + w[1], [packed, natural], rows)
        ins = (plan.exchange(sent),) + w[2]
        sent, upper, hidden = run(gelu_body, ins, [packed, natural, natural], rows)
        values = plan.exchange(sent)
        if index < count - 1:
            sent, inner_two = run(left_body, (values,) + w[3], [packed, natural], rows)
            branch = plan.exchange(sent)
        else:
            inner_two = run(unpack_body, (values,), [natural], products=0)[0]
        saved.append((state, inner_one, upper, hidden, inner_two))

    waiting = [(), ()]
    totals = [[None] * 4 for index in range(count)]

    def step(body, ins, outs, products=2):
        results = run(body, ins, outs + grads, rows, products, after=waiting.pop(0))
        stay, leave = results[-2:]
        other = plan.swap_halves(leave)
        waiting.append((other,))
        return results[:-2], stay.astype(F32) + other.astype(F32)

    def collect(index, values):
        if index == 0:
            other = [lax.ppermute(v.astype(BF16), "segment", [(1, 0)]) for v in values]
        else:
            other = swap_segments(jnp.stack([v.astype(BF16) for v in values]))
        return [value + other[at].astype(F32) for at, value in enumerate(values)]

    sent = run(pack_body, (grad,), [packed], rows, products=0)[0]
    for index in reversed(range(count)):
        w = weights[index]
        state, inner_one, upper, hidden, inner_two = saved[index]
        ins = (plan.exchange(sent), inner_two) + w[3]
        (sent,), grad_l2 = step(back_left_body, ins, [packed])
        ins = (plan.exchange(sent), hidden, upper) + w[2]
        (sent,), grad_r2 = step(back_gelu_body, ins, [packed])
        ins = (plan.exchange(sent), inner_one) + w[1]
        if index > 0:
            (sent,), grad_l1 = step(back_left_body, ins, [packed])
            ins = (plan.exchange(sent), state, grad) + w[0]
            (sent, grad), grad_r1 = step(back_right_body, ins, [packed, natural])
            totals[index] = collect(index, [grad_r1, grad_l1, grad_r2, grad_l2])
        else:
            (sent,), grad_l1 = step(last_left_body, ins, [kernels.wide])
            sent = lax.all_to_all(sent, "blk", 0, 0, tiled=True)
            stay, leave = run(end_body, (sent, micro), grads, half=False)
            other = lax.ppermute(leave, "segment", [(1, 0)])
            late = collect(index, [grad_l1, grad_r2, grad_l2])
            totals[index] = [stay + other.astype(F32)] + late

    outs = []
    for at in range(4):
        slots = []
        for place in range(2):
            total = jnp.zeros(factors[0].shape[1:], F32)
            for index in range(count):
                here = (owners[index] == segment) & (places[index] == place)
                total = jnp.where(here, totals[index][at], total)
            slots.append(total)
        outs.append(jnp.stack(slots))
    return tuple(outs)


def apply(weight, values):
    return jnp.einsum("bij,bit->bjt", weight, values, preferred_element_type=F32)


def apply_back(weight, values):
    return jnp.einsum("bij,bjt->bit", weight, values, preferred_element_type=F32)


def outer(values, grad):
    return jnp.einsum("bit,bjt->bij", values, grad, preferred_element_type=F32).astype(BF16)


def spread(plan, factor, owner, half):
    every = lax.all_gather(factor, "segment", axis=0)
    factor = lax.dynamic_index_in_dim(every, owner, 0, keepdims=False)
    if plan.halves == 1:
        return factor
    other = plan.swap_halves(factor)
    lower = jnp.where(half == 0, factor, other)
    upper = jnp.where(half == 0, other, factor)
    return jnp.concatenate([lower, upper], axis=1)


def collect(plan, parts, half):
    if plan.halves == 1:
        return lax.psum(parts.astype(F32), "segment")
    lower, upper = parts[:, : plan.own], parts[:, plan.own :]
    kept = jnp.where(half == 0, lower, upper)
    other = plan.swap_halves(jnp.where(half == 0, upper, lower))
    return lax.psum(kept.astype(F32) + other.astype(F32), "segment")


def token_chunk(plan, values, half):
    mine = lax.axis_index("segment")
    per_micro = values.shape[-1] // plan.tokens

    def chunk(at):
        at = mine * plan.halves + at
        micro = lax.dynamic_index_in_dim(values, at // per_micro, 0, keepdims=False)
        start = (at % per_micro) * plan.tokens
        return lax.dynamic_slice_in_dim(micro, start, plan.tokens, 2)

    if plan.halves == 1:
        return chunk(0)
    kept, other = chunk(half), plan.swap_halves(chunk(1 - half))
    lower = jnp.where(half == 0, kept, other)
    upper = jnp.where(half == 0, other, kept)
    return jnp.concatenate([lower, upper], axis=0)


def many_segments(plan, inputs, factors, cotangent, sections):
    segment = lax.axis_index("segment")
    half = lax.axis_index("blk") // plan.group
    slots = factors[0].shape[0]

    def trade(values):
        return plan.unpack(plan.exchange(plan.pack(values.astype(BF16))))

    count = plan.segments * slots - 1
    ends = jnp.cumsum(sections)
    layers, weights = [], []
    for index in range(count):
        owner = jnp.minimum(jnp.sum((index >= ends).astype(jnp.int32)), plan.segments - 1)
        slot = jnp.clip(index - (ends[owner] - sections[owner]), 0, slots - 1)
        layers.append((owner, slot, index < ends[-1]))
        picked = [lax.dynamic_index_in_dim(f, slot, 0, keepdims=True) for f in factors]
        weights.append(spread(plan, jnp.concatenate(picked, axis=0), owner, half))

    state = token_chunk(plan, inputs, half)
    grad = token_chunk(plan, cotangent, half)
    saved = []
    for index in range(count):
        w = weights[index]
        inner_one = trade(apply(w[0], state))
        upper = trade(apply(w[1], inner_one))
        hidden = gelu(upper.astype(F32)).astype(BF16)
        inner_two = trade(apply(w[2], hidden))
        saved.append((state, inner_one, upper, hidden, inner_two))
        if index < count - 1:
            branch = trade(apply(w[3], inner_two))
            total = (state.astype(F32) + branch.astype(F32)).astype(BF16)
            state = jnp.where(layers[index][2], total, state)

    totals = [None] * count
    for index in reversed(range(count)):
        w = weights[index]
        state, inner_one, upper, hidden, inner_two = saved[index]
        grad_c = trade(grad)
        grad_a = trade(apply_back(w[3], grad_c))
        parts = [outer(hidden, grad_a), outer(inner_two, grad_c)]
        grad_u = apply_back(w[2], grad_a) * gelu_slope(upper.astype(F32))
        grad_c = trade(grad_u)
        grad_a = trade(apply_back(w[1], grad_c))
        parts = [outer(state, grad_a), outer(inner_one, grad_c)] + parts
        totals[index] = collect(plan, jnp.stack(parts), half)
        total = (apply_back(w[0], grad_a) + grad.astype(F32)).astype(BF16)
        grad = jnp.where(layers[index][2], total, grad)

    outs = []
    for at in range(4):
        rows = []
        for place in range(slots):
            total = jnp.zeros(factors[0].shape[1:], F32)
            for index, (owner, slot, active) in enumerate(layers):
                here = active & (owner == segment) & (slot == place)
                total = jnp.where(here, totals[index][at], total)
            rows.append(total)
        outs.append(jnp.stack(rows))
    return tuple(outs)


def shards(inputs, first_right, first_left, second_right, second_left, cotangent, sections):
    segments = lax.axis_size("segment")
    devices = lax.axis_size("blk")
    plan = Plan(segments, devices, inputs.shape[0], inputs.shape[2], inputs.shape[3])
    factors = (first_right, first_left, second_right, second_left)
    run = two_segments if plan.kernels else many_segments
    return run(plan, inputs, factors, cotangent, sections)


def solution(mesh):
    whole = P("segment", "blk", None, None)
    tokens = P(None, "blk", None, None)
    in_specs = (tokens, whole, whole, whole, whole, tokens, P())
    return jax.shard_map(
        shards, mesh=mesh, in_specs=in_specs, out_specs=(whole,) * 4, check_vma=False
    )
```

time: 603 us -> 634 us (1.051)
  blocking collectives: 150 us -> 13.8 us
  waiting for transfers between devices: 240 us -> 316 us
  starting transfers between devices: 90.5 us -> 154 us
  local copies, waits for them, and re-layouts: 29 us -> 75.3 us
  other arithmetic: 52.9 us -> 29.4 us
  Pallas kernels: 29.6 us -> 37.7 us
    all_to_all x13 -> x1, blocking collectives: 150 us -> 13.8 us  [exchange(): lax.all_to_all(packed, 'blk', 0, 0, axis_index_groups=self.groups, tiled=...]
    ppermute x18 -> x35, waiting for transfers between devices: 209 us -> 295 us  [the longest x24 264 us: swap_halves(): lax.ppermute(value, 'blk', [(at, (at + self.group) % self.devices) for at...]
    unnamed x148 -> x262, local copies, waits for them, and re-layouts: 21.8 us -> 72.6 us
    ppermute x18 -> x35, starting transfers between devices: 28.7 us -> 57.6 us  [the longest x24 39.5 us: swap_halves(): lax.ppermute(value, 'blk', [(at, (at + self.group) % self.devices) for at...]
    all_to_all x10 -> x20, starting transfers between devices: 61.8 us -> 86.1 us  [exchange(): lax.all_to_all(packed, 'blk', 0, 0, axis_index_groups=self.groups, tiled=...]
    select_n x15 -> x6, other arithmetic: 18.9 us -> 4.66 us  [the longest x4 4.58 us: pick(): return jnp.where(owners[index] == segment, mine, theirs)]
    another operation x8 -> x18, other arithmetic: 8.52 us -> 20.2 us  [the longest x8 11.4 us: two_segments(): outs.append(jnp.stack(slots))]
    all_to_all x0 -> x2, starting transfers between devices: none -> 10 us  [two_segments(): sent = lax.all_to_all(sent, 'blk', 0, 0, tiled=True)]
  transfers between devices with their start and end apart: 28 -> 57, of which waited for: 21 -> 36; matrix products, arithmetic and copies ran while one was open for 8% -> 5% of each run, Pallas kernels for 2% -> 2%
where the time goes in v2:
time: 634 us; the launch traced here: 630 us
  waiting for transfers between devices  316 us (50%)
  starting transfers between devices  154 us (24%)
  local copies, waits for them, and re-layouts  75.3 us (12%)
  Pallas kernels  37.7 us (6%)
  other arithmetic  29.4 us (5%)
  blocking collectives  13.8 us (2%)
    ppermute x24, waiting for transfers between devices, swap_halves(): lax.ppermute(value, 'blk', [(at, (at + self.group) % self.devices) for at...  264 us
    all_to_all x20, starting transfers between devices, exchange(): lax.all_to_all(packed, 'blk', 0, 0, axis_index_groups=self.groups, tiled=...  86.1 us
    unnamed x262, local copies, waits for them, and re-layouts  72.6 us
    ppermute x24, starting transfers between devices, swap_halves(): lax.ppermute(value, 'blk', [(at, (at + self.group) % self.devices) for at...  39.5 us
    pallas_call x25, Pallas kernels, run(): pl.pallas_call(kernel, out_shape=shapes, in_specs=specs + [pl.BlockSpec(m...  37.7 us
    all_to_all x20, waiting for transfers between devices, exchange(): lax.all_to_all(packed, 'blk', 0, 0, axis_index_groups=self.groups, tiled=...  20.8 us
    all_to_all x1, blocking collectives, exchange(): lax.all_to_all(packed, 'blk', 0, 0, axis_index_groups=self.groups, tiled=...  13.8 us
  transfers between devices with their start and end apart: 57, of which 36 were waited for; matrix products, arithmetic and copies ran while one was open for 5% of the time, Pallas kernels for 2%

profile of v2, /device:TPU:0, one launch (start us, length us, event | category | flops | bytes accessed | tf_op | source)
XLA Modules:
  0.0 629.6 jit_solution(5778935152894313482)
XLA Ops:
  10.1 11.7 %collective-permute-done.2 = bf16[8,128,128]{2,1,0:T(8,128)(2,1)S(1)} collective-permute-done((bf16[8,128,128]{2,1,0:T(8,128)(2,1)S(1)}, bf16[8,128,128]{2,1,0:T(8,128)(2,1)S(1)}, u32[]{:S(2)}, u32[]{:S(2)}) %collective-permute-start.2) | collective-permute-done | bytes 262176 | tf_op jit(solution)/shard_map/ppermute | solution.py:304
  23.1 5.9 all-to-all-start.1
  38.4 17.1 %collective-permute-done.4.refs_3_.refs_4_ = bf16[8,128,128]{2,1,0:T(8,128)(2,1)S(1)} collective-permute-done((bf16[8,128,128]{2,1,0:T(8,128)(2,1)S(1)}, bf16[8,128,128]{2,1,0:T(8,128)(2,1)S(1)}, u32[]{:S(2)}, u32[]{:S(2)}) %collective-permute-start.4) | collective-permute-done | bytes 262176 | tf_op jit(solution)/shard_map/ppermute | solution.py:64
  65.9 12.0 %collective-permute-done.6.refs_3_.refs_5_ = bf16[8,128,128]{2,1,0:T(8,128)(2,1)S(1)} collective-permute-done((bf16[8,128,128]{2,1,0:T(8,128)(2,1)S(1)}, bf16[8,128,128]{2,1,0:T(8,128)(2,1)S(1)}, u32[]{:S(2)}, u32[]{:S(2)}) %collective-permute-start.6) | collective-permute-done | bytes 262176 | tf_op jit(solution)/shard_map/ppermute | solution.py:64
  87.8 14.7 %collective-permute-done.8.refs_3_.refs_4_ = bf16[8,128,128]{2,1,0:T(8,128)(2,1)S(1)} collective-permute-done((bf16[8,128,128]{2,1,0:T(8,128)(2,1)S(1)}, bf16[8,128,128]{2,1,0:T(8,128)(2,1)S(1)}, u32[]{:S(2)}, u32[]{:S(2)}) %collective-permute-start.8) | collective-permute-done | bytes 262176 | tf_op jit(solution)/shard_map/ppermute | solution.py:64
  113.1 18.4 %collective-permute-done.1 = bf16[8,128,128]{2,1,0:T(8,128)(2,1)S(1)} collective-permute-done((bf16[8,128,128]{2,1,0:T(8,128)(2,1)S(1)}, bf16[8,128,128]{2,1,0:T(8,128)(2,1)S(1)}, u32[]{:S(2)}, u32[]{:S(2)}) %collective-permute-start.1) | collective-permute-done | bytes 262176 | tf_op jit(solution)/shard_map/ppermute | solution.py:64
  145.2 15.1 %collective-permute-done.11.refs_3_.refs_4_ = bf16[8,128,128]{2,1,0:T(8,128)(2,1)S(1)} collective-permute-done((bf16[8,128,128]{2,1,0:T(8,128)(2,1)S(1)}, bf16[8,128,128]{2,1,0:T(8,128)(2,1)S(1)}, u32[]{:S(2)}, u32[]{:S(2)}) %collective-permute-start.11) | collective-permute-done | bytes 262176 | tf_op jit(solution)/shard_map/ppermute | solution.py:64
  168.4 14.6 %collective-permute-done.12.refs_3_.refs_5_ = bf16[8,128,128]{2,1,0:T(8,128)(2,1)S(1)} collective-permute-done((bf16[8,128,128]{2,1,0:T(8,128)(2,1)S(1)}, bf16[8,128,128]{2,1,0:T(8,128)(2,1)S(1)}, u32[]{:S(2)}, u32[]{:S(2)}) %collective-permute-start.12) | collective-permute-done | bytes 262176 | tf_op jit(solution)/shard_map/ppermute | solution.py:64
  192.2 14.5 %collective-permute-done.13.refs_3_.refs_4_ = bf16[8,128,128]{2,1,0:T(8,128)(2,1)S(1)} collective-permute-done((bf16[8,128,128]{2,1,0:T(8,128)(2,1)S(1)}, bf16[8,128,128]{2,1,0:T(8,128)(2,1)S(1)}, u32[]{:S(2)}, u32[]{:S(2)}) %collective-permute-start.13) | collective-permute-done | bytes 262176 | tf_op jit(solution)/shard_map/ppermute | solution.py:64
  215.0 14.5 %collective-permute-done.14.refs_4_.refs_5_ = bf16[8,128,128]{2,1,0:T(8,128)(2,1)S(1)} collective-permute-done((bf16[8,128,128]{2,1,0:T(8,128)(2,1)S(1)}, bf16[8,128,128]{2,1,0:T(8,128)(2,1)S(1)}, u32[]{:S(2)}, u32[]{:S(2)}) %collective-permute-start.14) | collective-permute-done | bytes 262176 | tf_op jit(solution)/shard_map/ppermute | solution.py:64
  239.0 14.2 %collective-permute-done.15.refs_3_.refs_4_ = bf16[8,128,128]{2,1,0:T(8,128)(2,1)S(1)} collective-permute-done((bf16[8,128,128]{2,1,0:T(8,128)(2,1)S(1)}, bf16[8,128,128]{2,1,0:T(8,128)(2,1)S(1)}, u32[]{:S(2)}, u32[]{:S(2)}) %collective-permute-start.15) | collective-permute-done | bytes 262176 | tf_op jit(solution)/shard_map/ppermute | solution.py:64
  262.0 10.9 %collective-permute-done.16.refs_3_.refs_5_ = bf16[8,128,128]{2,1,0:T(8,128)(2,1)S(1)} collective-permute-done((bf16[8,128,128]{2,1,0:T(8,128)(2,1)S(1)}, bf16[8,128,128]{2,1,0:T(8,128)(2,1)S(1)}, u32[]{:S(2)}, u32[]{:S(2)}) %collective-permute-start.16) | collective-permute-done | bytes 262176 | tf_op jit(solution)/shard_map/ppermute | solution.py:64
  287.3 12.9 %collective-permute-done = bf16[8,128,128]{2,1,0:T(8,128)(2,1)S(1)} collective-permute-done((bf16[8,128,128]{2,1,0:T(8,128)(2,1)S(1)}, bf16[8,128,128]{2,1,0:T(8,128)(2,1)S(1)}, u32[]{:S(2)}, u32[]{:S(2)}) %collective-permute-start) | collective-permute-done | bytes 262176 | tf_op jit(solution)/shard_map/ppermute | solution.py:64
  309.7 8.3 %collective-permute-done.17.refs_4_ = bf16[8,128,128]{2,1,0:T(8,128)(2,1)S(1)} collective-permute-done((bf16[8,128,128]{2,1,0:T(8,128)(2,1)}, bf16[8,128,128]{2,1,0:T(8,128)(2,1)S(1)}, u32[]{:S(2)}, u32[]{:S(2)}) %collective-permute-start.17) | collective-permute-done | bytes 262176 | tf_op jit(solution)/shard_map/ppermute | solution.py:64
  325.7 13.8 %all_to_all.115.refs_1_ = bf16[8,16,16,128]{3,2,1,0:T(8,128)(2,1)S(1)} all-to-all(bf16[8,16,16,128]{3,2,1,0:T(8,128)(2,1)S(1)} %get-tuple-element.74), channel_id=1, replica_groups={{0,1,2,3,4,5,6,7},{8,9,10,11,12,13,14,15},{16,17,18,19,20,21,22,23},{24..., dimensions={0} | all-to-all | bytes 1048576 | tf_op jit(solution)/shard_map/all_to_all | solution.py:61
  349.8 9.7 %collective-permute-done.18.refs_5_ = bf16[8,128,128]{2,1,0:T(8,128)(2,1)S(1)} collective-permute-done((bf16[8,128,128]{2,1,0:T(8,128)(2,1)}, bf16[8,128,128]{2,1,0:T(8,128)(2,1)S(1)}, u32[]{:S(2)}, u32[]{:S(2)}) %collective-permute-start.18) | collective-permute-done | bytes 262176 | tf_op jit(solution)/shard_map/ppermute | solution.py:64
  375.4 9.8 %collective-permute-done.19.refs_6_ = bf16[8,128,128]{2,1,0:T(8,128)(2,1)S(1)} collective-permute-done((bf16[8,128,128]{2,1,0:T(8,128)(2,1)}, bf16[8,128,128]{2,1,0:T(8,128)(2,1)S(1)}, u32[]{:S(2)}, u32[]{:S(2)}) %collective-permute-start.19) | collective-permute-done | bytes 262176 | tf_op jit(solution)/shard_map/ppermute | solution.py:64
  400.9 9.9 %collective-permute-done.21.refs_5_ = bf16[8,128,128]{2,1,0:T(8,128)(2,1)S(1)} collective-permute-done((bf16[8,128,128]{2,1,0:T(8,128)(2,1)}, bf16[8,128,128]{2,1,0:T(8,128)(2,1)S(1)}, u32[]{:S(2)}, u32[]{:S(2)}) %collective-permute-start.21) | collective-permute-done | bytes 262176 | tf_op jit(solution)/shard_map/ppermute | solution.py:64
  425.5 9.7 %collective-permute-done.20.refs_6_ = bf16[8,128,128]{2,1,0:T(8,128)(2,1)S(1)} collective-permute-done((bf16[8,128,128]{2,1,0:T(8,128)(2,1)S(1)}, bf16[8,128,128]{2,1,0:T(8,128)(2,1)S(1)}, u32[]{:S(2)}, u32[]{:S(2)}) %collective-permute-start.20) | collective-permute-done | bytes 262176 | tf_op jit(solution)/shard_map/ppermute | solution.py:64
  451.0 10.1 %collective-permute-done.23.refs_5_ = bf16[8,128,128]{2,1,0:T(8,128)(2,1)S(1)} collective-permute-done((bf16[8,128,128]{2,1,0:T(8,128)(2,1)}, bf16[8,128,128]{2,1,0:T(8,128)(2,1)S(1)}, u32[]{:S(2)}, u32[]{:S(2)}) %collective-permute-start.23) | collective-permute-done | bytes 262176 | tf_op jit(solution)/shard_map/ppermute | solution.py:64
  478.2 7.2 %collective-permute-done.24.refs_6_ = bf16[8,128,128]{2,1,0:T(8,128)(2,1)S(1)} collective-permute-done((bf16[8,128,128]{2,1,0:T(8,128)(2,1)}, bf16[8,128,128]{2,1,0:T(8,128)(2,1)S(1)}, u32[]{:S(2)}, u32[]{:S(2)}) %collective-permute-start.24) | collective-permute-done | bytes 262176 | tf_op jit(solution)/shard_map/ppermute | solution.py:64
  509.2 16.4 %collective-permute-done.26.refs_5_ = bf16[8,128,128]{2,1,0:T(8,128)(2,1)S(1)} collective-permute-done((bf16[8,128,128]{2,1,0:T(8,128)(2,1)S(1)}, bf16[8,128,128]{2,1,0:T(8,128)(2,1)S(1)}, u32[]{:S(2)}, u32[]{:S(2)}) %collective-permute-start.26) | collective-permute-done | bytes 262176 | tf_op jit(solution)/shard_map/ppermute | solution.py:64
  565.1 7.3 %collective-permute-done.34 = bf16[8,128,128]{2,1,0:T(8,128)(2,1)S(1)} collective-permute-done((bf16[8,128,128]{2,1,0:T(8,128)(2,1)}, bf16[8,128,128]{2,1,0:T(8,128)(2,1)S(1)}, u32[]{:S(2)}, u32[]{:S(2)}) %collective-permute-start.34) | collective-permute-done | bytes 262176 | tf_op jit(solution)/shard_map/ppermute | solution.py:364
  590.1 20.2 %collective-permute-done.30 = bf16[8,128,128]{2,1,0:T(8,128)(2,1)S(1)} collective-permute-done((bf16[8,128,128]{2,1,0:T(8,128)(2,1)S(1)}, bf16[8,128,128]{2,1,0:T(8,128)(2,1)S(1)}, u32[]{:S(2)}, u32[]{:S(2)}) %collective-permute-start.30) | collective-permute-done | bytes 262176 | tf_op jit(solution)/shard_map/ppermute | solution.py:64
  (411 shorter events, 327.1 us)
Async XLA Ops:
  0.7 21.2 %collective-permute-start.9 = (bf16[2,8,128,128]{3,2,1,0:T(8,128)(2,1)}, bf16[2,8,128,128]{3,2,1,0:T(8,128)(2,1)S(1)}, u32[]{:S(2)}, u32[]{:S(2)}) collective-permute-start(bf16[2,8,128,128]{3,2,1,0:T(8,128)(2,1)} %param.8), channel_id=1, source_target_pairs={{0,16},{16,0},{1,17},{17,1},{2,18},{18,2},{3,19},{19,3},{4,20},{20... | collective-permute-start | bytes 1572872 | tf_op jit(solution)/shard_map/ppermute | solution.py:275
  6.8 25.2 %collective-permute-start.3 = (bf16[2,8,128,128]{3,2,1,0:T(8,128)(2,1)S(1)}, bf16[2,8,128,128]{3,2,1,0:T(8,128)(2,1)}, u32[]{:S(2)}, u32[]{:S(2)}) collective-permute-start(bf16[2,8,128,128]{3,2,1,0:T(8,128)(2,1)S(1)} %copy-done.129), channel_id=1, source_target_pairs={{0,16},{16,0},{1,17},{17,1},{2,18},{18,2},{3,19},{19,3},{4,20},{20... | collective-permute-start | bytes 1572872 | tf_op jit(solution)/shard_map/ppermute | solution.py:275
  23.1 32.4 %all-to-all-start.1 = ((bf16[16,128,128]{2,1,0:T(8,128)(2,1)}), bf16[16,128,128]{2,1,0:T(8,128)(2,1)S(1)}, u32[]{:S(2)}, u32[]{:S(2)}) async-start(bf16[16,128,128]{2,1,0:T(8,128)(2,1)} %start_body.1), calls=%async_computation.1 | async-start | bytes 1048576 | tf_op jit(solution)/shard_map/all_to_all | solution.py:327
  33.2 22.4 %collective-permute-start.4 = (bf16[8,128,128]{2,1,0:T(8,128)(2,1)S(1)}, bf16[8,128,128]{2,1,0:T(8,128)(2,1)S(1)}, u32[]{:S(2)}, u32[]{:S(2)}) collective-permute-start(bf16[8,128,128]{2,1,0:T(8,128)(2,1)S(1)} %get-tuple-element.138.refs_2_.refs_3_), channel_id=1, source_target_pairs={{0,8},{1,9},{2,10},{3,11},{4,12},{5,13},{6,14},{7,15},{8,0},{9,1},... | collective-permute-start | bytes 786440 | tf_op jit(solution)/shard_map/ppermute | solution.py:64
  35.9 25.5 %collective-permute-start.5 = (bf16[2,8,128,128]{3,2,1,0:T(8,128)(2,1)}, bf16[2,8,128,128]{3,2,1,0:T(8,128)(2,1)}, u32[]{:S(2)}, u32[]{:S(2)}) collective-permute-start(bf16[2,8,128,128]{3,2,1,0:T(8,128)(2,1)} %param.10), channel_id=1, source_target_pairs={{0,16},{16,0},{1,17},{17,1},{2,18},{18,2},{3,19},{19,3},{4,20},{20... | collective-permute-start | bytes 1572872 | tf_op jit(solution)/shard_map/ppermute | solution.py:275
  57.9 20.0 %all-to-all-start.2 = ((bf16[8,16,16,128]{3,2,1,0:T(8,128)(2,1)}), bf16[8,16,16,128]{3,2,1,0:T(8,128)(2,1)S(1)}, u32[]{:S(2)}, u32[]{:S(2)}) async-start(bf16[8,16,16,128]{3,2,1,0:T(8,128)(2,1)} %copy-done.86), calls=%async_computation.2 | async-start | bytes 1048576 | tf_op jit(solution)/shard_map/all_to_all | solution.py:61
  63.4 22.0 %collective-permute-start.7 = (bf16[2,8,128,128]{3,2,1,0:T(8,128)(2,1)}, bf16[2,8,128,128]{3,2,1,0:T(8,128)(2,1)}, u32[]{:S(2)}, u32[]{:S(2)}) collective-permute-start(bf16[2,8,128,128]{3,2,1,0:T(8,128)(2,1)} %param.11), channel_id=1, source_target_pairs={{0,16},{16,0},{1,17},{17,1},{2,18},{18,2},{3,19},{19,3},{4,20},{20... | collective-permute-start | bytes 1572872 | tf_op jit(solution)/shard_map/ppermute | solution.py:275
  81.2 21.3 %all-to-all-start.3 = ((bf16[8,16,16,128]{3,2,1,0:T(8,128)(2,1)}), bf16[8,16,16,128]{3,2,1,0:T(8,128)(2,1)}, u32[]{:S(2)}, u32[]{:S(2)}) async-start(bf16[8,16,16,128]{3,2,1,0:T(8,128)(2,1)} %copy-done.87), calls=%async_computation.3 | async-start | bytes 1048576 | tf_op jit(solution)/shard_map/all_to_all | solution.py:61
  105.8 30.7 %all-to-all-start.4 = ((bf16[8,16,16,128]{3,2,1,0:T(8,128)(2,1)}), bf16[8,16,16,128]{3,2,1,0:T(8,128)(2,1)}, u32[]{:S(2)}, u32[]{:S(2)}) async-start(bf16[8,16,16,128]{3,2,1,0:T(8,128)(2,1)} %copy-done.84), calls=%async_computation.4 | async-start | bytes 1048576 | tf_op jit(solution)/shard_map/all_to_all | solution.py:61
  110.1 21.4 %collective-permute-start.1 = (bf16[8,128,128]{2,1,0:T(8,128)(2,1)S(1)}, bf16[8,128,128]{2,1,0:T(8,128)(2,1)S(1)}, u32[]{:S(2)}, u32[]{:S(2)}) collective-permute-start(bf16[8,128,128]{2,1,0:T(8,128)(2,1)S(1)} %get-tuple-element.143), channel_id=1, source_target_pairs={{0,8},{1,9},{2,10},{3,11},{4,12},{5,13},{6,14},{7,15},{8,0},{9,1},... | collective-permute-start | bytes 786440 | tf_op jit(solution)/shard_map/ppermute | solution.py:64
  110.4 26.1 %collective-permute-start.10 = (bf16[8,128,128]{2,1,0:T(8,128)(2,1)S(1)}, bf16[8,128,128]{2,1,0:T(8,128)(2,1)S(1)}, u32[]{:S(2)}, u32[]{:S(2)}) collective-permute-start(bf16[8,128,128]{2,1,0:T(8,128)(2,1)S(1)} %get-tuple-element.140.refs_3_.refs_4_), channel_id=1, source_target_pairs={{0,8},{1,9},{2,10},{3,11},{4,12},{5,13},{6,14},{7,15},{8,0},{9,1},... | collective-permute-start | bytes 786440 | tf_op jit(solution)/shard_map/ppermute | solution.py:64
  210.1 20.2 %all-to-all-start.8 = ((bf16[8,16,16,128]{3,2,1,0:T(8,128)(2,1)}), bf16[8,16,16,128]{3,2,1,0:T(8,128)(2,1)}, u32[]{:S(2)}, u32[]{:S(2)}) async-start(bf16[8,16,16,128]{3,2,1,0:T(8,128)(2,1)} %copy-done.96), calls=%async_computation.8 | async-start | bytes 1048576 | tf_op jit(solution)/shard_map/all_to_all | solution.py:61
  279.2 22.4 %all-to-all-start.11 = ((bf16[8,16,16,128]{3,2,1,0:T(8,128)(2,1)}), bf16[8,16,16,128]{3,2,1,0:T(8,128)(2,1)}, u32[]{:S(2)}, u32[]{:S(2)}) async-start(bf16[8,16,16,128]{3,2,1,0:T(8,128)(2,1)} %copy-done.85), calls=%async_computation.11 | async-start | bytes 1048576 | tf_op jit(solution)/shard_map/all_to_all | solution.py:61
  367.7 19.6 %all-to-all-start.14 = ((bf16[8,16,16,128]{3,2,1,0:T(8,128)(2,1)}), bf16[8,16,16,128]{3,2,1,0:T(8,128)(2,1)}, u32[]{:S(2)}, u32[]{:S(2)}) async-start(bf16[8,16,16,128]{3,2,1,0:T(8,128)(2,1)} %copy-done.92), calls=%async_computation.14 | async-start | bytes 1048576 | tf_op jit(solution)/shard_map/all_to_all | solution.py:61
  493.8 31.9 %all-to-all-start.19 = ((bf16[8,16,16,128]{3,2,1,0:T(8,128)(2,1)}), bf16[8,16,16,128]{3,2,1,0:T(8,128)(2,1)}, u32[]{:S(2)}, u32[]{:S(2)}) async-start(bf16[8,16,16,128]{3,2,1,0:T(8,128)(2,1)} %copy-done.82), calls=%async_computation.19 | async-start | bytes 1048576 | tf_op jit(solution)/shard_map/all_to_all | solution.py:61
  501.9 61.4 %collective-permute-start.22 = (bf16[4,8,128,128]{3,2,1,0:T(8,128)(2,1)}, bf16[4,8,128,128]{3,2,1,0:T(8,128)(2,1)}, u32[]{:S(2)}, u32[]{:S(2)}) collective-permute-start(bf16[4,8,128,128]{3,2,1,0:T(8,128)(2,1)} %pad_maximum_fusion), channel_id=1, source_target_pairs={{0,16},{16,0},{1,17},{17,1},{2,18},{18,2},{3,19},{19,3},{4,20},{20... | collective-permute-start | bytes 3145736 | tf_op jit(solution)/shard_map/ppermute | solution.py:275
  504.4 21.3 %collective-permute-start.26 = (bf16[8,128,128]{2,1,0:T(8,128)(2,1)S(1)}, bf16[8,128,128]{2,1,0:T(8,128)(2,1)S(1)}, u32[]{:S(2)}, u32[]{:S(2)}) collective-permute-start(bf16[8,128,128]{2,1,0:T(8,128)(2,1)S(1)} %copy-done.113), channel_id=1, source_target_pairs={{0,8},{1,9},{2,10},{3,11},{4,12},{5,13},{6,14},{7,15},{8,0},{9,1},... | collective-permute-start | bytes 786440 | tf_op jit(solution)/shard_map/ppermute | solution.py:64
  509.0 28.1 %collective-permute-start.25 = (bf16[8,128,128]{2,1,0:T(8,128)(2,1)}, bf16[8,128,128]{2,1,0:T(8,128)(2,1)S(1)}, u32[]{:S(2)}, u32[]{:S(2)}) collective-permute-start(bf16[8,128,128]{2,1,0:T(8,128)(2,1)} %get-tuple-element.101), channel_id=1, source_target_pairs={{0,8},{1,9},{2,10},{3,11},{4,12},{5,13},{6,14},{7,15},{8,0},{9,1},... | collective-permute-start | bytes 786440 | tf_op jit(solution)/shard_map/ppermute | solution.py:64
  539.3 25.7 %collective-permute-start.27 = (bf16[4,8,128,128]{3,2,1,0:T(8,128)(2,1)}, bf16[4,8,128,128]{3,2,1,0:T(8,128)(2,1)}, u32[]{:S(2)}, u32[]{:S(2)}) collective-permute-start(bf16[4,8,128,128]{3,2,1,0:T(8,128)(2,1)} %pad_maximum_fusion.1), channel_id=1, source_target_pairs={{0,16},{16,0},{1,17},{17,1},{2,18},{18,2},{3,19},{19,3},{4,20},{20... | collective-permute-start | bytes 3145736 | tf_op jit(solution)/shard_map/ppermute | solution.py:275
  539.4 20.5 %collective-permute-start.28 = (bf16[8,128,128]{2,1,0:T(8,128)(2,1)}, bf16[8,128,128]{2,1,0:T(8,128)(2,1)S(1)}, u32[]{:S(2)}, u32[]{:S(2)}) collective-permute-start(bf16[8,128,128]{2,1,0:T(8,128)(2,1)} %get-tuple-element.113), channel_id=1, source_target_pairs={{0,8},{1,9},{2,10},{3,11},{4,12},{5,13},{6,14},{7,15},{8,0},{9,1},... | collective-permute-start | bytes 786440 | tf_op jit(solution)/shard_map/ppermute | solution.py:64
  563.2 23.4 %collective-permute-start.32 = (bf16[8,128,128]{2,1,0:T(8,128)(2,1)}, bf16[8,128,128]{2,1,0:T(8,128)(2,1)}, u32[]{:S(2)}, u32[]{:S(2)}) collective-permute-start(bf16[8,128,128]{2,1,0:T(8,128)(2,1)} %get-tuple-element.120), channel_id=1, source_target_pairs={{0,8},{1,9},{2,10},{3,11},{4,12},{5,13},{6,14},{7,15},{8,0},{9,1},... | collective-permute-start | bytes 786440 | tf_op jit(solution)/shard_map/ppermute | solution.py:64
  579.6 35.3 %all-to-all-start.22 = ((bf16[16,128,128]{2,1,0:T(8,128)(2,1)}), bf16[16,128,128]{2,1,0:T(8,128)(2,1)S(1)}, u32[]{:S(2)}, u32[]{:S(2)}) async-start(bf16[16,128,128]{2,1,0:T(8,128)(2,1)} %copy-done.81), calls=%async_computation.22 | async-start | bytes 1048576 | tf_op jit(solution)/shard_map/all_to_all | solution.py:385
  583.7 26.5 %collective-permute-start.30 = (bf16[8,128,128]{2,1,0:T(8,128)(2,1)S(1)}, bf16[8,128,128]{2,1,0:T(8,128)(2,1)S(1)}, u32[]{:S(2)}, u32[]{:S(2)}) collective-permute-start(bf16[8,128,128]{2,1,0:T(8,128)(2,1)S(1)} %get-tuple-element.118), channel_id=1, source_target_pairs={{0,8},{1,9},{2,10},{3,11},{4,12},{5,13},{6,14},{7,15},{8,0},{9,1},... | collective-permute-start | bytes 786440 | tf_op jit(solution)/shard_map/ppermute | solution.py:64
  587.7 24.7 %collective-permute-start.33 = (bf16[8,128,128]{2,1,0:T(8,128)(2,1)S(1)}, bf16[8,128,128]{2,1,0:T(8,128)(2,1)S(1)}, u32[]{:S(2)}, u32[]{:S(2)}) collective-permute-start(bf16[8,128,128]{2,1,0:T(8,128)(2,1)S(1)} %fusion.9), channel_id=1, source_target_pairs={{16,0},{17,1},{18,2},{19,3},{20,4},{21,5},{22,6},{23,7},{24,8},{25... | collective-permute-start | bytes 786440 | tf_op jit(solution)/shard_map/ppermute | solution.py:364
  (164 other events, 1012.0 us)

commit v3 on v2

v3 whole, which is shorter than its diff:
```python
import functools
import math

import jax
import jax.numpy as jnp
from jax import lax
from jax.experimental import pallas as pl
from jax.experimental.pallas import tpu as pltpu
from jax.sharding import PartitionSpec as P

F32 = jnp.float32
BF16 = jnp.bfloat16
ROOT = math.sqrt(2.0 / math.pi)


def gelu(u):
    return 0.5 * u * (1.0 + jnp.tanh(ROOT * (u + 0.044715 * (u * u * u))))


def gelu_slope(u):
    square = u * u
    th = jnp.tanh(ROOT * (u + 0.044715 * (u * square)))
    inner = ROOT * (1.0 + 3 * 0.044715 * square)
    return 0.5 * (1.0 + th) + 0.5 * u * (1.0 - th * th) * inner


class Plan:
    def __init__(self, segments, devices, micros, blocks, tokens):
        self.segments = segments
        self.devices = devices
        self.halves = 2 if micros * tokens >= 256 * segments and devices % 2 == 0 else 1
        self.group = devices // self.halves
        self.own = blocks // devices
        self.held = self.own * self.halves
        self.size = blocks
        self.tokens = micros * tokens // (segments * self.halves)
        self.kernels = segments == 2 and micros == 2 and self.own == 8 and tokens % 128 == 0
        self.groups = None
        if self.halves > 1:
            self.groups = [
                [half * self.group + rank for rank in range(self.group)]
                for half in range(self.halves)
            ]

    def packed_shape(self):
        return (self.group, self.held, self.held, self.tokens)

    def natural_shape(self):
        return (self.held, self.size, self.tokens)

    def pack(self, values):
        split = values.reshape(self.held, self.halves, self.group, self.own, self.tokens)
        return split.transpose(2, 1, 3, 0, 4).reshape(self.packed_shape())

    def unpack(self, packed):
        split = packed.reshape(self.group, self.held, self.halves, self.own, self.tokens)
        return split.transpose(1, 2, 0, 3, 4).reshape(self.natural_shape())

    def exchange(self, packed):
        return lax.all_to_all(packed, "blk", 0, 0, axis_index_groups=self.groups, tiled=True)

    def swap_halves(self, value):
        return lax.ppermute(
            value, "blk", [(at, (at + self.group) % self.devices) for at in range(self.devices)]
        )


def matmul(a, b, over_a, over_b):
    return lax.dot_general(a, b, (((over_a,), (over_b,)), ((), ())), preferred_element_type=F32)


def read(plan, ref, at):
    pair = slice(at // 2 * 2 * plan.own, (at // 2 + 1) * 2 * plan.own)
    rows = ref[:, pair].astype(F32)[:, at % 2 * plan.own : (at % 2 + 1) * plan.own]
    return rows.reshape(plan.size, rows.shape[-1])


def start_work(plan, at, scatter, weight, gradient, state):
    scatter(matmul(weight, state[at], 0, 0))


def residual_work(plan, at, scatter, weight, gradient, branch, state, result):
    total = (state[at].astype(F32) + read(plan, branch, at)).astype(BF16)
    result[at] = total
    scatter(matmul(weight, total, 0, 0))


def left_work(plan, at, scatter, weight, gradient, values, kept):
    natural = read(plan, values, at).astype(BF16)
    kept[at] = natural
    scatter(matmul(weight, natural, 0, 0))


def gelu_work(plan, at, scatter, weight, gradient, values, upper, hidden):
    natural = read(plan, values, at)
    upper[at] = natural.astype(BF16)
    active = gelu(natural).astype(BF16)
    hidden[at] = active
    scatter(matmul(weight, active, 0, 0))


def pack_work(plan, at, scatter, weight, gradient, values):
    scatter(values[at].astype(F32))


def unpack_work(plan, at, scatter, weight, gradient, values, out):
    out[at] = read(plan, values, at).astype(BF16)


def back_left_work(plan, at, scatter, weight, gradient, grad, kept):
    natural = read(plan, grad, at).astype(BF16)
    scatter(matmul(weight, natural, 1, 0))
    gradient(matmul(kept[at], natural, 1, 1))


def back_gelu_work(plan, at, scatter, weight, gradient, grad, hidden, upper):
    natural = read(plan, grad, at).astype(BF16)
    grad_hidden = matmul(weight, natural, 1, 0)
    scatter(grad_hidden * gelu_slope(upper[at].astype(F32)))
    gradient(matmul(hidden[at], natural, 1, 1))


def back_right_work(plan, at, scatter, weight, gradient, grad, state, above, result):
    natural = read(plan, grad, at).astype(BF16)
    total = matmul(weight, natural, 1, 0) + above[at].astype(F32)
    result[at] = total.astype(BF16)
    scatter(total)
    gradient(matmul(state[at], natural, 1, 1))


def end_work(plan, at, scatter, weight, gradient, grad, state):
    natural = read(plan, grad, at).astype(BF16)
    gradient(matmul(state[at], natural, 1, 1))


class Kernels:
    def __init__(self, plan, tokens, picks):
        self.plan = plan
        self.picks = picks
        self.tokens = tokens
        self.natural = (plan.own, plan.size, tokens)
        self.sent = (plan.devices, plan.own * plan.own, tokens)
        self.square = (plan.own, plan.size, plan.size)

    def run(self, work, ins, packed=0, weight=None, send=True, naturals=0, grads=False, after=()):
        plan, tokens, picks = self.plan, self.tokens, self.picks
        turn_blocks = plan.own // 2
        natural = pl.BlockSpec((turn_blocks,) + self.natural[1:], lambda turn, picks: (turn, 0, 0))
        arrived = pl.BlockSpec(
            (plan.devices, turn_blocks * plan.own, tokens), lambda turn, picks: (0, turn, 0)
        )
        square = (turn_blocks,) + self.square[1:]
        in_specs = [arrived] * packed + [natural] * (len(ins) - packed)
        operands = list(ins)
        layer, mine, theirs = weight or (0, None, None)
        matrices = [m for m in (mine, theirs) if m is not None]
        for matrix in matrices:
            operands.append(matrix)
            if len(matrix.shape) == 4:
                spec = pl.BlockSpec(
                    (None,) + square, lambda turn, picks: (picks[2 * layer], turn, 0, 0)
                )
            else:
                spec = pl.BlockSpec(square, lambda turn, picks: (turn, 0, 0))
            in_specs.append(spec)
        operands += after
        in_specs += [pl.BlockSpec(memory_space=pl.ANY)] * len(after)
        outs, out_specs, scratch = [], [], []
        if send:
            outs.append(jax.ShapeDtypeStruct(self.sent, BF16))
            out_specs.append(pl.BlockSpec(self.sent, lambda turn, picks: (0, 0, 0)))
            scratch.append(pltpu.VMEM((tokens // 128, plan.size * plan.own, 128), F32))
        outs += [jax.ShapeDtypeStruct(self.natural, BF16)] * naturals
        out_specs += [natural] * naturals
        if grads:
            outs += [jax.ShapeDtypeStruct(self.square, dtype) for dtype in (F32, BF16)]
            out_specs += [pl.BlockSpec(square, lambda turn, picks: (turn, 0, 0))] * 2

        def kernel(picks, *refs):
            refs = list(refs)
            turn = pl.program_id(0)
            inner = [refs.pop(0) for i in ins]
            factors = [refs.pop(0) for i in matrices]
            del refs[: len(after)]
            out = refs.pop(0) if send else None
            inner += [refs.pop(0) for i in range(naturals)]
            gradients = [refs.pop(0) for i in range(2 if grads else 0)]
            store = refs[0] if send else None

            def scatter(at, values):
                rows = pl.ds(turn * turn_blocks + at, plan.size, stride=plan.own)
                for part in range(tokens // 128):
                    store[part, rows, :] = values[:, part * 128 : (part + 1) * 128]

            def gradient(at, values):
                for ref in gradients:
                    ref[at] = values.astype(ref.dtype)

            here = picks[2 * layer + 1] == 1
            for at in range(turn_blocks):
                matrix = None
                if len(factors) == 2:
                    matrix = jnp.where(here, factors[0][at], factors[1][at])
                elif factors:
                    matrix = factors[0][at]
                put = functools.partial(scatter, at)
                work(plan, at, put, matrix, functools.partial(gradient, at), *inner)
            if send:

                @pl.when(turn == 1)
                def _():
                    for part in range(tokens // 128):
                        rows = store[part].astype(BF16)
                        rows = rows.reshape(plan.devices, plan.own * plan.own, 128)
                        out[:, :, part * 128 : (part + 1) * 128] = rows

        volume = sum(math.prod(i.shape) * i.dtype.itemsize for i in ins)
        volume += sum(math.prod(o.shape) * o.dtype.itemsize for o in outs)
        products = (1 if matrices else 0) + (1 if grads else 0)
        flops = products * 2 * plan.own * plan.size * plan.size * tokens
        return pl.pallas_call(
            kernel,
            out_shape=outs,
            grid_spec=pltpu.PrefetchScalarGridSpec(
                num_scalar_prefetch=1,
                grid=(2,),
                in_specs=in_specs,
                out_specs=out_specs,
                scratch_shapes=scratch,
            ),
            compiler_params=pltpu.CompilerParams(
                vmem_limit_bytes=60 * 1024 * 1024, dimension_semantics=("arbitrary",)
            ),
            cost_estimate=pl.CostEstimate(flops=flops, bytes_accessed=volume, transcendentals=0),
            name=work.__name__,
        )(picks, *operands)


def two_segments(plan, inputs, factors, cotangent, sections):
    segment = lax.axis_index("segment")
    both = [(0, 1), (1, 0)]
    count = 3

    owners = [jnp.int32(0), 2 - sections[0], jnp.int32(1)]
    slots = [jnp.int32(0), sections[0] - 1, sections[1] - 1]
    picks = []
    for owner, slot in zip(owners, slots):
        picks += [jnp.clip(slot, 0, 1), (owner == segment).astype(jnp.int32)]
    kernels = Kernels(plan, inputs.shape[3], jnp.stack(picks).astype(jnp.int32))
    run = kernels.run

    def exchange(value):
        return lax.all_to_all(value, "blk", 0, 0, tiled=True)

    micro = lax.dynamic_index_in_dim(inputs, segment, 0, keepdims=False)
    grad = lax.dynamic_index_in_dim(cotangent, segment, 0, keepdims=False)
    early = lax.ppermute(factors[0][0], "segment", [(0, 1)])
    early = jnp.where(segment == 0, factors[0][0], early)
    received = [lax.ppermute(factor, "segment", both) for factor in factors]

    def weight(layer, at):
        if layer == 0 and at == 0:
            return layer, early, None
        return layer, factors[at], received[at]

    saved = []
    state, branch = micro, None
    for layer in range(count):
        if layer == 0:
            sent = run(start_work, (state,), 0, weight(0, 0))[0]
        else:
            sent, state = run(residual_work, (branch, state), 1, weight(layer, 0), naturals=1)
        sent, inner = run(left_work, (exchange(sent),), 1, weight(layer, 1), naturals=1)
        sent, upper, hidden = run(gelu_work, (exchange(sent),), 1, weight(layer, 2), naturals=2)
        values = exchange(sent)
        if layer < count - 1:
            sent, inner_two = run(left_work, (values,), 1, weight(layer, 3), naturals=1)
            branch = exchange(sent)
        else:
            inner_two = run(unpack_work, (values,), 1, send=False, naturals=1)[0]
        saved.append((state, inner, upper, hidden, inner_two))

    waiting = [(), ()]
    parts = [[None] * 4 for layer in range(count)]

    def step(layer, at, work, ins, naturals=0):
        after = waiting.pop(0)
        use = weight(layer, at)
        *results, stay, leave = run(work, ins, 1, use, True, naturals, True, after)
        other = lax.ppermute(leave, "segment", [(1, 0)] if layer == 0 else both)
        waiting.append((other,))
        parts[layer][at] = (stay, other)
        return results if naturals else results[0]

    sent = run(pack_work, (grad,))[0]
    for layer in reversed(range(count)):
        state, inner, upper, hidden, inner_two = saved[layer]
        sent = step(layer, 3, back_left_work, (exchange(sent), inner_two))
        sent = step(layer, 2, back_gelu_work, (exchange(sent), hidden, upper))
        sent = step(layer, 1, back_left_work, (exchange(sent), inner))
        if layer > 0:
            ins = (exchange(sent), state, grad)
            sent, grad = step(layer, 0, back_right_work, ins, 1)
    ins = (exchange(sent), state)
    stay, leave = run(end_work, ins, 1, send=False, grads=True, after=waiting.pop(0))
    parts[0][0] = (stay, lax.ppermute(leave, "segment", [(1, 0)]))

    outs = []
    first_has_two = sections[0] == 2
    for at in range(4):
        zero, one, two = [stay + other.astype(F32) for stay, other in (p[at] for p in parts)]
        low = jnp.where(segment == 0, zero, jnp.where(first_has_two, two, one))
        high = jnp.where(segment == 0, one, two)
        high = jnp.where(first_has_two == (segment == 0), high, 0.0)
        outs.append(jnp.stack([low, high]))
    return tuple(outs)


def apply(weight, values):
    return jnp.einsum("bij,bit->bjt", weight, values, preferred_element_type=F32)


def apply_back(weight, values):
    return jnp.einsum("bij,bjt->bit", weight, values, preferred_element_type=F32)


def outer(values, grad):
    return jnp.einsum("bit,bjt->bij", values, grad, preferred_element_type=F32).astype(BF16)


def spread(plan, factor, owner, half):
    every = lax.all_gather(factor, "segment", axis=0)
    factor = lax.dynamic_index_in_dim(every, owner, 0, keepdims=False)
    if plan.halves == 1:
        return factor
    other = plan.swap_halves(factor)
    lower = jnp.where(half == 0, factor, other)
    upper = jnp.where(half == 0, other, factor)
    return jnp.concatenate([lower, upper], axis=1)


def collect(plan, parts, half):
    if plan.halves == 1:
        return lax.psum(parts.astype(F32), "segment")
    lower, upper = parts[:, : plan.own], parts[:, plan.own :]
    kept = jnp.where(half == 0, lower, upper)
    other = plan.swap_halves(jnp.where(half == 0, upper, lower))
    return lax.psum(kept.astype(F32) + other.astype(F32), "segment")


def token_chunk(plan, values, half):
    mine = lax.axis_index("segment")
    per_micro = values.shape[-1] // plan.tokens

    def chunk(at):
        at = mine * plan.halves + at
        micro = lax.dynamic_index_in_dim(values, at // per_micro, 0, keepdims=False)
        start = (at % per_micro) * plan.tokens
        return lax.dynamic_slice_in_dim(micro, start, plan.tokens, 2)

    if plan.halves == 1:
        return chunk(0)
    kept, other = chunk(half), plan.swap_halves(chunk(1 - half))
    lower = jnp.where(half == 0, kept, other)
    upper = jnp.where(half == 0, other, kept)
    return jnp.concatenate([lower, upper], axis=0)


def many_segments(plan, inputs, factors, cotangent, sections):
    segment = lax.axis_index("segment")
    half = lax.axis_index("blk") // plan.group
    slots = factors[0].shape[0]

    def trade(values):
        return plan.unpack(plan.exchange(plan.pack(values.astype(BF16))))

    count = plan.segments * slots - 1
    ends = jnp.cumsum(sections)
    layers, weights = [], []
    for index in range(count):
        owner = jnp.minimum(jnp.sum((index >= ends).astype(jnp.int32)), plan.segments - 1)
        slot = jnp.clip(index - (ends[owner] - sections[owner]), 0, slots - 1)
        layers.append((owner, slot, index < ends[-1]))
        picked = [lax.dynamic_index_in_dim(f, slot, 0, keepdims=True) for f in factors]
        weights.append(spread(plan, jnp.concatenate(picked, axis=0), owner, half))

    state = token_chunk(plan, inputs, half)
    grad = token_chunk(plan, cotangent, half)
    saved = []
    for index in range(count):
        w = weights[index]
        inner_one = trade(apply(w[0], state))
        upper = trade(apply(w[1], inner_one))
        hidden = gelu(upper.astype(F32)).astype(BF16)
        inner_two = trade(apply(w[2], hidden))
        saved.append((state, inner_one, upper, hidden, inner_two))
        if index < count - 1:
            branch = trade(apply(w[3], inner_two))
            total = (state.astype(F32) + branch.astype(F32)).astype(BF16)
            state = jnp.where(layers[index][2], total, state)

    totals = [None] * count
    for index in reversed(range(count)):
        w = weights[index]
        state, inner_one, upper, hidden, inner_two = saved[index]
        grad_c = trade(grad)
        grad_a = trade(apply_back(w[3], grad_c))
        parts = [outer(hidden, grad_a), outer(inner_two, grad_c)]
        grad_u = apply_back(w[2], grad_a) * gelu_slope(upper.astype(F32))
        grad_c = trade(grad_u)
        grad_a = trade(apply_back(w[1], grad_c))
        parts = [outer(state, grad_a), outer(inner_one, grad_c)] + parts
        totals[index] = collect(plan, jnp.stack(parts), half)
        total = (apply_back(w[0], grad_a) + grad.astype(F32)).astype(BF16)
        grad = jnp.where(layers[index][2], total, grad)

    outs = []
    for at in range(4):
        rows = []
        for place in range(slots):
            total = jnp.zeros(factors[0].shape[1:], F32)
            for index, (owner, slot, active) in enumerate(layers):
                here = active & (owner == segment) & (slot == place)
                total = jnp.where(here, totals[index][at], total)
            rows.append(total)
        outs.append(jnp.stack(rows))
    return tuple(outs)


def shards(inputs, first_right, first_left, second_right, second_left, cotangent, sections):
    segments = lax.axis_size("segment")
    devices = lax.axis_size("blk")
    plan = Plan(segments, devices, inputs.shape[0], inputs.shape[2], inputs.shape[3])
    factors = (first_right, first_left, second_right, second_left)
    run = two_segments if plan.kernels else many_segments
    return run(plan, inputs, factors, cotangent, sections)


def solution(mesh):
    whole = P("segment", "blk", None, None)
    tokens = P(None, "blk", None, None)
    in_specs = (tokens, whole, whole, whole, whole, tokens, P())
    return jax.shard_map(
        shards, mesh=mesh, in_specs=in_specs, out_specs=(whole,) * 4, check_vma=False
    )
```

time: 634 us -> 562 us (0.89)
  blocking collectives: 13.8 us -> 133 us
  waiting for transfers between devices: 316 us -> 202 us
  local copies, waits for them, and re-layouts: 75.3 us -> 20.7 us
  starting transfers between devices: 154 us -> 106 us
  Pallas kernels: 37.7 us -> 85 us
  other arithmetic: 29.4 us -> 7.85 us
    ppermute x35 -> x17, waiting for transfers between devices: 295 us -> 128 us  [the longest x11 70.7 us: step(): other = lax.ppermute(leave, 'segment', [(1, 0)] if layer == 0 else both)]
    all_to_all x1 -> x7, blocking collectives: 13.8 us -> 133 us  [exchange(): return lax.all_to_all(value, 'blk', 0, 0, tiled=True)]
    unnamed x262 -> x130, local copies, waits for them, and re-layouts: 72.6 us -> 16.7 us
    all_to_all x22 -> x16, waiting for transfers between devices: 20.8 us -> 74.2 us  [exchange(): return lax.all_to_all(value, 'blk', 0, 0, tiled=True)]
    pallas_call x25, Pallas kernels: 37.7 us -> 85 us  [run(): pl.pallas_call(kernel, out_shape=outs, grid_spec=pltpu.PrefetchScalarGrid...]
    ppermute x35 -> x17, starting transfers between devices: 57.6 us -> 32.4 us  [the longest x11 18.3 us: step(): other = lax.ppermute(leave, 'segment', [(1, 0)] if layer == 0 else both)]
    all_to_all x22 -> x16, starting transfers between devices: 96.1 us -> 73.9 us  [exchange(): return lax.all_to_all(value, 'blk', 0, 0, tiled=True)]
    another operation x18 -> x8, other arithmetic: 20.2 us -> 7.12 us  [two_segments(): outs.append(jnp.stack([low, high]))]
  transfers between devices with their start and end apart: 57 -> 33, of which waited for: 36 -> 31; matrix products, arithmetic and copies ran while one was open for 5% -> 2% of each run, Pallas kernels for 2% -> 1%
where the time goes in v3:
time: 562 us; the launch traced here: 558 us
  waiting for transfers between devices  202 us (36%)
  blocking collectives  133 us (24%)
  starting transfers between devices  106 us (19%)
  Pallas kernels  85 us (15%)
  local copies, waits for them, and re-layouts  20.7 us (4%)
  other arithmetic  7.85 us (1%)
    all_to_all x7, blocking collectives, exchange(): return lax.all_to_all(value, 'blk', 0, 0, tiled=True)  133 us
    pallas_call x25, Pallas kernels, run(): pl.pallas_call(kernel, out_shape=outs, grid_spec=pltpu.PrefetchScalarGrid...  85 us
    all_to_all x16, waiting for transfers between devices, exchange(): return lax.all_to_all(value, 'blk', 0, 0, tiled=True)  74.2 us
    all_to_all x16, starting transfers between devices, exchange(): return lax.all_to_all(value, 'blk', 0, 0, tiled=True)  73.9 us
    ppermute x11, waiting for transfers between devices, step(): other = lax.ppermute(leave, 'segment', [(1, 0)] if layer == 0 else both)  70.7 us
    ppermute x4, waiting for transfers between devices, two_segments(): received = [lax.ppermute(factor, 'segment', both) for factor in factors]  50 us
    ppermute x11, starting transfers between devices, step(): other = lax.ppermute(leave, 'segment', [(1, 0)] if layer == 0 else both)  18.3 us
    unnamed x130, local copies, waits for them, and re-layouts  16.7 us
  transfers between devices with their start and end apart: 33, of which 31 were waited for; matrix products, arithmetic and copies ran while one was open for 2% of the time, Pallas kernels for 1%

profile of v3, /device:TPU:0, one launch (start us, length us, event | category | flops | bytes accessed | tf_op | source)
XLA Modules:
  0.0 558.5 jit_solution(12977631161674044407)
XLA Ops:
  24.5 12.5 %collective-permute-done.1.refs_2_.refs_3_ = bf16[2,8,128,128]{3,2,1,0:T(8,128)(2,1)S(1)} collective-permute-done((bf16[2,8,128,128]{3,2,1,0:T(8,128)(2,1)S(1)}, bf16[2,8,128,128]{3,2,1,0:T(8,128)(2,1)S(1)}, u32[]{:S(2)}, u32[]{:S(2)}) %collective-permute-start.1) | collective-permute-done | bytes 524320 | tf_op jit(solution)/shard_map/ppermute | solution.py:259
  49.6 12.5 %collective-permute-done.2.refs_2_.refs_4_ = bf16[2,8,128,128]{3,2,1,0:T(8,128)(2,1)S(1)} collective-permute-done((bf16[2,8,128,128]{3,2,1,0:T(8,128)(2,1)S(1)}, bf16[2,8,128,128]{3,2,1,0:T(8,128)(2,1)S(1)}, u32[]{:S(2)}, u32[]{:S(2)}) %collective-permute-start.2) | collective-permute-done | bytes 524320 | tf_op jit(solution)/shard_map/ppermute | solution.py:259
  75.0 12.5 %collective-permute-done.3.refs_2_.refs_3_ = bf16[2,8,128,128]{3,2,1,0:T(8,128)(2,1)S(1)} collective-permute-done((bf16[2,8,128,128]{3,2,1,0:T(8,128)(2,1)S(1)}, bf16[2,8,128,128]{3,2,1,0:T(8,128)(2,1)S(1)}, u32[]{:S(2)}, u32[]{:S(2)}) %collective-permute-start.3) | collective-permute-done | bytes 524320 | tf_op jit(solution)/shard_map/ppermute | solution.py:259
  99.9 12.4 %collective-permute-done.4.refs_3_.refs_4_ = bf16[2,8,128,128]{3,2,1,0:T(8,128)(2,1)S(1)} collective-permute-done((bf16[2,8,128,128]{3,2,1,0:T(8,128)(2,1)S(1)}, bf16[2,8,128,128]{3,2,1,0:T(8,128)(2,1)S(1)}, u32[]{:S(2)}, u32[]{:S(2)}) %collective-permute-start.4) | collective-permute-done | bytes 524320 | tf_op jit(solution)/shard_map/ppermute | solution.py:259
  117.2 20.3 %all_to_all.115.refs_0_ = bf16[16,64,256]{2,1,0:T(8,128)(2,1)} all-to-all(bf16[16,64,256]{2,1,0:T(8,128)(2,1)} %get-tuple-element.66), channel_id=1, replica_groups=mesh['segment'=2,'blk'=16] {'blk'}, dimensions={0} | all-to-all | bytes 1048576 | tf_op jit(solution)/shard_map/all_to_all | solution.py:253
  140.9 18.7 %all_to_all.116.refs_0_ = bf16[16,64,256]{2,1,0:T(8,128)(2,1)} all-to-all(bf16[16,64,256]{2,1,0:T(8,128)(2,1)} %get-tuple-element.67), channel_id=1, replica_groups=mesh['segment'=2,'blk'=16] {'blk'}, dimensions={0} | all-to-all | bytes 1048576 | tf_op jit(solution)/shard_map/all_to_all | solution.py:253
  163.2 18.7 %all_to_all.117.refs_0_ = bf16[16,64,256]{2,1,0:T(8,128)(2,1)} all-to-all(bf16[16,64,256]{2,1,0:T(8,128)(2,1)} %get-tuple-element.68), channel_id=1, replica_groups=mesh['segment'=2,'blk'=16] {'blk'}, dimensions={0} | all-to-all | bytes 1048576 | tf_op jit(solution)/shard_map/all_to_all | solution.py:253
  185.2 18.7 %all_to_all.118.refs_0_ = bf16[16,64,256]{2,1,0:T(8,128)(2,1)} all-to-all(bf16[16,64,256]{2,1,0:T(8,128)(2,1)} %get-tuple-element.69), channel_id=1, replica_groups=mesh['segment'=2,'blk'=16] {'blk'}, dimensions={0} | all-to-all | bytes 1048576 | tf_op jit(solution)/shard_map/all_to_all | solution.py:253
  207.2 18.7 %all_to_all.119.refs_0_ = bf16[16,64,256]{2,1,0:T(8,128)(2,1)} all-to-all(bf16[16,64,256]{2,1,0:T(8,128)(2,1)} %get-tuple-element.71), channel_id=1, replica_groups=mesh['segment'=2,'blk'=16] {'blk'}, dimensions={0} | all-to-all | bytes 1048576 | tf_op jit(solution)/shard_map/all_to_all | solution.py:253
  229.2 18.7 %all_to_all.120.refs_0_ = bf16[16,64,256]{2,1,0:T(8,128)(2,1)} all-to-all(bf16[16,64,256]{2,1,0:T(8,128)(2,1)} %get-tuple-element.72), channel_id=1, replica_groups=mesh['segment'=2,'blk'=16] {'blk'}, dimensions={0} | all-to-all | bytes 1048576 | tf_op jit(solution)/shard_map/all_to_all | solution.py:253
  259.3 10.9 %all-to-all-done.11.refs_0_ = bf16[16,64,256]{2,1,0:T(8,128)(2,1)S(1)} async-done(((bf16[16,64,256]{2,1,0:T(8,128)(2,1)}), bf16[16,64,256]{2,1,0:T(8,128)(2,1)S(1)}, u32[]{:S(2)}, u32[]{:S(2)}) %all-to-all-start.11) | async-done | bytes 524320 | tf_op jit(solution)/shard_map/all_to_all | solution.py:253
  277.6 12.0 %all-to-all-done.refs_0_ = bf16[16,64,256]{2,1,0:T(8,128)(2,1)S(1)} async-done(((bf16[16,64,256]{2,1,0:T(8,128)(2,1)}), bf16[16,64,256]{2,1,0:T(8,128)(2,1)S(1)}, u32[]{:S(2)}, u32[]{:S(2)}) %all-to-all-start) | async-done | bytes 524320 | tf_op jit(solution)/shard_map/all_to_all | solution.py:253
  293.9 18.7 %all_to_all.121.refs_0_ = bf16[16,64,256]{2,1,0:T(8,128)(2,1)} all-to-all(bf16[16,64,256]{2,1,0:T(8,128)(2,1)} %get-tuple-element.74), channel_id=1, replica_groups=mesh['segment'=2,'blk'=16] {'blk'}, dimensions={0} | all-to-all | bytes 1048576 | tf_op jit(solution)/shard_map/all_to_all | solution.py:253
  322.4 6.9 %collective-permute-done.5.refs_4_ = bf16[8,128,128]{2,1,0:T(8,128)(2,1)S(1)} collective-permute-done((bf16[8,128,128]{2,1,0:T(8,128)(2,1)S(1)}, bf16[8,128,128]{2,1,0:T(8,128)(2,1)S(1)}, u32[]{:S(2)}, u32[]{:S(2)}) %collective-permute-start.5) | collective-permute-done | bytes 262176 | tf_op jit(solution)/shard_map/ppermute | solution.py:290
  345.4 6.9 %collective-permute-done.6.refs_5_ = bf16[8,128,128]{2,1,0:T(8,128)(2,1)S(1)} collective-permute-done((bf16[8,128,128]{2,1,0:T(8,128)(2,1)S(1)}, bf16[8,128,128]{2,1,0:T(8,128)(2,1)S(1)}, u32[]{:S(2)}, u32[]{:S(2)}) %collective-permute-start.6) | collective-permute-done | bytes 262176 | tf_op jit(solution)/shard_map/ppermute | solution.py:290
  368.6 6.9 %collective-permute-done.7.refs_4_ = bf16[8,128,128]{2,1,0:T(8,128)(2,1)S(1)} collective-permute-done((bf16[8,128,128]{2,1,0:T(8,128)(2,1)S(1)}, bf16[8,128,128]{2,1,0:T(8,128)(2,1)S(1)}, u32[]{:S(2)}, u32[]{:S(2)}) %collective-permute-start.7) | collective-permute-done | bytes 262176 | tf_op jit(solution)/shard_map/ppermute | solution.py:290
  391.6 6.9 %collective-permute-done.8.refs_5_ = bf16[8,128,128]{2,1,0:T(8,128)(2,1)S(1)} collective-permute-done((bf16[8,128,128]{2,1,0:T(8,128)(2,1)S(1)}, bf16[8,128,128]{2,1,0:T(8,128)(2,1)S(1)}, u32[]{:S(2)}, u32[]{:S(2)}) %collective-permute-start.8) | collective-permute-done | bytes 262176 | tf_op jit(solution)/shard_map/ppermute | solution.py:290
  414.9 6.9 %collective-permute-done.9.refs_4_ = bf16[8,128,128]{2,1,0:T(8,128)(2,1)S(1)} collective-permute-done((bf16[8,128,128]{2,1,0:T(8,128)(2,1)S(1)}, bf16[8,128,128]{2,1,0:T(8,128)(2,1)S(1)}, u32[]{:S(2)}, u32[]{:S(2)}) %collective-permute-start.9) | collective-permute-done | bytes 262176 | tf_op jit(solution)/shard_map/ppermute | solution.py:290
  437.8 6.9 %collective-permute-done.10.refs_5_ = bf16[8,128,128]{2,1,0:T(8,128)(2,1)S(1)} collective-permute-done((bf16[8,128,128]{2,1,0:T(8,128)(2,1)S(1)}, bf16[8,128,128]{2,1,0:T(8,128)(2,1)S(1)}, u32[]{:S(2)}, u32[]{:S(2)}) %collective-permute-start.10) | collective-permute-done | bytes 262176 | tf_op jit(solution)/shard_map/ppermute | solution.py:290
  461.0 6.9 %collective-permute-done.11.refs_4_ = bf16[8,128,128]{2,1,0:T(8,128)(2,1)S(1)} collective-permute-done((bf16[8,128,128]{2,1,0:T(8,128)(2,1)S(1)}, bf16[8,128,128]{2,1,0:T(8,128)(2,1)S(1)}, u32[]{:S(2)}, u32[]{:S(2)}) %collective-permute-start.11) | collective-permute-done | bytes 262176 | tf_op jit(solution)/shard_map/ppermute | solution.py:290
  484.0 6.9 %collective-permute-done.12.refs_5_ = bf16[8,128,128]{2,1,0:T(8,128)(2,1)S(1)} collective-permute-done((bf16[8,128,128]{2,1,0:T(8,128)(2,1)S(1)}, bf16[8,128,128]{2,1,0:T(8,128)(2,1)S(1)}, u32[]{:S(2)}, u32[]{:S(2)}) %collective-permute-start.12) | collective-permute-done | bytes 262176 | tf_op jit(solution)/shard_map/ppermute | solution.py:290
  506.7 9.2 %collective-permute-done.13.refs_4_ = bf16[8,128,128]{2,1,0:T(8,128)(2,1)S(1)} collective-permute-done((bf16[8,128,128]{2,1,0:T(8,128)(2,1)S(1)}, bf16[8,128,128]{2,1,0:T(8,128)(2,1)S(1)}, u32[]{:S(2)}, u32[]{:S(2)}) %collective-permute-start.13) | collective-permute-done | bytes 262176 | tf_op jit(solution)/shard_map/ppermute | solution.py:290
  534.2 6.2 %collective-permute-done.14.refs_2_ = bf16[8,128,128]{2,1,0:T(8,128)(2,1)S(1)} collective-permute-done((bf16[8,128,128]{2,1,0:T(8,128)(2,1)}, bf16[8,128,128]{2,1,0:T(8,128)(2,1)S(1)}, u32[]{:S(2)}, u32[]{:S(2)}) %collective-permute-start.14) | collective-permute-done | bytes 262176 | tf_op jit(solution)/shard_map/ppermute | solution.py:290
  550.5 6.6 %collective-permute-done.15 = bf16[8,128,128]{2,1,0:T(8,128)(2,1)S(1)} collective-permute-done((bf16[8,128,128]{2,1,0:T(8,128)(2,1)}, bf16[8,128,128]{2,1,0:T(8,128)(2,1)S(1)}, u32[]{:S(2)}, u32[]{:S(2)}) %collective-permute-start.15) | collective-permute-done | bytes 262176 | tf_op jit(solution)/shard_map/ppermute | solution.py:306
  (218 shorter events, 272.2 us)
Async XLA Ops:
  1.7 10.4 %collective-permute-start = (bf16[8,128,128]{2,1,0:T(8,128)(2,1)S(1)}, bf16[8,128,128]{2,1,0:T(8,128)(2,1)S(1)}, u32[]{:S(2)}, u32[]{:S(2)}) collective-permute-start(bf16[8,128,128]{2,1,0:T(8,128)(2,1)S(1)} %slice_bitcast_fusion), channel_id=1, source_target_pairs={{0,16},{1,17},{2,18},{3,19},{4,20},{5,21},{6,22},{7,23},{8,24},{9,... | collective-permute-start | bytes 786440 | tf_op jit(solution)/shard_map/ppermute | solution.py:257
  15.9 21.1 %all-to-all-start.1 = ((bf16[16,64,256]{2,1,0:T(8,128)(2,1)}), bf16[16,64,256]{2,1,0:T(8,128)(2,1)S(1)}, u32[]{:S(2)}, u32[]{:S(2)}) async-start(bf16[16,64,256]{2,1,0:T(8,128)(2,1)} %start_work.1), calls=%async_computation.1 | async-start | bytes 1048576 | tf_op jit(solution)/shard_map/all_to_all | solution.py:253
  22.0 15.0 %collective-permute-start.1 = (bf16[2,8,128,128]{3,2,1,0:T(8,128)(2,1)S(1)}, bf16[2,8,128,128]{3,2,1,0:T(8,128)(2,1)S(1)}, u32[]{:S(2)}, u32[]{:S(2)}) collective-permute-start(bf16[2,8,128,128]{3,2,1,0:T(8,128)(2,1)S(1)} %copy-done.1), channel_id=1, source_target_pairs={{0,16},{16,0},{1,17},{17,1},{2,18},{18,2},{3,19},{19,3},{4,20},{20... | collective-permute-start | bytes 1572872 | tf_op jit(solution)/shard_map/ppermute | solution.py:259
  41.9 20.4 %all-to-all-start.2 = ((bf16[16,64,256]{2,1,0:T(8,128)(2,1)}), bf16[16,64,256]{2,1,0:T(8,128)(2,1)S(1)}, u32[]{:S(2)}, u32[]{:S(2)}) async-start(bf16[16,64,256]{2,1,0:T(8,128)(2,1)} %get-tuple-element.63), calls=%async_computation.2 | async-start | bytes 1048576 | tf_op jit(solution)/shard_map/all_to_all | solution.py:253
  47.8 14.3 %collective-permute-start.2 = (bf16[2,8,128,128]{3,2,1,0:T(8,128)(2,1)S(1)}, bf16[2,8,128,128]{3,2,1,0:T(8,128)(2,1)S(1)}, u32[]{:S(2)}, u32[]{:S(2)}) collective-permute-start(bf16[2,8,128,128]{3,2,1,0:T(8,128)(2,1)S(1)} %copy-done.3), channel_id=1, source_target_pairs={{0,16},{16,0},{1,17},{17,1},{2,18},{18,2},{3,19},{19,3},{4,20},{20... | collective-permute-start | bytes 1572872 | tf_op jit(solution)/shard_map/ppermute | solution.py:259
  67.3 20.3 %all-to-all-start.3 = ((bf16[16,64,256]{2,1,0:T(8,128)(2,1)}), bf16[16,64,256]{2,1,0:T(8,128)(2,1)S(1)}, u32[]{:S(2)}, u32[]{:S(2)}) async-start(bf16[16,64,256]{2,1,0:T(8,128)(2,1)} %get-tuple-element.64), calls=%async_computation.3 | async-start | bytes 1048576 | tf_op jit(solution)/shard_map/all_to_all | solution.py:253
  73.2 14.3 %collective-permute-start.3 = (bf16[2,8,128,128]{3,2,1,0:T(8,128)(2,1)S(1)}, bf16[2,8,128,128]{3,2,1,0:T(8,128)(2,1)S(1)}, u32[]{:S(2)}, u32[]{:S(2)}) collective-permute-start(bf16[2,8,128,128]{3,2,1,0:T(8,128)(2,1)S(1)} %copy-done.5), channel_id=1, source_target_pairs={{0,16},{16,0},{1,17},{17,1},{2,18},{18,2},{3,19},{19,3},{4,20},{20... | collective-permute-start | bytes 1572872 | tf_op jit(solution)/shard_map/ppermute | solution.py:259
  92.4 20.2 %all-to-all-start.4 = ((bf16[16,64,256]{2,1,0:T(8,128)(2,1)}), bf16[16,64,256]{2,1,0:T(8,128)(2,1)S(1)}, u32[]{:S(2)}, u32[]{:S(2)}) async-start(bf16[16,64,256]{2,1,0:T(8,128)(2,1)} %get-tuple-element.65), calls=%async_computation.4 | async-start | bytes 1048576 | tf_op jit(solution)/shard_map/all_to_all | solution.py:253
  98.1 14.2 %collective-permute-start.4 = (bf16[2,8,128,128]{3,2,1,0:T(8,128)(2,1)S(1)}, bf16[2,8,128,128]{3,2,1,0:T(8,128)(2,1)S(1)}, u32[]{:S(2)}, u32[]{:S(2)}) collective-permute-start(bf16[2,8,128,128]{3,2,1,0:T(8,128)(2,1)S(1)} %copy-done.7), channel_id=1, source_target_pairs={{0,16},{16,0},{1,17},{17,1},{2,18},{18,2},{3,19},{19,3},{4,20},{20... | collective-permute-start | bytes 1572872 | tf_op jit(solution)/shard_map/ppermute | solution.py:259
  251.7 18.5 %all-to-all-start.11 = ((bf16[16,64,256]{2,1,0:T(8,128)(2,1)}), bf16[16,64,256]{2,1,0:T(8,128)(2,1)S(1)}, u32[]{:S(2)}, u32[]{:S(2)}) async-start(bf16[16,64,256]{2,1,0:T(8,128)(2,1)} %get-tuple-element.73), calls=%async_computation.11 | async-start | bytes 1048576 | tf_op jit(solution)/shard_map/all_to_all | solution.py:253
  271.0 18.6 %all-to-all-start = ((bf16[16,64,256]{2,1,0:T(8,128)(2,1)}), bf16[16,64,256]{2,1,0:T(8,128)(2,1)S(1)}, u32[]{:S(2)}, u32[]{:S(2)}) async-start(bf16[16,64,256]{2,1,0:T(8,128)(2,1)} %pack_work.1), calls=%async_computation | async-start | bytes 1048576 | tf_op jit(solution)/shard_map/all_to_all | solution.py:253
  316.4 18.7 %all-to-all-start.13 = ((bf16[16,64,256]{2,1,0:T(8,128)(2,1)}), bf16[16,64,256]{2,1,0:T(8,128)(2,1)S(1)}, u32[]{:S(2)}, u32[]{:S(2)}) async-start(bf16[16,64,256]{2,1,0:T(8,128)(2,1)} %get-tuple-element.77), calls=%async_computation.13 | async-start | bytes 1048576 | tf_op jit(solution)/shard_map/all_to_all | solution.py:253
  339.3 18.7 %all-to-all-start.14 = ((bf16[16,64,256]{2,1,0:T(8,128)(2,1)}), bf16[16,64,256]{2,1,0:T(8,128)(2,1)S(1)}, u32[]{:S(2)}, u32[]{:S(2)}) async-start(bf16[16,64,256]{2,1,0:T(8,128)(2,1)} %get-tuple-element.80), calls=%async_computation.14 | async-start | bytes 1048576 | tf_op jit(solution)/shard_map/all_to_all | solution.py:253
  362.6 18.7 %all-to-all-start.15 = ((bf16[16,64,256]{2,1,0:T(8,128)(2,1)}), bf16[16,64,256]{2,1,0:T(8,128)(2,1)S(1)}, u32[]{:S(2)}, u32[]{:S(2)}) async-start(bf16[16,64,256]{2,1,0:T(8,128)(2,1)} %get-tuple-element.83), calls=%async_computation.15 | async-start | bytes 1048576 | tf_op jit(solution)/shard_map/all_to_all | solution.py:253
  385.5 18.7 %all-to-all-start.16 = ((bf16[16,64,256]{2,1,0:T(8,128)(2,1)}), bf16[16,64,256]{2,1,0:T(8,128)(2,1)S(1)}, u32[]{:S(2)}, u32[]{:S(2)}) async-start(bf16[16,64,256]{2,1,0:T(8,128)(2,1)} %get-tuple-element.86), calls=%async_computation.16 | async-start | bytes 1048576 | tf_op jit(solution)/shard_map/all_to_all | solution.py:253
  408.8 18.7 %all-to-all-start.17 = ((bf16[16,64,256]{2,1,0:T(8,128)(2,1)}), bf16[16,64,256]{2,1,0:T(8,128)(2,1)S(1)}, u32[]{:S(2)}, u32[]{:S(2)}) async-start(bf16[16,64,256]{2,1,0:T(8,128)(2,1)} %get-tuple-element.90), calls=%async_computation.17 | async-start | bytes 1048576 | tf_op jit(solution)/shard_map/all_to_all | solution.py:253
  431.8 18.7 %all-to-all-start.18 = ((bf16[16,64,256]{2,1,0:T(8,128)(2,1)}), bf16[16,64,256]{2,1,0:T(8,128)(2,1)S(1)}, u32[]{:S(2)}, u32[]{:S(2)}) async-start(bf16[16,64,256]{2,1,0:T(8,128)(2,1)} %get-tuple-element.93), calls=%async_computation.18 | async-start | bytes 1048576 | tf_op jit(solution)/shard_map/all_to_all | solution.py:253
  454.9 18.7 %all-to-all-start.19 = ((bf16[16,64,256]{2,1,0:T(8,128)(2,1)}), bf16[16,64,256]{2,1,0:T(8,128)(2,1)S(1)}, u32[]{:S(2)}, u32[]{:S(2)}) async-start(bf16[16,64,256]{2,1,0:T(8,128)(2,1)} %get-tuple-element.96), calls=%async_computation.19 | async-start | bytes 1048576 | tf_op jit(solution)/shard_map/all_to_all | solution.py:253
  477.9 18.7 %all-to-all-start.20 = ((bf16[16,64,256]{2,1,0:T(8,128)(2,1)}), bf16[16,64,256]{2,1,0:T(8,128)(2,1)S(1)}, u32[]{:S(2)}, u32[]{:S(2)}) async-start(bf16[16,64,256]{2,1,0:T(8,128)(2,1)} %get-tuple-element.99), calls=%async_computation.20 | async-start | bytes 1048576 | tf_op jit(solution)/shard_map/all_to_all | solution.py:253
  501.2 18.7 %all-to-all-start.21 = ((bf16[16,64,256]{2,1,0:T(8,128)(2,1)}), bf16[16,64,256]{2,1,0:T(8,128)(2,1)S(1)}, u32[]{:S(2)}, u32[]{:S(2)}) async-start(bf16[16,64,256]{2,1,0:T(8,128)(2,1)} %get-tuple-element.103), calls=%async_computation.21 | async-start | bytes 1048576 | tf_op jit(solution)/shard_map/all_to_all | solution.py:253
  505.4 10.5 %collective-permute-start.13 = (bf16[8,128,128]{2,1,0:T(8,128)(2,1)S(1)}, bf16[8,128,128]{2,1,0:T(8,128)(2,1)S(1)}, u32[]{:S(2)}, u32[]{:S(2)}) collective-permute-start(bf16[8,128,128]{2,1,0:T(8,128)(2,1)S(1)} %copy-done.58), channel_id=1, source_target_pairs={{16,0},{17,1},{18,2},{19,3},{20,4},{21,5},{22,6},{23,7},{24,8},{25... | collective-permute-start | bytes 786440 | tf_op jit(solution)/shard_map/ppermute | solution.py:290
  524.4 18.7 %all-to-all-start.22 = ((bf16[16,64,256]{2,1,0:T(8,128)(2,1)}), bf16[16,64,256]{2,1,0:T(8,128)(2,1)S(1)}, u32[]{:S(2)}, u32[]{:S(2)}) async-start(bf16[16,64,256]{2,1,0:T(8,128)(2,1)} %get-tuple-element.106), calls=%async_computation.22 | async-start | bytes 1048576 | tf_op jit(solution)/shard_map/all_to_all | solution.py:253
  529.2 11.2 %collective-permute-start.14 = (bf16[8,128,128]{2,1,0:T(8,128)(2,1)}, bf16[8,128,128]{2,1,0:T(8,128)(2,1)S(1)}, u32[]{:S(2)}, u32[]{:S(2)}) collective-permute-start(bf16[8,128,128]{2,1,0:T(8,128)(2,1)} %get-tuple-element.107), channel_id=1, source_target_pairs={{16,0},{17,1},{18,2},{19,3},{20,4},{21,5},{22,6},{23,7},{24,8},{25... | collective-permute-start | bytes 786440 | tf_op jit(solution)/shard_map/ppermute | solution.py:290
  532.9 15.2 %collective-permute-start.16 = (bf16[8,128,128]{2,1,0:T(8,128)(2,1)}, bf16[8,128,128]{2,1,0:T(8,128)(2,1)S(1)}, u32[]{:S(2)}, u32[]{:S(2)}) collective-permute-start(bf16[8,128,128]{2,1,0:T(8,128)(2,1)} %get-tuple-element.113), channel_id=1, source_target_pairs={{16,0},{17,1},{18,2},{19,3},{20,4},{21,5},{22,6},{23,7},{24,8},{25... | collective-permute-start | bytes 786440 | tf_op jit(solution)/shard_map/ppermute | solution.py:290
  (74 other events, 367.4 us)

commit v4 on v3

--- a/solution.py
+++ b/solution.py
@@ -85,39 +85,38 @@
     scatter(matmul(weight, total, 0, 0))
 
 
-def left_work(plan, at, scatter, weight, gradient, values, kept):
-    natural = read(plan, values, at).astype(BF16)
-    kept[at] = natural
-    scatter(matmul(weight, natural, 0, 0))
-
-
-def gelu_work(plan, at, scatter, weight, gradient, values, upper, hidden):
-    natural = read(plan, values, at)
-    upper[at] = natural.astype(BF16)
-    active = gelu(natural).astype(BF16)
-    hidden[at] = active
-    scatter(matmul(weight, active, 0, 0))
+def left_work(plan, at, scatter, weight, gradient, values):
+    scatter(matmul(weight, read(plan, values, at).astype(BF16), 0, 0))
+
+
+def gelu_work(plan, at, scatter, weight, gradient, values):
+    scatter(matmul(weight, gelu(read(plan, values, at)).astype(BF16), 0, 0))
 
 
 def pack_work(plan, at, scatter, weight, gradient, values):
     scatter(values[at].astype(F32))
 
 
-def unpack_work(plan, at, scatter, weight, gradient, values, out):
-    out[at] = read(plan, values, at).astype(BF16)
-
-
-def back_left_work(plan, at, scatter, weight, gradient, grad, kept):
+def last_back_left_work(plan, at, scatter, weight, gradient, grad):
+    scatter(matmul(weight, read(plan, grad, at).astype(BF16), 1, 0))
+
+
+def last_outer_work(plan, at, scatter, weight, gradient, grad, values):
+    natural = read(plan, grad, at).astype(BF16)
+    gradient(matmul(read(plan, values, at).astype(BF16), natural, 1, 1))
+
+
+def back_left_work(plan, at, scatter, weight, gradient, grad, values):
     natural = read(plan, grad, at).astype(BF16)
     scatter(matmul(weight, natural, 1, 0))
-    gradient(matmul(kept[at], natural, 1, 1))
-
-
-def back_gelu_work(plan, at, scatter, weight, gradient, grad, hidden, upper):
+    gradient(matmul(read(plan, values, at).astype(BF16), natural, 1, 1))
+
+
+def back_gelu_work(plan, at, scatter, weight, gradient, grad, values):
     natural = read(plan, grad, at).astype(BF16)
-    grad_hidden = matmul(weight, natural, 1, 0)
-    scatter(grad_hidden * gelu_slope(upper[at].astype(F32)))
-    gradient(matmul(hidden[at], natural, 1, 1))
+    upper = read(plan, values, at)
+    scatter(matmul(weight, natural, 1, 0) * gelu_slope(upper))
+    gradient(matmul(gelu(upper).astype(BF16), natural, 1, 1))
 
 
 def back_right_work(plan, at, scatter, weight, gradient, grad, state, above, result):
@@ -142,62 +141,73 @@
         self.sent = (plan.devices, plan.own * plan.own, tokens)
         self.square = (plan.own, plan.size, plan.size)
 
-    def run(self, work, ins, packed=0, weight=None, send=True, naturals=0, grads=False, after=()):
+    def run(
+        self, work, ins, packed=0, weight=None, send=True, naturals=0, grads=False, after=(), join=None
+    ):
         plan, tokens, picks = self.plan, self.tokens, self.picks
-        turn_blocks = plan.own // 2
-        natural = pl.BlockSpec((turn_blocks,) + self.natural[1:], lambda turn, picks: (turn, 0, 0))
-        arrived = pl.BlockSpec(
-            (plan.devices, turn_blocks * plan.own, tokens), lambda turn, picks: (0, turn, 0)
-        )
-        square = (turn_blocks,) + self.square[1:]
-        in_specs = [arrived] * packed + [natural] * (len(ins) - packed)
-        operands = list(ins)
+        rows = plan.own * plan.own
+
+        def whole(shape):
+            return pl.BlockSpec(shape, lambda turn, picks: (0,) * len(shape))
+
+        def one_part(part):
+            return pl.BlockSpec((plan.devices, rows, tokens), lambda turn, picks: (0, part, 0))
+
+        natural, square = whole(self.natural), whole(self.square)
+        operands, in_specs = [], []
+        for at, value in enumerate(ins):
+            value, part = value if isinstance(value, tuple) else (value, 0)
+            operands.append(value)
+            in_specs.append(one_part(part) if at < packed else natural)
         layer, mine, theirs = weight or (0, None, None)
         matrices = [m for m in (mine, theirs) if m is not None]
         for matrix in matrices:
             operands.append(matrix)
             if len(matrix.shape) == 4:
-                spec = pl.BlockSpec(
-                    (None,) + square, lambda turn, picks: (picks[2 * layer], turn, 0, 0)
-                )
+                block = (None,) + self.square
+                in_specs.append(pl.BlockSpec(block, lambda turn, picks: (picks[2 * layer], 0, 0, 0)))
             else:
-                spec = pl.BlockSpec(square, lambda turn, picks: (turn, 0, 0))
-            in_specs.append(spec)
-        operands += after
-        in_specs += [pl.BlockSpec(memory_space=pl.ANY)] * len(after)
+                in_specs.append(square)
+        unread = list(after) + ([] if join is None else [join])
+        operands += unread
+        in_specs += [pl.BlockSpec(memory_space=pl.ANY)] * len(unread)
+        aliases = {} if join is None else {len(operands): 0}
         outs, out_specs, scratch = [], [], []
-        if send:
+        if send is True:
             outs.append(jax.ShapeDtypeStruct(self.sent, BF16))
-            out_specs.append(pl.BlockSpec(self.sent, lambda turn, picks: (0, 0, 0)))
+            out_specs.append(one_part(0))
+        elif send is not None:
+            outs.append(jax.ShapeDtypeStruct((plan.devices, 2 * rows, tokens), BF16))
+            out_specs.append(one_part(send))
+        if send is not None:
             scratch.append(pltpu.VMEM((tokens // 128, plan.size * plan.own, 128), F32))
         outs += [jax.ShapeDtypeStruct(self.natural, BF16)] * naturals
         out_specs += [natural] * naturals
         if grads:
-            outs += [jax.ShapeDtypeStruct(self.square, dtype) for dtype in (F32, BF16)]
-            out_specs += [pl.BlockSpec(square, lambda turn, picks: (turn, 0, 0))] * 2
+            outs.append(jax.ShapeDtypeStruct(self.square, BF16))
+            out_specs.append(square)
 
         def kernel(picks, *refs):
             refs = list(refs)
-            turn = pl.program_id(0)
             inner = [refs.pop(0) for i in ins]
             factors = [refs.pop(0) for i in matrices]
-            del refs[: len(after)]
-            out = refs.pop(0) if send else None
+            del refs[: len(unread)]
+            out = refs.pop(0) if send is not None else None
             inner += [refs.pop(0) for i in range(naturals)]
-            gradients = [refs.pop(0) for i in range(2 if grads else 0)]
-            store = refs[0] if send else None
+            gradients = [refs.pop(0)] if grads else []
+            store = refs[0] if send is not None else None
 
             def scatter(at, values):
-                rows = pl.ds(turn * turn_blocks + at, plan.size, stride=plan.own)
+                spread = pl.ds(at, plan.size, stride=plan.own)
                 for part in range(tokens // 128):
-                    store[part, rows, :] = values[:, part * 128 : (part + 1) * 128]
+                    store[part, spread, :] = values[:, part * 128 : (part + 1) * 128]
 
             def gradient(at, values):
                 for ref in gradients:
                     ref[at] = values.astype(ref.dtype)
 
             here = picks[2 * layer + 1] == 1
-            for at in range(turn_blocks):
+            for at in range(plan.own):
                 matrix = None
                 if len(factors) == 2:
                     matrix = jnp.where(here, factors[0][at], factors[1][at])
@@ -205,17 +215,12 @@
                     matrix = factors[0][at]
                 put = functools.partial(scatter, at)
                 work(plan, at, put, matrix, functools.partial(gradient, at), *inner)
-            if send:
-
-                @pl.when(turn == 1)
-                def _():
-                    for part in range(tokens // 128):
-                        rows = store[part].astype(BF16)
-                        rows = rows.reshape(plan.devices, plan.own * plan.own, 128)
-                        out[:, :, part * 128 : (part + 1) * 128] = rows
-
-        volume = sum(math.prod(i.shape) * i.dtype.itemsize for i in ins)
-        volume += sum(math.prod(o.shape) * o.dtype.itemsize for o in outs)
+            if send is not None:
+                for part in range(tokens // 128):
+                    values = store[part].astype(BF16).reshape(plan.devices, rows, 128)
+                    out[:, :, part * 128 : (part + 1) * 128] = values
+
+        volume = sum(math.prod(o.shape) * o.dtype.itemsize for o in operands + outs)
         products = (1 if matrices else 0) + (1 if grads else 0)
         flops = products * 2 * plan.own * plan.size * plan.size * tokens
         return pl.pallas_call(
@@ -223,11 +228,12 @@
             out_shape=outs,
             grid_spec=pltpu.PrefetchScalarGridSpec(
                 num_scalar_prefetch=1,
-                grid=(2,),
+                grid=(1,),
                 in_specs=in_specs,
                 out_specs=out_specs,
                 scratch_shapes=scratch,
             ),
+            input_output_aliases=aliases,
             compiler_params=pltpu.CompilerParams(
                 vmem_limit_bytes=60 * 1024 * 1024, dimension_semantics=("arbitrary",)
             ),
@@ -263,52 +269,68 @@
             return layer, early, None
         return layer, factors[at], received[at]
 
-    saved = []
-    state, branch = micro, None
-    for layer in range(count):
-        if layer == 0:
-            sent = run(start_work, (state,), 0, weight(0, 0))[0]
-        else:
-            sent, state = run(residual_work, (branch, state), 1, weight(layer, 0), naturals=1)
-        sent, inner = run(left_work, (exchange(sent),), 1, weight(layer, 1), naturals=1)
-        sent, upper, hidden = run(gelu_work, (exchange(sent),), 1, weight(layer, 2), naturals=2)
-        values = exchange(sent)
-        if layer < count - 1:
-            sent, inner_two = run(left_work, (values,), 1, weight(layer, 3), naturals=1)
-            branch = exchange(sent)
-        else:
-            inner_two = run(unpack_work, (values,), 1, send=False, naturals=1)[0]
-        saved.append((state, inner, upper, hidden, inner_two))
-
     waiting = [(), ()]
     parts = [[None] * 4 for layer in range(count)]
 
-    def step(layer, at, work, ins, naturals=0):
-        after = waiting.pop(0)
-        use = weight(layer, at)
-        *results, stay, leave = run(work, ins, 1, use, True, naturals, True, after)
+    def step(layer, at, work, ins, packed=2, naturals=0, plain=False, **options):
+        use = None if plain else weight(layer, at)
+        after = waiting.pop(0) if waiting and not plain else ()
+        results = run(work, ins, packed, use, naturals=naturals, grads=True, after=after, **options)
+        *results, leave = results
         other = lax.ppermute(leave, "segment", [(1, 0)] if layer == 0 else both)
-        waiting.append((other,))
-        parts[layer][at] = (stay, other)
-        return results if naturals else results[0]
-
-    sent = run(pack_work, (grad,))[0]
-    for layer in reversed(range(count)):
-        state, inner, upper, hidden, inner_two = saved[layer]
-        sent = step(layer, 3, back_left_work, (exchange(sent), inner_two))
-        sent = step(layer, 2, back_gelu_work, (exchange(sent), hidden, upper))
-        sent = step(layer, 1, back_left_work, (exchange(sent), inner))
+        if not plain:
+            waiting.append((other,))
+        parts[layer][at] = (leave, other)
+        return results
+
+    saved = []
+    state = micro
+    sent = run(start_work, (state,), 0, weight(0, 0))[0]
+    inner = exchange(sent)
+    upper = exchange(run(left_work, (inner,), 1, weight(0, 1))[0])
+    inner_two = exchange(run(gelu_work, (upper,), 1, weight(0, 2))[0])
+    branch = exchange(run(left_work, (inner_two,), 1, weight(0, 3))[0])
+    saved.append((state, inner, upper, inner_two))
+
+    beside = run(pack_work, (grad,), send=1)[0]
+    ins = (branch, state)
+    sent, state = run(residual_work, ins, 1, weight(1, 0), send=0, naturals=1, join=beside)
+    values = exchange(sent)
+    inner, last_grad_c = (values, 0), (values, 1)
+    upper = exchange(run(left_work, (inner,), 1, weight(1, 1))[0])
+    beside = run(last_back_left_work, (last_grad_c,), 1, weight(2, 3), send=1)[0]
+    values = exchange(run(gelu_work, (upper,), 1, weight(1, 2), send=0, join=beside)[0])
+    inner_two, last_grad_a = (values, 0), (values, 1)
+    branch = exchange(run(left_work, (inner_two,), 1, weight(1, 3))[0])
+    saved.append((state, inner, upper, inner_two))
+
+    sent, state = run(residual_work, (branch, state), 1, weight(2, 0), naturals=1)
+    inner = exchange(sent)
+    upper = exchange(run(left_work, (inner,), 1, weight(2, 1))[0])
+
+    sent = step(2, 2, back_gelu_work, (last_grad_a, upper))[0]
+    beside = run(gelu_work, (upper,), 1, weight(2, 2), send=1)[0]
+    sent = step(2, 1, back_left_work, (exchange(sent), inner), send=0, join=beside)[0]
+    values = exchange(sent)
+    grad_a, inner_two = (values, 0), (values, 1)
+    sent, grad = step(2, 0, back_right_work, (grad_a, state, grad), 1, 1)
+    step(2, 3, last_outer_work, (last_grad_c, inner_two), plain=True, send=None)
+    for layer in (1, 0):
+        state, inner, upper, inner_two = saved[layer]
+        sent = step(layer, 3, back_left_work, (exchange(sent), inner_two))[0]
+        sent = step(layer, 2, back_gelu_work, (exchange(sent), upper))[0]
+        sent = step(layer, 1, back_left_work, (exchange(sent), inner))[0]
         if layer > 0:
             ins = (exchange(sent), state, grad)
-            sent, grad = step(layer, 0, back_right_work, ins, 1)
-    ins = (exchange(sent), state)
-    stay, leave = run(end_work, ins, 1, send=False, grads=True, after=waiting.pop(0))
-    parts[0][0] = (stay, lax.ppermute(leave, "segment", [(1, 0)]))
+            sent, grad = step(layer, 0, back_right_work, ins, 1, 1)
+    step(0, 0, end_work, (exchange(sent), state), 1, plain=True, send=None)
 
     outs = []
     first_has_two = sections[0] == 2
     for at in range(4):
-        zero, one, two = [stay + other.astype(F32) for stay, other in (p[at] for p in parts)]
+        zero, one, two = [
+            stay.astype(F32) + other.astype(F32) for stay, other in (p[at] for p in parts)
+        ]
         low = jnp.where(segment == 0, zero, jnp.where(first_has_two, two, one))
         high = jnp.where(segment == 0, one, two)
         high = jnp.where(first_has_two == (segment == 0), high, 0.0)

time: 562 us -> 530 us (0.943)
  blocking collectives: 133 us -> 117 us
  waiting for transfers between devices: 202 us -> 188 us
    all_to_all x7 -> x5, blocking collectives: 133 us -> 117 us  [exchange(): return lax.all_to_all(value, 'blk', 0, 0, tiled=True)]
    ppermute x1 -> x0, waiting for transfers between devices: 6.63 us -> none  [two_segments(): parts[0][0] = (stay, lax.ppermute(leave, 'segment', [(1, 0)]))]
    ppermute x11 -> x12, waiting for transfers between devices: 70.7 us -> 65.5 us  [step(): other = lax.ppermute(leave, 'segment', [(1, 0)] if layer == 0 else both)]
    all_to_all x16 -> x15, waiting for transfers between devices: 74.2 us -> 76.4 us  [exchange(): return lax.all_to_all(value, 'blk', 0, 0, tiled=True)]
    ppermute x11 -> x12, starting transfers between devices: 18.3 us -> 20.3 us  [step(): other = lax.ppermute(leave, 'segment', [(1, 0)] if layer == 0 else both)]
    unnamed x130 -> x110, local copies, waits for them, and re-layouts: 16.7 us -> 15.6 us
    all_to_all x16 -> x15, starting transfers between devices: 73.9 us -> 73.4 us  [exchange(): return lax.all_to_all(value, 'blk', 0, 0, tiled=True)]
  transfers between devices with their start and end apart: 33 -> 32, of which waited for: 31 -> 29; matrix products, arithmetic and copies ran while one was open for 2% -> 2% of each run, Pallas kernels for 1% -> 3%
where the time goes in v4:
time: 530 us; the launch traced here: 527 us
  waiting for transfers between devices  188 us (35%)
  blocking collectives  117 us (22%)
  starting transfers between devices  107 us (20%)
  Pallas kernels  83.3 us (16%)
  local copies, waits for them, and re-layouts  20.6 us (4%)
  other arithmetic  7.95 us (2%)
    all_to_all x5, blocking collectives, exchange(): return lax.all_to_all(value, 'blk', 0, 0, tiled=True)  117 us
    pallas_call x25, Pallas kernels, run(): pl.pallas_call(kernel, out_shape=outs, grid_spec=pltpu.PrefetchScalarGrid...  83.3 us
    all_to_all x15, waiting for transfers between devices, exchange(): return lax.all_to_all(value, 'blk', 0, 0, tiled=True)  76.4 us
    all_to_all x15, starting transfers between devices, exchange(): return lax.all_to_all(value, 'blk', 0, 0, tiled=True)  73.4 us
    ppermute x12, waiting for transfers between devices, step(): other = lax.ppermute(leave, 'segment', [(1, 0)] if layer == 0 else both)  65.5 us
    ppermute x4, waiting for transfers between devices, two_segments(): received = [lax.ppermute(factor, 'segment', both) for factor in factors]  45.2 us
    ppermute x12, starting transfers between devices, step(): other = lax.ppermute(leave, 'segment', [(1, 0)] if layer == 0 else both)  20.3 us
    unnamed x110, local copies, waits for them, and re-layouts  15.6 us
  transfers between devices with their start and end apart: 32, of which 29 were waited for; matrix products, arithmetic and copies ran while one was open for 2% of the time, Pallas kernels for 3%

profile of v4, /device:TPU:0, one launch (start us, length us, event | category | flops | bytes accessed | tf_op | source)
XLA Modules:
  0.0 526.9 jit_solution(15856672769237916279)
XLA Ops:
  15.8 6.0 %all-to-all-start = ((bf16[16,64,256]{2,1,0:T(8,128)(2,1)}), bf16[16,64,256]{2,1,0:T(8,128)(2,1)S(1)}, u32[]{:S(2)}, u32[]{:S(2)}) async-start(bf16[16,64,256]{2,1,0:T(8,128)(2,1)} %start_work.1), calls=%async_computation | async-start | bytes 1048576 | tf_op jit(solution)/shard_map/all_to_all | solution.py:259
  24.5 12.5 %collective-permute-done.1.refs_2_.refs_3_ = bf16[2,8,128,128]{3,2,1,0:T(8,128)(2,1)S(1)} collective-permute-done((bf16[2,8,128,128]{3,2,1,0:T(8,128)(2,1)S(1)}, bf16[2,8,128,128]{3,2,1,0:T(8,128)(2,1)S(1)}, u32[]{:S(2)}, u32[]{:S(2)}) %collective-permute-start.1) | collective-permute-done | bytes 524320 | tf_op jit(solution)/shard_map/ppermute | solution.py:265
  41.6 5.9 %all-to-all-start.1 = ((bf16[16,64,256]{2,1,0:T(8,128)(2,1)}), bf16[16,64,256]{2,1,0:T(8,128)(2,1)S(1)}, u32[]{:S(2)}, u32[]{:S(2)}) async-start(bf16[16,64,256]{2,1,0:T(8,128)(2,1)} %left_work.5), calls=%async_computation.1 | async-start | bytes 1048576 | tf_op jit(solution)/shard_map/all_to_all | solution.py:259
  49.3 12.5 %collective-permute-done.2.refs_2_.refs_3_ = bf16[2,8,128,128]{3,2,1,0:T(8,128)(2,1)S(1)} collective-permute-done((bf16[2,8,128,128]{3,2,1,0:T(8,128)(2,1)S(1)}, bf16[2,8,128,128]{3,2,1,0:T(8,128)(2,1)S(1)}, u32[]{:S(2)}, u32[]{:S(2)}) %collective-permute-start.2) | collective-permute-done | bytes 524320 | tf_op jit(solution)/shard_map/ppermute | solution.py:265
  74.5 12.5 %collective-permute-done.3.refs_2_.refs_3_ = bf16[2,8,128,128]{3,2,1,0:T(8,128)(2,1)S(1)} collective-permute-done((bf16[2,8,128,128]{3,2,1,0:T(8,128)(2,1)S(1)}, bf16[2,8,128,128]{3,2,1,0:T(8,128)(2,1)S(1)}, u32[]{:S(2)}, u32[]{:S(2)}) %collective-permute-start.3) | collective-permute-done | bytes 524320 | tf_op jit(solution)/shard_map/ppermute | solution.py:265
  104.0 7.7 %collective-permute-done.4.refs_3_.refs_4_ = bf16[2,8,128,128]{3,2,1,0:T(8,128)(2,1)S(1)} collective-permute-done((bf16[2,8,128,128]{3,2,1,0:T(8,128)(2,1)S(1)}, bf16[2,8,128,128]{3,2,1,0:T(8,128)(2,1)S(1)}, u32[]{:S(2)}, u32[]{:S(2)}) %collective-permute-start.4) | collective-permute-done | bytes 524320 | tf_op jit(solution)/shard_map/ppermute | solution.py:265
  116.7 30.7 %all_to_all.100.refs_0_.refs_1_ = bf16[16,128,256]{2,1,0:T(8,128)(2,1)} all-to-all(bf16[16,128,256]{2,1,0:T(8,128)(2,1)} %get-tuple-element.29), channel_id=1, replica_groups=mesh['segment'=2,'blk'=16] {'blk'}, dimensions={0} | all-to-all | bytes 2097152 | tf_op jit(solution)/shard_map/all_to_all | solution.py:259
  158.6 11.4 %all-to-all-done.5.refs_0_.refs_1_ = bf16[16,64,256]{2,1,0:T(8,128)(2,1)S(1)} async-done(((bf16[16,64,256]{2,1,0:T(8,128)(2,1)}), bf16[16,64,256]{2,1,0:T(8,128)(2,1)S(1)}, u32[]{:S(2)}, u32[]{:S(2)}) %all-to-all-start.5) | async-done | bytes 524320 | tf_op jit(solution)/shard_map/all_to_all | solution.py:259
  174.1 29.1 %all_to_all.101.refs_0_.refs_1_ = bf16[16,128,256]{2,1,0:T(8,128)(2,1)} all-to-all(bf16[16,128,256]{2,1,0:T(8,128)(2,1)} %gelu_work.4), channel_id=1, replica_groups=mesh['segment'=2,'blk'=16] {'blk'}, dimensions={0} | all-to-all | bytes 2097152 | tf_op jit(solution)/shard_map/all_to_all | solution.py:259
  206.4 19.5 %all_to_all.102.refs_0_ = bf16[16,64,256]{2,1,0:T(8,128)(2,1)} all-to-all(bf16[16,64,256]{2,1,0:T(8,128)(2,1)} %left_work.8), channel_id=1, replica_groups=mesh['segment'=2,'blk'=16] {'blk'}, dimensions={0} | all-to-all | bytes 1048576 | tf_op jit(solution)/shard_map/all_to_all | solution.py:259
  229.1 18.7 %all_to_all.103.refs_0_.refs_1_ = bf16[16,64,256]{2,1,0:T(8,128)(2,1)} all-to-all(bf16[16,64,256]{2,1,0:T(8,128)(2,1)} %get-tuple-element.31), channel_id=1, replica_groups=mesh['segment'=2,'blk'=16] {'blk'}, dimensions={0} | all-to-all | bytes 1048576 | tf_op jit(solution)/shard_map/all_to_all | solution.py:259
  250.9 18.7 %all_to_all.104.refs_1_.refs_0_ = bf16[16,64,256]{2,1,0:T(8,128)(2,1)} all-to-all(bf16[16,64,256]{2,1,0:T(8,128)(2,1)} %left_work.9), channel_id=1, replica_groups=mesh['segment'=2,'blk'=16] {'blk'}, dimensions={0} | all-to-all | bytes 1048576 | tf_op jit(solution)/shard_map/all_to_all | solution.py:259
  280.9 11.1 %all-to-all-done.10.refs_0_ = bf16[16,64,256]{2,1,0:T(8,128)(2,1)S(1)} async-done(((bf16[16,64,256]{2,1,0:T(8,128)(2,1)}), bf16[16,64,256]{2,1,0:T(8,128)(2,1)S(1)}, u32[]{:S(2)}, u32[]{:S(2)}) %all-to-all-start.10) | async-done | bytes 524320 | tf_op jit(solution)/shard_map/all_to_all | solution.py:259
  302.2 6.9 %collective-permute-done.5.refs_5_ = bf16[8,128,128]{2,1,0:T(8,128)(2,1)S(1)} collective-permute-done((bf16[8,128,128]{2,1,0:T(8,128)(2,1)S(1)}, bf16[8,128,128]{2,1,0:T(8,128)(2,1)S(1)}, u32[]{:S(2)}, u32[]{:S(2)}) %collective-permute-start.5) | collective-permute-done | bytes 262176 | tf_op jit(solution)/shard_map/ppermute | solution.py:280
  309.2 14.2 %all-to-all-done.11.refs_0_.refs_1_ = bf16[16,128,256]{2,1,0:T(8,128)(2,1)S(1)} async-done(((bf16[16,128,256]{2,1,0:T(8,128)(2,1)}), bf16[16,128,256]{2,1,0:T(8,128)(2,1)S(1)}, u32[]{:S(2)}, u32[]{:S(2)}) %all-to-all-start.11) | async-done | bytes 1048608 | tf_op jit(solution)/shard_map/all_to_all | solution.py:259
  328.2 7.0 %all-to-all-start.12 = ((bf16[16,64,256]{2,1,0:T(8,128)(2,1)}), bf16[16,64,256]{2,1,0:T(8,128)(2,1)S(1)}, u32[]{:S(2)}, u32[]{:S(2)}) async-start(bf16[16,64,256]{2,1,0:T(8,128)(2,1)} %get-tuple-element.36), calls=%async_computation.12 | async-start | bytes 1048576 | tf_op jit(solution)/shard_map/all_to_all | solution.py:259
  337.0 6.9 %collective-permute-done.6.refs_4_ = bf16[8,128,128]{2,1,0:T(8,128)(2,1)S(1)} collective-permute-done((bf16[8,128,128]{2,1,0:T(8,128)(2,1)S(1)}, bf16[8,128,128]{2,1,0:T(8,128)(2,1)S(1)}, u32[]{:S(2)}, u32[]{:S(2)}) %collective-permute-start.6) | collective-permute-done | bytes 262176 | tf_op jit(solution)/shard_map/ppermute | solution.py:280
  360.0 6.9 %collective-permute-done.7.refs_4_ = bf16[8,128,128]{2,1,0:T(8,128)(2,1)S(1)} collective-permute-done((bf16[8,128,128]{2,1,0:T(8,128)(2,1)S(1)}, bf16[8,128,128]{2,1,0:T(8,128)(2,1)S(1)}, u32[]{:S(2)}, u32[]{:S(2)}) %collective-permute-start.7) | collective-permute-done | bytes 262176 | tf_op jit(solution)/shard_map/ppermute | solution.py:280
  383.4 6.9 %collective-permute-done.8.refs_4_ = bf16[8,128,128]{2,1,0:T(8,128)(2,1)S(1)} collective-permute-done((bf16[8,128,128]{2,1,0:T(8,128)(2,1)S(1)}, bf16[8,128,128]{2,1,0:T(8,128)(2,1)S(1)}, u32[]{:S(2)}, u32[]{:S(2)}) %collective-permute-start.8) | collective-permute-done | bytes 262176 | tf_op jit(solution)/shard_map/ppermute | solution.py:280
  406.3 6.9 %collective-permute-done.9.refs_5_ = bf16[8,128,128]{2,1,0:T(8,128)(2,1)S(1)} collective-permute-done((bf16[8,128,128]{2,1,0:T(8,128)(2,1)S(1)}, bf16[8,128,128]{2,1,0:T(8,128)(2,1)S(1)}, u32[]{:S(2)}, u32[]{:S(2)}) %collective-permute-start.9) | collective-permute-done | bytes 262176 | tf_op jit(solution)/shard_map/ppermute | solution.py:280
  429.6 6.9 %collective-permute-done.10.refs_4_ = bf16[8,128,128]{2,1,0:T(8,128)(2,1)S(1)} collective-permute-done((bf16[8,128,128]{2,1,0:T(8,128)(2,1)S(1)}, bf16[8,128,128]{2,1,0:T(8,128)(2,1)S(1)}, u32[]{:S(2)}, u32[]{:S(2)}) %collective-permute-start.10) | collective-permute-done | bytes 262176 | tf_op jit(solution)/shard_map/ppermute | solution.py:280
  452.5 6.9 %collective-permute-done.11.refs_4_ = bf16[8,128,128]{2,1,0:T(8,128)(2,1)S(1)} collective-permute-done((bf16[8,128,128]{2,1,0:T(8,128)(2,1)S(1)}, bf16[8,128,128]{2,1,0:T(8,128)(2,1)S(1)}, u32[]{:S(2)}, u32[]{:S(2)}) %collective-permute-start.11) | collective-permute-done | bytes 262176 | tf_op jit(solution)/shard_map/ppermute | solution.py:280
  502.9 6.1 %collective-permute-done.15 = bf16[8,128,128]{2,1,0:T(8,128)(2,1)S(1)} collective-permute-done((bf16[8,128,128]{2,1,0:T(8,128)(2,1)}, bf16[8,128,128]{2,1,0:T(8,128)(2,1)S(1)}, u32[]{:S(2)}, u32[]{:S(2)}) %collective-permute-start.15) | collective-permute-done | bytes 262176 | tf_op jit(solution)/shard_map/ppermute | solution.py:280
  518.9 6.7 %collective-permute-done.13 = bf16[8,128,128]{2,1,0:T(8,128)(2,1)S(1)} collective-permute-done((bf16[8,128,128]{2,1,0:T(8,128)(2,1)}, bf16[8,128,128]{2,1,0:T(8,128)(2,1)S(1)}, u32[]{:S(2)}, u32[]{:S(2)}) %collective-permute-start.13) | collective-permute-done | bytes 262176 | tf_op jit(solution)/shard_map/ppermute | solution.py:280
  (194 shorter events, 244.1 us)
Async XLA Ops:
  1.7 10.4 %collective-permute-start = (bf16[8,128,128]{2,1,0:T(8,128)(2,1)S(1)}, bf16[8,128,128]{2,1,0:T(8,128)(2,1)S(1)}, u32[]{:S(2)}, u32[]{:S(2)}) collective-permute-start(bf16[8,128,128]{2,1,0:T(8,128)(2,1)S(1)} %slice_bitcast_fusion), channel_id=1, source_target_pairs={{0,16},{1,17},{2,18},{3,19},{4,20},{5,21},{6,22},{7,23},{8,24},{9,... | collective-permute-start | bytes 786440 | tf_op jit(solution)/shard_map/ppermute | solution.py:263
  15.8 21.1 %all-to-all-start = ((bf16[16,64,256]{2,1,0:T(8,128)(2,1)}), bf16[16,64,256]{2,1,0:T(8,128)(2,1)S(1)}, u32[]{:S(2)}, u32[]{:S(2)}) async-start(bf16[16,64,256]{2,1,0:T(8,128)(2,1)} %start_work.1), calls=%async_computation | async-start | bytes 1048576 | tf_op jit(solution)/shard_map/all_to_all | solution.py:259
  21.9 15.0 %collective-permute-start.1 = (bf16[2,8,128,128]{3,2,1,0:T(8,128)(2,1)S(1)}, bf16[2,8,128,128]{3,2,1,0:T(8,128)(2,1)S(1)}, u32[]{:S(2)}, u32[]{:S(2)}) collective-permute-start(bf16[2,8,128,128]{3,2,1,0:T(8,128)(2,1)S(1)} %copy-done.2), channel_id=1, source_target_pairs={{0,16},{16,0},{1,17},{17,1},{2,18},{18,2},{3,19},{19,3},{4,20},{20... | collective-permute-start | bytes 1572872 | tf_op jit(solution)/shard_map/ppermute | solution.py:265
  41.6 20.4 %all-to-all-start.1 = ((bf16[16,64,256]{2,1,0:T(8,128)(2,1)}), bf16[16,64,256]{2,1,0:T(8,128)(2,1)S(1)}, u32[]{:S(2)}, u32[]{:S(2)}) async-start(bf16[16,64,256]{2,1,0:T(8,128)(2,1)} %left_work.5), calls=%async_computation.1 | async-start | bytes 1048576 | tf_op jit(solution)/shard_map/all_to_all | solution.py:259
  47.5 14.3 %collective-permute-start.2 = (bf16[2,8,128,128]{3,2,1,0:T(8,128)(2,1)S(1)}, bf16[2,8,128,128]{3,2,1,0:T(8,128)(2,1)S(1)}, u32[]{:S(2)}, u32[]{:S(2)}) collective-permute-start(bf16[2,8,128,128]{3,2,1,0:T(8,128)(2,1)S(1)} %copy-done.1), channel_id=1, source_target_pairs={{0,16},{16,0},{1,17},{17,1},{2,18},{18,2},{3,19},{19,3},{4,20},{20... | collective-permute-start | bytes 1572872 | tf_op jit(solution)/shard_map/ppermute | solution.py:265
  66.8 20.3 %all-to-all-start.2 = ((bf16[16,64,256]{2,1,0:T(8,128)(2,1)}), bf16[16,64,256]{2,1,0:T(8,128)(2,1)S(1)}, u32[]{:S(2)}, u32[]{:S(2)}) async-start(bf16[16,64,256]{2,1,0:T(8,128)(2,1)} %gelu_work.3), calls=%async_computation.2 | async-start | bytes 1048576 | tf_op jit(solution)/shard_map/all_to_all | solution.py:259
  72.7 14.3 %collective-permute-start.3 = (bf16[2,8,128,128]{3,2,1,0:T(8,128)(2,1)S(1)}, bf16[2,8,128,128]{3,2,1,0:T(8,128)(2,1)S(1)}, u32[]{:S(2)}, u32[]{:S(2)}) collective-permute-start(bf16[2,8,128,128]{3,2,1,0:T(8,128)(2,1)S(1)} %copy-done.5), channel_id=1, source_target_pairs={{0,16},{16,0},{1,17},{17,1},{2,18},{18,2},{3,19},{19,3},{4,20},{20... | collective-permute-start | bytes 1572872 | tf_op jit(solution)/shard_map/ppermute | solution.py:265
  91.7 20.2 %all-to-all-start.3 = ((bf16[16,64,256]{2,1,0:T(8,128)(2,1)}), bf16[16,64,256]{2,1,0:T(8,128)(2,1)S(1)}, u32[]{:S(2)}, u32[]{:S(2)}) async-start(bf16[16,64,256]{2,1,0:T(8,128)(2,1)} %left_work.6), calls=%async_computation.3 | async-start | bytes 1048576 | tf_op jit(solution)/shard_map/all_to_all | solution.py:259
  97.5 14.2 %collective-permute-start.4 = (bf16[2,8,128,128]{3,2,1,0:T(8,128)(2,1)S(1)}, bf16[2,8,128,128]{3,2,1,0:T(8,128)(2,1)S(1)}, u32[]{:S(2)}, u32[]{:S(2)}) collective-permute-start(bf16[2,8,128,128]{3,2,1,0:T(8,128)(2,1)S(1)} %copy-done.7), channel_id=1, source_target_pairs={{0,16},{16,0},{1,17},{17,1},{2,18},{18,2},{3,19},{19,3},{4,20},{20... | collective-permute-start | bytes 1572872 | tf_op jit(solution)/shard_map/ppermute | solution.py:265
  150.5 19.5 %all-to-all-start.5 = ((bf16[16,64,256]{2,1,0:T(8,128)(2,1)}), bf16[16,64,256]{2,1,0:T(8,128)(2,1)S(1)}, u32[]{:S(2)}, u32[]{:S(2)}) async-start(bf16[16,64,256]{2,1,0:T(8,128)(2,1)} %left_work.7), calls=%async_computation.5 | async-start | bytes 1048576 | tf_op jit(solution)/shard_map/all_to_all | solution.py:259
  273.5 18.5 %all-to-all-start.10 = ((bf16[16,64,256]{2,1,0:T(8,128)(2,1)}), bf16[16,64,256]{2,1,0:T(8,128)(2,1)S(1)}, u32[]{:S(2)}, u32[]{:S(2)}) async-start(bf16[16,64,256]{2,1,0:T(8,128)(2,1)} %get-tuple-element.32), calls=%async_computation.10 | async-start | bytes 1048576 | tf_op jit(solution)/shard_map/all_to_all | solution.py:259
  296.2 27.2 %all-to-all-start.11 = ((bf16[16,128,256]{2,1,0:T(8,128)(2,1)}), bf16[16,128,256]{2,1,0:T(8,128)(2,1)S(1)}, u32[]{:S(2)}, u32[]{:S(2)}) async-start(bf16[16,128,256]{2,1,0:T(8,128)(2,1)} %get-tuple-element.33), calls=%async_computation.11 | async-start | bytes 2097152 | tf_op jit(solution)/shard_map/all_to_all | solution.py:259
  328.2 21.5 %all-to-all-start.12 = ((bf16[16,64,256]{2,1,0:T(8,128)(2,1)}), bf16[16,64,256]{2,1,0:T(8,128)(2,1)S(1)}, u32[]{:S(2)}, u32[]{:S(2)}) async-start(bf16[16,64,256]{2,1,0:T(8,128)(2,1)} %get-tuple-element.36), calls=%async_computation.12 | async-start | bytes 1048576 | tf_op jit(solution)/shard_map/all_to_all | solution.py:259
  354.0 18.7 %all-to-all-start.13 = ((bf16[16,64,256]{2,1,0:T(8,128)(2,1)}), bf16[16,64,256]{2,1,0:T(8,128)(2,1)S(1)}, u32[]{:S(2)}, u32[]{:S(2)}) async-start(bf16[16,64,256]{2,1,0:T(8,128)(2,1)} %get-tuple-element.38), calls=%async_computation.13 | async-start | bytes 1048576 | tf_op jit(solution)/shard_map/all_to_all | solution.py:259
  377.4 18.7 %all-to-all-start.14 = ((bf16[16,64,256]{2,1,0:T(8,128)(2,1)}), bf16[16,64,256]{2,1,0:T(8,128)(2,1)S(1)}, u32[]{:S(2)}, u32[]{:S(2)}) async-start(bf16[16,64,256]{2,1,0:T(8,128)(2,1)} %get-tuple-element.40), calls=%async_computation.14 | async-start | bytes 1048576 | tf_op jit(solution)/shard_map/all_to_all | solution.py:259
  400.3 18.7 %all-to-all-start.15 = ((bf16[16,64,256]{2,1,0:T(8,128)(2,1)}), bf16[16,64,256]{2,1,0:T(8,128)(2,1)S(1)}, u32[]{:S(2)}, u32[]{:S(2)}) async-start(bf16[16,64,256]{2,1,0:T(8,128)(2,1)} %get-tuple-element.42), calls=%async_computation.15 | async-start | bytes 1048576 | tf_op jit(solution)/shard_map/all_to_all | solution.py:259
  423.6 18.7 %all-to-all-start.16 = ((bf16[16,64,256]{2,1,0:T(8,128)(2,1)}), bf16[16,64,256]{2,1,0:T(8,128)(2,1)S(1)}, u32[]{:S(2)}, u32[]{:S(2)}) async-start(bf16[16,64,256]{2,1,0:T(8,128)(2,1)} %get-tuple-element.45), calls=%async_computation.16 | async-start | bytes 1048576 | tf_op jit(solution)/shard_map/all_to_all | solution.py:259
  446.5 18.7 %all-to-all-start.17 = ((bf16[16,64,256]{2,1,0:T(8,128)(2,1)}), bf16[16,64,256]{2,1,0:T(8,128)(2,1)S(1)}, u32[]{:S(2)}, u32[]{:S(2)}) async-start(bf16[16,64,256]{2,1,0:T(8,128)(2,1)} %get-tuple-element.47), calls=%async_computation.17 | async-start | bytes 1048576 | tf_op jit(solution)/shard_map/all_to_all | solution.py:259
  469.9 18.7 %all-to-all-start.18 = ((bf16[16,64,256]{2,1,0:T(8,128)(2,1)}), bf16[16,64,256]{2,1,0:T(8,128)(2,1)S(1)}, u32[]{:S(2)}, u32[]{:S(2)}) async-start(bf16[16,64,256]{2,1,0:T(8,128)(2,1)} %get-tuple-element.49), calls=%async_computation.18 | async-start | bytes 1048576 | tf_op jit(solution)/shard_map/all_to_all | solution.py:259
  474.2 11.0 %collective-permute-start.12 = (bf16[8,128,128]{2,1,0:T(8,128)(2,1)S(1)}, bf16[8,128,128]{2,1,0:T(8,128)(2,1)S(1)}, u32[]{:S(2)}, u32[]{:S(2)}) collective-permute-start(bf16[8,128,128]{2,1,0:T(8,128)(2,1)S(1)} %copy-done.51), channel_id=1, source_target_pairs={{16,0},{17,1},{18,2},{19,3},{20,4},{21,5},{22,6},{23,7},{24,8},{25... | collective-permute-start | bytes 786440 | tf_op jit(solution)/shard_map/ppermute | solution.py:280
  478.4 20.8 %collective-permute-start.16 = (bf16[8,128,128]{2,1,0:T(8,128)(2,1)}, bf16[8,128,128]{2,1,0:T(8,128)(2,1)}, u32[]{:S(2)}, u32[]{:S(2)}) collective-permute-start(bf16[8,128,128]{2,1,0:T(8,128)(2,1)} %last_outer_work.1), channel_id=1, source_target_pairs={{0,16},{16,0},{1,17},{17,1},{2,18},{18,2},{3,19},{19,3},{4,20},{20... | collective-permute-start | bytes 786440 | tf_op jit(solution)/shard_map/ppermute | solution.py:280
  492.9 18.7 %all-to-all-start.19 = ((bf16[16,64,256]{2,1,0:T(8,128)(2,1)}), bf16[16,64,256]{2,1,0:T(8,128)(2,1)S(1)}, u32[]{:S(2)}, u32[]{:S(2)}) async-start(bf16[16,64,256]{2,1,0:T(8,128)(2,1)} %get-tuple-element.51), calls=%async_computation.19 | async-start | bytes 1048576 | tf_op jit(solution)/shard_map/all_to_all | solution.py:259
  497.8 11.2 %collective-permute-start.15 = (bf16[8,128,128]{2,1,0:T(8,128)(2,1)}, bf16[8,128,128]{2,1,0:T(8,128)(2,1)S(1)}, u32[]{:S(2)}, u32[]{:S(2)}) collective-permute-start(bf16[8,128,128]{2,1,0:T(8,128)(2,1)} %get-tuple-element.53), channel_id=1, source_target_pairs={{16,0},{17,1},{18,2},{19,3},{20,4},{21,5},{22,6},{23,7},{24,8},{25... | collective-permute-start | bytes 786440 | tf_op jit(solution)/shard_map/ppermute | solution.py:280
  501.6 15.0 %collective-permute-start.14 = (bf16[8,128,128]{2,1,0:T(8,128)(2,1)S(1)}, bf16[8,128,128]{2,1,0:T(8,128)(2,1)}, u32[]{:S(2)}, u32[]{:S(2)}) collective-permute-start(bf16[8,128,128]{2,1,0:T(8,128)(2,1)S(1)} %copy-done.53), channel_id=1, source_target_pairs={{16,0},{17,1},{18,2},{19,3},{20,4},{21,5},{22,6},{23,7},{24,8},{25... | collective-permute-start | bytes 786440 | tf_op jit(solution)/shard_map/ppermute | solution.py:280
  (63 other events, 303.1 us)

commit v5 on v4

--- a/solution.py
+++ b/solution.py
@@ -146,56 +146,101 @@
     ):
         plan, tokens, picks = self.plan, self.tokens, self.picks
         rows = plan.own * plan.own
-
-        def whole(shape):
-            return pl.BlockSpec(shape, lambda turn, picks: (0,) * len(shape))
-
-        def one_part(part):
-            return pl.BlockSpec((plan.devices, rows, tokens), lambda turn, picks: (0, part, 0))
-
-        natural, square = whole(self.natural), whole(self.square)
-        operands, in_specs = [], []
-        for at, value in enumerate(ins):
-            value, part = value if isinstance(value, tuple) else (value, 0)
-            operands.append(value)
-            in_specs.append(one_part(part) if at < packed else natural)
+        pieces = 2
+        span = plan.own // pieces
+        arrays = [value[0] if isinstance(value, tuple) else value for value in ins]
+        places = [value[1] if isinstance(value, tuple) else 0 for value in ins]
+        direct = 1 if packed else 0
         layer, mine, theirs = weight or (0, None, None)
         matrices = [m for m in (mine, theirs) if m is not None]
-        for matrix in matrices:
-            operands.append(matrix)
-            if len(matrix.shape) == 4:
-                block = (None,) + self.square
-                in_specs.append(pl.BlockSpec(block, lambda turn, picks: (picks[2 * layer], 0, 0, 0)))
-            else:
-                in_specs.append(square)
         unread = list(after) + ([] if join is None else [join])
-        operands += unread
-        in_specs += [pl.BlockSpec(memory_space=pl.ANY)] * len(unread)
+        operands = arrays + matrices + unread
         aliases = {} if join is None else {len(operands): 0}
-        outs, out_specs, scratch = [], [], []
-        if send is True:
-            outs.append(jax.ShapeDtypeStruct(self.sent, BF16))
-            out_specs.append(one_part(0))
-        elif send is not None:
-            outs.append(jax.ShapeDtypeStruct((plan.devices, 2 * rows, tokens), BF16))
-            out_specs.append(one_part(send))
+        outs = []
         if send is not None:
+            parts = 1 if send is True else 2
+            outs.append(jax.ShapeDtypeStruct((plan.devices, parts * rows, tokens), BF16))
+        outs += [jax.ShapeDtypeStruct(self.natural, BF16)] * naturals
+        outs += [jax.ShapeDtypeStruct(self.square, BF16)] * (1 if grads else 0)
+        blocks = outs[0 if send is None else 1 :]
+        scratch = [pltpu.VMEM(self.sent, BF16)] * (packed - direct)
+        scratch += [pltpu.VMEM(self.natural, BF16)] * (len(ins) - packed)
+        scratch += [pltpu.VMEM(self.square, BF16)] * (1 if matrices else 0)
+        scratch += [pltpu.VMEM(block.shape, block.dtype) for block in blocks]
+        if send is not None:
+            scratch.append(pltpu.VMEM(self.sent, BF16))
             scratch.append(pltpu.VMEM((tokens // 128, plan.size * plan.own, 128), F32))
-        outs += [jax.ShapeDtypeStruct(self.natural, BF16)] * naturals
-        out_specs += [natural] * naturals
-        if grads:
-            outs.append(jax.ShapeDtypeStruct(self.square, BF16))
-            out_specs.append(square)
+        scratch.append(pltpu.SemaphoreType.DMA((len(ins) + 1, pieces)))
+        scratch.append(pltpu.SemaphoreType.DMA((len(outs) + 1, pieces)))
 
         def kernel(picks, *refs):
             refs = list(refs)
-            inner = [refs.pop(0) for i in ins]
-            factors = [refs.pop(0) for i in matrices]
-            del refs[: len(unread)]
-            out = refs.pop(0) if send is not None else None
-            inner += [refs.pop(0) for i in range(naturals)]
-            gradients = [refs.pop(0)] if grads else []
-            store = refs[0] if send is not None else None
+
+            def take(count):
+                return [refs.pop(0) for i in range(count)]
+
+            sources, factors = take(len(ins)), take(len(matrices))
+            take(len(unread))
+            out = take(1)[0] if send is not None else None
+            targets = take(len(blocks))
+            inner = []
+            if direct:
+                inner.append(sources[0].at[:, pl.ds(places[0] * rows, rows)])
+            inner += take(len(ins) - direct)
+            matrix = take(1)[0] if matrices else None
+            results = take(len(blocks))
+            ready, store = take(2) if send is not None else (None, None)
+            in_sems, out_sems = take(2)
+            here = picks[2 * layer + 1] == 1
+
+            def arrival(at, piece):
+                source, target = sources[at], inner[at]
+                if at < packed:
+                    width = span * plan.own
+                    source = source.at[:, pl.ds(places[at] * rows + piece * width, width)]
+                    target = target.at[:, pl.ds(piece * width, width)]
+                else:
+                    source = source.at[pl.ds(piece * span, span)]
+                    target = target.at[pl.ds(piece * span, span)]
+                return pltpu.make_async_copy(source, target, in_sems.at[at, piece])
+
+            def factor(which, piece):
+                source = factors[which]
+                if len(source.shape) == 4:
+                    source = source.at[picks[2 * layer]]
+                part = pl.ds(piece * span, span)
+                sem = in_sems.at[len(ins), piece]
+                return pltpu.make_async_copy(source.at[part], matrix.at[part], sem)
+
+            def departure(at, piece):
+                part = pl.ds(piece * span, span)
+                sem = out_sems.at[at, piece]
+                return pltpu.make_async_copy(results[at].at[part], targets[at].at[part], sem)
+
+            width = plan.devices // pieces
+
+            def sending(piece):
+                part = pl.ds(piece * width, width)
+                first = 0 if send is True else send * rows
+                target = out.at[part, pl.ds(first, rows)]
+                sem = out_sems.at[len(outs), piece]
+                return pltpu.make_async_copy(ready.at[part], target, sem)
+
+            for piece in range(pieces):
+                if len(factors) == 2:
+
+                    @pl.when(here)
+                    def _():
+                        factor(0, piece).start()
+
+                    @pl.when(jnp.logical_not(here))
+                    def _():
+                        factor(1, piece).start()
+
+                elif factors:
+                    factor(0, piece).start()
+                for at in range(direct, len(ins)):
+                    arrival(at, piece).start()
 
             def scatter(at, values):
                 spread = pl.ds(at, plan.size, stride=plan.own)
@@ -203,40 +248,53 @@
                     store[part, spread, :] = values[:, part * 128 : (part + 1) * 128]
 
             def gradient(at, values):
-                for ref in gradients:
+                for ref in results[naturals:]:
                     ref[at] = values.astype(ref.dtype)
 
-            here = picks[2 * layer + 1] == 1
             for at in range(plan.own):
-                matrix = None
-                if len(factors) == 2:
-                    matrix = jnp.where(here, factors[0][at], factors[1][at])
-                elif factors:
-                    matrix = factors[0][at]
+                piece = at // span
+                if at % span == 0:
+                    if factors:
+                        factor(0, piece).wait()
+                    for place in range(direct, len(ins)):
+                        arrival(place, piece).wait()
                 put = functools.partial(scatter, at)
-                work(plan, at, put, matrix, functools.partial(gradient, at), *inner)
-            if send is not None:
-                for part in range(tokens // 128):
-                    values = store[part].astype(BF16).reshape(plan.devices, rows, 128)
-                    out[:, :, part * 128 : (part + 1) * 128] = values
-
+                used = matrix[at] if factors else None
+                refs_of_work = inner + results[:naturals]
+                work(plan, at, put, used, functools.partial(gradient, at), *refs_of_work)
+                if at % span == span - 1:
+                    for place in range(len(blocks)):
+                        departure(place, piece).start()
+            for piece in range(pieces):
+                if send is None:
+                    break
+                part = slice(piece * width, (piece + 1) * width)
+                for chunk in range(tokens // 128):
+                    values = store[chunk, part.start * rows : part.stop * rows].astype(BF16)
+                    lanes = slice(chunk * 128, (chunk + 1) * 128)
+                    ready[part, :, lanes] = values.reshape(width, rows, 128)
+                sending(piece).start()
+            for piece in range(pieces):
+                for place in range(len(blocks)):
+                    departure(place, piece).wait()
+                if send is not None:
+                    sending(piece).wait()
+
+        anywhere = pl.BlockSpec(memory_space=pl.ANY)
+        here_already = [pl.BlockSpec(memory_space=pltpu.VMEM)] * direct
         volume = sum(math.prod(o.shape) * o.dtype.itemsize for o in operands + outs)
         products = (1 if matrices else 0) + (1 if grads else 0)
         flops = products * 2 * plan.own * plan.size * plan.size * tokens
         return pl.pallas_call(
             kernel,
             out_shape=outs,
-            grid_spec=pltpu.PrefetchScalarGridSpec(
-                num_scalar_prefetch=1,
-                grid=(1,),
-                in_specs=in_specs,
-                out_specs=out_specs,
-                scratch_shapes=scratch,
-            ),
+            in_specs=[pl.BlockSpec(memory_space=pltpu.SMEM)]
+            + here_already
+            + [anywhere] * (len(operands) - direct),
+            out_specs=[anywhere] * len(outs),
+            scratch_shapes=scratch,
             input_output_aliases=aliases,
-            compiler_params=pltpu.CompilerParams(
-                vmem_limit_bytes=60 * 1024 * 1024, dimension_semantics=("arbitrary",)
-            ),
+            compiler_params=pltpu.CompilerParams(vmem_limit_bytes=52 * 1024 * 1024),
             cost_estimate=pl.CostEstimate(flops=flops, bytes_accessed=volume, transcendentals=0),
             name=work.__name__,
         )(picks, *operands)

time: 530 us -> 520 us (0.981)
  Pallas kernels: 83.3 us -> 71 us
  waiting for transfers between devices: 188 us -> 200 us
  starting transfers between devices: 107 us -> 97.1 us
    pallas_call x25, Pallas kernels: 83.3 us -> 71 us  [run(): pl.pallas_call(kernel, out_shape=outs, in_specs=[pl.BlockSpec(memory_spac...]
    ppermute x12, waiting for transfers between devices: 65.5 us -> 76.5 us  [step(): other = lax.ppermute(leave, 'segment', [(1, 0)] if layer == 0 else both)]
    ppermute x12, starting transfers between devices: 20.3 us -> 9.46 us  [step(): other = lax.ppermute(leave, 'segment', [(1, 0)] if layer == 0 else both)]
    unnamed x110 -> x126, local copies, waits for them, and re-layouts: 15.6 us -> 18.3 us
  transfers between devices with their start and end apart: 32 -> 32, of which waited for: 29 -> 26; matrix products, arithmetic and copies ran while one was open for 2% -> 1% of each run, Pallas kernels for 3% -> 3%
where the time goes in v5:
time: 520 us; the launch traced here: 517 us
  waiting for transfers between devices  200 us (38%)
  blocking collectives  116 us (22%)
  starting transfers between devices  97.1 us (19%)
  Pallas kernels  71 us (14%)
  local copies, waits for them, and re-layouts  21.1 us (4%)
  other arithmetic  8.22 us (2%)
    all_to_all x5, blocking collectives, exchange(): return lax.all_to_all(value, 'blk', 0, 0, tiled=True)  116 us
    ppermute x12, waiting for transfers between devices, step(): other = lax.ppermute(leave, 'segment', [(1, 0)] if layer == 0 else both)  76.5 us
    all_to_all x15, waiting for transfers between devices, exchange(): return lax.all_to_all(value, 'blk', 0, 0, tiled=True)  73.7 us
    all_to_all x15, starting transfers between devices, exchange(): return lax.all_to_all(value, 'blk', 0, 0, tiled=True)  73.1 us
    pallas_call x25, Pallas kernels, run(): pl.pallas_call(kernel, out_shape=outs, in_specs=[pl.BlockSpec(memory_spac...  71 us
    ppermute x4, waiting for transfers between devices, two_segments(): received = [lax.ppermute(factor, 'segment', both) for factor in factors]  47 us
    unnamed x126, local copies, waits for them, and re-layouts  18.3 us
  transfers between devices with their start and end apart: 32, of which 26 were waited for; matrix products, arithmetic and copies ran while one was open for 1% of the time, Pallas kernels for 3%

profile of v5, /device:TPU:0, one launch (start us, length us, event | category | flops | bytes accessed | tf_op | source)
XLA Modules:
  0.0 517.1 jit_solution(10924181791824245069)
XLA Ops:
  15.5 6.1 %all-to-all-start = ((bf16[16,64,256]{2,1,0:T(8,128)(2,1)}), bf16[16,64,256]{2,1,0:T(8,128)(2,1)S(1)}, u32[]{:S(2)}, u32[]{:S(2)}) async-start(bf16[16,64,256]{2,1,0:T(8,128)(2,1)} %start_work.1), calls=%async_computation | async-start | bytes 1048576 | tf_op jit(solution)/shard_map/all_to_all | solution.py:317
  24.1 12.5 %collective-permute-done.1.refs_2_.refs_3_ = bf16[2,8,128,128]{3,2,1,0:T(8,128)(2,1)S(1)} collective-permute-done((bf16[2,8,128,128]{3,2,1,0:T(8,128)(2,1)S(1)}, bf16[2,8,128,128]{3,2,1,0:T(8,128)(2,1)S(1)}, u32[]{:S(2)}, u32[]{:S(2)}) %collective-permute-start.1) | collective-permute-done | bytes 524320 | tf_op jit(solution)/shard_map/ppermute | solution.py:323
  48.9 12.5 %collective-permute-done.2.refs_2_.refs_3_ = bf16[2,8,128,128]{3,2,1,0:T(8,128)(2,1)S(1)} collective-permute-done((bf16[2,8,128,128]{3,2,1,0:T(8,128)(2,1)S(1)}, bf16[2,8,128,128]{3,2,1,0:T(8,128)(2,1)S(1)}, u32[]{:S(2)}, u32[]{:S(2)}) %collective-permute-start.2) | collective-permute-done | bytes 524320 | tf_op jit(solution)/shard_map/ppermute | solution.py:323
  64.8 5.9 %all-to-all-start.2 = ((bf16[16,64,256]{2,1,0:T(8,128)(2,1)}), bf16[16,64,256]{2,1,0:T(8,128)(2,1)}, u32[]{:S(2)}, u32[]{:S(2)}) async-start(bf16[16,64,256]{2,1,0:T(8,128)(2,1)} %copy-done.25), calls=%async_computation.2 | async-start | bytes 1048576 | tf_op jit(solution)/shard_map/all_to_all | solution.py:317
  73.1 12.4 %collective-permute-done.3.refs_2_.refs_3_ = bf16[2,8,128,128]{3,2,1,0:T(8,128)(2,1)S(1)} collective-permute-done((bf16[2,8,128,128]{3,2,1,0:T(8,128)(2,1)S(1)}, bf16[2,8,128,128]{3,2,1,0:T(8,128)(2,1)S(1)}, u32[]{:S(2)}, u32[]{:S(2)}) %collective-permute-start.3) | collective-permute-done | bytes 524320 | tf_op jit(solution)/shard_map/ppermute | solution.py:323
  100.5 9.6 %collective-permute-done.4.refs_3_.refs_4_ = bf16[2,8,128,128]{3,2,1,0:T(8,128)(2,1)} collective-permute-done((bf16[2,8,128,128]{3,2,1,0:T(8,128)(2,1)}, bf16[2,8,128,128]{3,2,1,0:T(8,128)(2,1)}, u32[]{:S(2)}, u32[]{:S(2)}) %collective-permute-start.4) | collective-permute-done | bytes 524320 | tf_op jit(solution)/shard_map/ppermute | solution.py:323
  113.9 30.8 %all_to_all.100.refs_0_.refs_1_ = bf16[16,128,256]{2,1,0:T(8,128)(2,1)} all-to-all(bf16[16,128,256]{2,1,0:T(8,128)(2,1)} %get-tuple-element.29), channel_id=1, replica_groups=mesh['segment'=2,'blk'=16] {'blk'}, dimensions={0} | all-to-all | bytes 2097152 | tf_op jit(solution)/shard_map/all_to_all | solution.py:317
  157.0 10.5 %all-to-all-done.5.refs_0_.refs_1_ = bf16[16,64,256]{2,1,0:T(8,128)(2,1)} async-done(((bf16[16,64,256]{2,1,0:T(8,128)(2,1)}), bf16[16,64,256]{2,1,0:T(8,128)(2,1)}, u32[]{:S(2)}, u32[]{:S(2)}) %all-to-all-start.5) | async-done | bytes 524320 | tf_op jit(solution)/shard_map/all_to_all | solution.py:317
  170.5 29.3 %all_to_all.101.refs_0_.refs_1_ = bf16[16,128,256]{2,1,0:T(8,128)(2,1)} all-to-all(bf16[16,128,256]{2,1,0:T(8,128)(2,1)} %gelu_work.4), channel_id=1, replica_groups=mesh['segment'=2,'blk'=16] {'blk'}, dimensions={0} | all-to-all | bytes 2097152 | tf_op jit(solution)/shard_map/all_to_all | solution.py:317
  202.1 19.2 %all_to_all.102.refs_0_ = bf16[16,64,256]{2,1,0:T(8,128)(2,1)S(1)} all-to-all(bf16[16,64,256]{2,1,0:T(8,128)(2,1)S(1)} %left_work.8), channel_id=1, replica_groups=mesh['segment'=2,'blk'=16] {'blk'}, dimensions={0} | all-to-all | bytes 1048576 | tf_op jit(solution)/shard_map/all_to_all | solution.py:317
  223.6 18.4 %all_to_all.103.refs_0_.refs_1_ = bf16[16,64,256]{2,1,0:T(8,128)(2,1)S(1)} all-to-all(bf16[16,64,256]{2,1,0:T(8,128)(2,1)S(1)} %get-tuple-element.31), channel_id=1, replica_groups=mesh['segment'=2,'blk'=16] {'blk'}, dimensions={0} | all-to-all | bytes 1048576 | tf_op jit(solution)/shard_map/all_to_all | solution.py:317
  244.2 18.4 %all_to_all.104.refs_1_.refs_0_ = bf16[16,64,256]{2,1,0:T(8,128)(2,1)S(1)} all-to-all(bf16[16,64,256]{2,1,0:T(8,128)(2,1)S(1)} %left_work.9), channel_id=1, replica_groups=mesh['segment'=2,'blk'=16] {'blk'}, dimensions={0} | all-to-all | bytes 1048576 | tf_op jit(solution)/shard_map/all_to_all | solution.py:317
  275.4 10.7 %all-to-all-done.10.refs_0_ = bf16[16,64,256]{2,1,0:T(8,128)(2,1)} async-done(((bf16[16,64,256]{2,1,0:T(8,128)(2,1)}), bf16[16,64,256]{2,1,0:T(8,128)(2,1)}, u32[]{:S(2)}, u32[]{:S(2)}) %all-to-all-start.10) | async-done | bytes 524320 | tf_op jit(solution)/shard_map/all_to_all | solution.py:317
  294.3 8.5 %collective-permute-done.5.refs_5_ = bf16[8,128,128]{2,1,0:T(8,128)(2,1)S(1)} collective-permute-done((bf16[8,128,128]{2,1,0:T(8,128)(2,1)S(1)}, bf16[8,128,128]{2,1,0:T(8,128)(2,1)S(1)}, u32[]{:S(2)}, u32[]{:S(2)}) %collective-permute-start.5) | collective-permute-done | bytes 262176 | tf_op jit(solution)/shard_map/ppermute | solution.py:338
  302.7 14.2 %all-to-all-done.11.refs_0_.refs_1_ = bf16[16,128,256]{2,1,0:T(8,128)(2,1)S(1)} async-done(((bf16[16,128,256]{2,1,0:T(8,128)(2,1)}), bf16[16,128,256]{2,1,0:T(8,128)(2,1)S(1)}, u32[]{:S(2)}, u32[]{:S(2)}) %all-to-all-start.11) | async-done | bytes 1048608 | tf_op jit(solution)/shard_map/all_to_all | solution.py:317
  323.2 6.9 %all-to-all-start.12 = ((bf16[16,64,256]{2,1,0:T(8,128)(2,1)}), bf16[16,64,256]{2,1,0:T(8,128)(2,1)S(1)}, u32[]{:S(2)}, u32[]{:S(2)}) async-start(bf16[16,64,256]{2,1,0:T(8,128)(2,1)} %get-tuple-element.36), calls=%async_computation.12 | async-start | bytes 1048576 | tf_op jit(solution)/shard_map/all_to_all | solution.py:317
  330.3 8.5 %collective-permute-done.6.refs_4_ = bf16[8,128,128]{2,1,0:T(8,128)(2,1)S(1)} collective-permute-done((bf16[8,128,128]{2,1,0:T(8,128)(2,1)S(1)}, bf16[8,128,128]{2,1,0:T(8,128)(2,1)S(1)}, u32[]{:S(2)}, u32[]{:S(2)}) %collective-permute-start.6) | collective-permute-done | bytes 262176 | tf_op jit(solution)/shard_map/ppermute | solution.py:338
  352.4 8.5 %collective-permute-done.7.refs_4_ = bf16[8,128,128]{2,1,0:T(8,128)(2,1)S(1)} collective-permute-done((bf16[8,128,128]{2,1,0:T(8,128)(2,1)S(1)}, bf16[8,128,128]{2,1,0:T(8,128)(2,1)S(1)}, u32[]{:S(2)}, u32[]{:S(2)}) %collective-permute-start.7) | collective-permute-done | bytes 262176 | tf_op jit(solution)/shard_map/ppermute | solution.py:338
  374.8 8.5 %collective-permute-done.8.refs_4_ = bf16[8,128,128]{2,1,0:T(8,128)(2,1)S(1)} collective-permute-done((bf16[8,128,128]{2,1,0:T(8,128)(2,1)S(1)}, bf16[8,128,128]{2,1,0:T(8,128)(2,1)S(1)}, u32[]{:S(2)}, u32[]{:S(2)}) %collective-permute-start.8) | collective-permute-done | bytes 262176 | tf_op jit(solution)/shard_map/ppermute | solution.py:338
  396.8 8.5 %collective-permute-done.9.refs_5_ = bf16[8,128,128]{2,1,0:T(8,128)(2,1)S(1)} collective-permute-done((bf16[8,128,128]{2,1,0:T(8,128)(2,1)S(1)}, bf16[8,128,128]{2,1,0:T(8,128)(2,1)S(1)}, u32[]{:S(2)}, u32[]{:S(2)}) %collective-permute-start.9) | collective-permute-done | bytes 262176 | tf_op jit(solution)/shard_map/ppermute | solution.py:338
  420.4 8.5 %collective-permute-done.10.refs_4_ = bf16[8,128,128]{2,1,0:T(8,128)(2,1)S(1)} collective-permute-done((bf16[8,128,128]{2,1,0:T(8,128)(2,1)S(1)}, bf16[8,128,128]{2,1,0:T(8,128)(2,1)S(1)}, u32[]{:S(2)}, u32[]{:S(2)}) %collective-permute-start.10) | collective-permute-done | bytes 262176 | tf_op jit(solution)/shard_map/ppermute | solution.py:338
  443.1 8.5 %collective-permute-done.11.refs_4_ = bf16[8,128,128]{2,1,0:T(8,128)(2,1)S(1)} collective-permute-done((bf16[8,128,128]{2,1,0:T(8,128)(2,1)S(1)}, bf16[8,128,128]{2,1,0:T(8,128)(2,1)S(1)}, u32[]{:S(2)}, u32[]{:S(2)}) %collective-permute-start.11) | collective-permute-done | bytes 262176 | tf_op jit(solution)/shard_map/ppermute | solution.py:338
  495.4 6.2 %collective-permute-done.15 = bf16[8,128,128]{2,1,0:T(8,128)(2,1)S(1)} collective-permute-done((bf16[8,128,128]{2,1,0:T(8,128)(2,1)}, bf16[8,128,128]{2,1,0:T(8,128)(2,1)S(1)}, u32[]{:S(2)}, u32[]{:S(2)}) %collective-permute-start.15) | collective-permute-done | bytes 262176 | tf_op jit(solution)/shard_map/ppermute | solution.py:338
  509.3 6.4 %collective-permute-done.13 = bf16[8,128,128]{2,1,0:T(8,128)(2,1)S(1)} collective-permute-done((bf16[8,128,128]{2,1,0:T(8,128)(2,1)S(1)}, bf16[8,128,128]{2,1,0:T(8,128)(2,1)S(1)}, u32[]{:S(2)}, u32[]{:S(2)}) %collective-permute-start.13) | collective-permute-done | bytes 262176 | tf_op jit(solution)/shard_map/ppermute | solution.py:338
  (210 shorter events, 223.6 us)
Async XLA Ops:
  1.7 10.4 %collective-permute-start = (bf16[8,128,128]{2,1,0:T(8,128)(2,1)S(1)}, bf16[8,128,128]{2,1,0:T(8,128)(2,1)S(1)}, u32[]{:S(2)}, u32[]{:S(2)}) collective-permute-start(bf16[8,128,128]{2,1,0:T(8,128)(2,1)S(1)} %slice_bitcast_fusion), channel_id=1, source_target_pairs={{0,16},{1,17},{2,18},{3,19},{4,20},{5,21},{6,22},{7,23},{8,24},{9,... | collective-permute-start | bytes 786440 | tf_op jit(solution)/shard_map/ppermute | solution.py:321
  15.5 21.1 %all-to-all-start = ((bf16[16,64,256]{2,1,0:T(8,128)(2,1)}), bf16[16,64,256]{2,1,0:T(8,128)(2,1)S(1)}, u32[]{:S(2)}, u32[]{:S(2)}) async-start(bf16[16,64,256]{2,1,0:T(8,128)(2,1)} %start_work.1), calls=%async_computation | async-start | bytes 1048576 | tf_op jit(solution)/shard_map/all_to_all | solution.py:317
  21.5 15.0 %collective-permute-start.1 = (bf16[2,8,128,128]{3,2,1,0:T(8,128)(2,1)S(1)}, bf16[2,8,128,128]{3,2,1,0:T(8,128)(2,1)S(1)}, u32[]{:S(2)}, u32[]{:S(2)}) collective-permute-start(bf16[2,8,128,128]{3,2,1,0:T(8,128)(2,1)S(1)} %copy-done.3), channel_id=1, source_target_pairs={{0,16},{16,0},{1,17},{17,1},{2,18},{18,2},{3,19},{19,3},{4,20},{20... | collective-permute-start | bytes 1572872 | tf_op jit(solution)/shard_map/ppermute | solution.py:323
  40.6 20.8 %all-to-all-start.1 = ((bf16[16,64,256]{2,1,0:T(8,128)(2,1)}), bf16[16,64,256]{2,1,0:T(8,128)(2,1)S(1)}, u32[]{:S(2)}, u32[]{:S(2)}) async-start(bf16[16,64,256]{2,1,0:T(8,128)(2,1)} %copy-done.24), calls=%async_computation.1 | async-start | bytes 1048576 | tf_op jit(solution)/shard_map/all_to_all | solution.py:317
  46.5 14.9 %collective-permute-start.2 = (bf16[2,8,128,128]{3,2,1,0:T(8,128)(2,1)S(1)}, bf16[2,8,128,128]{3,2,1,0:T(8,128)(2,1)S(1)}, u32[]{:S(2)}, u32[]{:S(2)}) collective-permute-start(bf16[2,8,128,128]{3,2,1,0:T(8,128)(2,1)S(1)} %copy-done.2), channel_id=1, source_target_pairs={{0,16},{16,0},{1,17},{17,1},{2,18},{18,2},{3,19},{19,3},{4,20},{20... | collective-permute-start | bytes 1572872 | tf_op jit(solution)/shard_map/ppermute | solution.py:323
  64.8 20.8 %all-to-all-start.2 = ((bf16[16,64,256]{2,1,0:T(8,128)(2,1)}), bf16[16,64,256]{2,1,0:T(8,128)(2,1)}, u32[]{:S(2)}, u32[]{:S(2)}) async-start(bf16[16,64,256]{2,1,0:T(8,128)(2,1)} %copy-done.25), calls=%async_computation.2 | async-start | bytes 1048576 | tf_op jit(solution)/shard_map/all_to_all | solution.py:317
  70.7 14.8 %collective-permute-start.3 = (bf16[2,8,128,128]{3,2,1,0:T(8,128)(2,1)S(1)}, bf16[2,8,128,128]{3,2,1,0:T(8,128)(2,1)S(1)}, u32[]{:S(2)}, u32[]{:S(2)}) collective-permute-start(bf16[2,8,128,128]{3,2,1,0:T(8,128)(2,1)S(1)} %copy-done.9), channel_id=1, source_target_pairs={{0,16},{16,0},{1,17},{17,1},{2,18},{18,2},{3,19},{19,3},{4,20},{20... | collective-permute-start | bytes 1572872 | tf_op jit(solution)/shard_map/ppermute | solution.py:323
  89.2 20.9 %all-to-all-start.3 = ((bf16[16,64,256]{2,1,0:T(8,128)(2,1)}), bf16[16,64,256]{2,1,0:T(8,128)(2,1)S(1)}, u32[]{:S(2)}, u32[]{:S(2)}) async-start(bf16[16,64,256]{2,1,0:T(8,128)(2,1)} %copy-done.23), calls=%async_computation.3 | async-start | bytes 1048576 | tf_op jit(solution)/shard_map/all_to_all | solution.py:317
  95.0 15.1 %collective-permute-start.4 = (bf16[2,8,128,128]{3,2,1,0:T(8,128)(2,1)}, bf16[2,8,128,128]{3,2,1,0:T(8,128)(2,1)}, u32[]{:S(2)}, u32[]{:S(2)}) collective-permute-start(bf16[2,8,128,128]{3,2,1,0:T(8,128)(2,1)} %refs_3_.3), channel_id=1, source_target_pairs={{0,16},{16,0},{1,17},{17,1},{2,18},{18,2},{3,19},{19,3},{4,20},{20... | collective-permute-start | bytes 1572872 | tf_op jit(solution)/shard_map/ppermute | solution.py:323
  147.7 19.7 %all-to-all-start.5 = ((bf16[16,64,256]{2,1,0:T(8,128)(2,1)}), bf16[16,64,256]{2,1,0:T(8,128)(2,1)}, u32[]{:S(2)}, u32[]{:S(2)}) async-start(bf16[16,64,256]{2,1,0:T(8,128)(2,1)} %left_work.7), calls=%async_computation.5 | async-start | bytes 1048576 | tf_op jit(solution)/shard_map/all_to_all | solution.py:317
  267.2 18.9 %all-to-all-start.10 = ((bf16[16,64,256]{2,1,0:T(8,128)(2,1)}), bf16[16,64,256]{2,1,0:T(8,128)(2,1)}, u32[]{:S(2)}, u32[]{:S(2)}) async-start(bf16[16,64,256]{2,1,0:T(8,128)(2,1)} %copy-done.39), calls=%async_computation.10 | async-start | bytes 1048576 | tf_op jit(solution)/shard_map/all_to_all | solution.py:317
  290.0 27.0 %all-to-all-start.11 = ((bf16[16,128,256]{2,1,0:T(8,128)(2,1)}), bf16[16,128,256]{2,1,0:T(8,128)(2,1)S(1)}, u32[]{:S(2)}, u32[]{:S(2)}) async-start(bf16[16,128,256]{2,1,0:T(8,128)(2,1)} %get-tuple-element.33), calls=%async_computation.11 | async-start | bytes 2097152 | tf_op jit(solution)/shard_map/all_to_all | solution.py:317
  323.2 21.4 %all-to-all-start.12 = ((bf16[16,64,256]{2,1,0:T(8,128)(2,1)}), bf16[16,64,256]{2,1,0:T(8,128)(2,1)S(1)}, u32[]{:S(2)}, u32[]{:S(2)}) async-start(bf16[16,64,256]{2,1,0:T(8,128)(2,1)} %get-tuple-element.36), calls=%async_computation.12 | async-start | bytes 1048576 | tf_op jit(solution)/shard_map/all_to_all | solution.py:317
  348.1 18.6 %all-to-all-start.13 = ((bf16[16,64,256]{2,1,0:T(8,128)(2,1)}), bf16[16,64,256]{2,1,0:T(8,128)(2,1)S(1)}, u32[]{:S(2)}, u32[]{:S(2)}) async-start(bf16[16,64,256]{2,1,0:T(8,128)(2,1)} %get-tuple-element.38), calls=%async_computation.13 | async-start | bytes 1048576 | tf_op jit(solution)/shard_map/all_to_all | solution.py:317
  370.4 18.6 %all-to-all-start.14 = ((bf16[16,64,256]{2,1,0:T(8,128)(2,1)}), bf16[16,64,256]{2,1,0:T(8,128)(2,1)S(1)}, u32[]{:S(2)}, u32[]{:S(2)}) async-start(bf16[16,64,256]{2,1,0:T(8,128)(2,1)} %get-tuple-element.40), calls=%async_computation.14 | async-start | bytes 1048576 | tf_op jit(solution)/shard_map/all_to_all | solution.py:317
  392.5 18.6 %all-to-all-start.15 = ((bf16[16,64,256]{2,1,0:T(8,128)(2,1)}), bf16[16,64,256]{2,1,0:T(8,128)(2,1)S(1)}, u32[]{:S(2)}, u32[]{:S(2)}) async-start(bf16[16,64,256]{2,1,0:T(8,128)(2,1)} %get-tuple-element.42), calls=%async_computation.15 | async-start | bytes 1048576 | tf_op jit(solution)/shard_map/all_to_all | solution.py:317
  416.0 18.6 %all-to-all-start.16 = ((bf16[16,64,256]{2,1,0:T(8,128)(2,1)}), bf16[16,64,256]{2,1,0:T(8,128)(2,1)S(1)}, u32[]{:S(2)}, u32[]{:S(2)}) async-start(bf16[16,64,256]{2,1,0:T(8,128)(2,1)} %get-tuple-element.45), calls=%async_computation.16 | async-start | bytes 1048576 | tf_op jit(solution)/shard_map/all_to_all | solution.py:317
  438.8 18.5 %all-to-all-start.17 = ((bf16[16,64,256]{2,1,0:T(8,128)(2,1)}), bf16[16,64,256]{2,1,0:T(8,128)(2,1)S(1)}, u32[]{:S(2)}, u32[]{:S(2)}) async-start(bf16[16,64,256]{2,1,0:T(8,128)(2,1)} %get-tuple-element.47), calls=%async_computation.17 | async-start | bytes 1048576 | tf_op jit(solution)/shard_map/all_to_all | solution.py:317
  462.6 18.7 %all-to-all-start.18 = ((bf16[16,64,256]{2,1,0:T(8,128)(2,1)}), bf16[16,64,256]{2,1,0:T(8,128)(2,1)S(1)}, u32[]{:S(2)}, u32[]{:S(2)}) async-start(bf16[16,64,256]{2,1,0:T(8,128)(2,1)} %copy-done.38), calls=%async_computation.18 | async-start | bytes 1048576 | tf_op jit(solution)/shard_map/all_to_all | solution.py:317
  466.8 11.2 %collective-permute-start.12 = (bf16[8,128,128]{2,1,0:T(8,128)(2,1)}, bf16[8,128,128]{2,1,0:T(8,128)(2,1)S(1)}, u32[]{:S(2)}, u32[]{:S(2)}) collective-permute-start(bf16[8,128,128]{2,1,0:T(8,128)(2,1)} %copy-done.56), channel_id=1, source_target_pairs={{16,0},{17,1},{18,2},{19,3},{20,4},{21,5},{22,6},{23,7},{24,8},{25... | collective-permute-start | bytes 786440 | tf_op jit(solution)/shard_map/ppermute | solution.py:338
  470.8 20.8 %collective-permute-start.16 = (bf16[8,128,128]{2,1,0:T(8,128)(2,1)}, bf16[8,128,128]{2,1,0:T(8,128)(2,1)}, u32[]{:S(2)}, u32[]{:S(2)}) collective-permute-start(bf16[8,128,128]{2,1,0:T(8,128)(2,1)} %last_outer_work.1), channel_id=1, source_target_pairs={{0,16},{16,0},{1,17},{17,1},{2,18},{18,2},{3,19},{19,3},{4,20},{20... | collective-permute-start | bytes 786440 | tf_op jit(solution)/shard_map/ppermute | solution.py:338
  485.5 18.7 %all-to-all-start.19 = ((bf16[16,64,256]{2,1,0:T(8,128)(2,1)}), bf16[16,64,256]{2,1,0:T(8,128)(2,1)S(1)}, u32[]{:S(2)}, u32[]{:S(2)}) async-start(bf16[16,64,256]{2,1,0:T(8,128)(2,1)} %get-tuple-element.51), calls=%async_computation.19 | async-start | bytes 1048576 | tf_op jit(solution)/shard_map/all_to_all | solution.py:317
  490.4 11.2 %collective-permute-start.15 = (bf16[8,128,128]{2,1,0:T(8,128)(2,1)}, bf16[8,128,128]{2,1,0:T(8,128)(2,1)S(1)}, u32[]{:S(2)}, u32[]{:S(2)}) collective-permute-start(bf16[8,128,128]{2,1,0:T(8,128)(2,1)} %copy-done.58), channel_id=1, source_target_pairs={{16,0},{17,1},{18,2},{19,3},{20,4},{21,5},{22,6},{23,7},{24,8},{25... | collective-permute-start | bytes 786440 | tf_op jit(solution)/shard_map/ppermute | solution.py:338
  494.1 12.9 %collective-permute-start.14 = (bf16[8,128,128]{2,1,0:T(8,128)(2,1)}, bf16[8,128,128]{2,1,0:T(8,128)(2,1)}, u32[]{:S(2)}, u32[]{:S(2)}) collective-permute-start(bf16[8,128,128]{2,1,0:T(8,128)(2,1)} %get-tuple-element.52), channel_id=1, source_target_pairs={{16,0},{17,1},{18,2},{19,3},{20,4},{21,5},{22,6},{23,7},{24,8},{25... | collective-permute-start | bytes 786440 | tf_op jit(solution)/shard_map/ppermute | solution.py:338
  (71 other events, 573.6 us)

commit v6 on v5

--- a/solution.py
+++ b/solution.py
@@ -318,14 +318,18 @@
 
     micro = lax.dynamic_index_in_dim(inputs, segment, 0, keepdims=False)
     grad = lax.dynamic_index_in_dim(cotangent, segment, 0, keepdims=False)
-    early = lax.ppermute(factors[0][0], "segment", [(0, 1)])
-    early = jnp.where(segment == 0, factors[0][0], early)
-    received = [lax.ppermute(factor, "segment", both) for factor in factors]
+    early = [lax.ppermute(factor[0], "segment", [(0, 1)]) for factor in factors]
+
+    first_has_two = sections[0] == 2
+    middle, late = [], []
+    for factor in factors:
+        leave = jnp.where(segment == 0, factor[1], factor[0])
+        middle.append(lax.ppermute(leave, "segment", both))
+        last = lax.ppermute(factor[1], "segment", [(1, 0)])
+        late.append(jnp.where(first_has_two, middle[-1], last))
 
     def weight(layer, at):
-        if layer == 0 and at == 0:
-            return layer, early, None
-        return layer, factors[at], received[at]
+        return layer, factors[at], (early, middle, late)[layer][at]
 
     waiting = [(), ()]
     parts = [[None] * 4 for layer in range(count)]
@@ -355,7 +359,8 @@
     sent, state = run(residual_work, ins, 1, weight(1, 0), send=0, naturals=1, join=beside)
     values = exchange(sent)
     inner, last_grad_c = (values, 0), (values, 1)
-    upper = exchange(run(left_work, (inner,), 1, weight(1, 1))[0])
+    sent = run(left_work, (inner,), 1, weight(1, 1), after=(late[3],))[0]
+    upper = exchange(sent)
     beside = run(last_back_left_work, (last_grad_c,), 1, weight(2, 3), send=1)[0]
     values = exchange(run(gelu_work, (upper,), 1, weight(1, 2), send=0, join=beside)[0])
     inner_two, last_grad_a = (values, 0), (values, 1)
@@ -384,7 +389,6 @@
     step(0, 0, end_work, (exchange(sent), state), 1, plain=True, send=None)
 
     outs = []
-    first_has_two = sections[0] == 2
     for at in range(4):
         zero, one, two = [
             stay.astype(F32) + other.astype(F32) for stay, other in (p[at] for p in parts)

time: 520 us -> 518 us (level)
  blocking collectives: 116 us -> 29.3 us
  starting transfers between devices: 97.1 us -> 156 us
  waiting for transfers between devices: 200 us -> 218 us
  local copies, waits for them, and re-layouts: 21.1 us -> 30.2 us
    all_to_all x5 -> x1, blocking collectives: 116 us -> 29.3 us  [exchange(): return lax.all_to_all(value, 'blk', 0, 0, tiled=True)]
    ppermute x12, starting transfers between devices: 9.46 us -> 33.7 us  [step(): other = lax.ppermute(leave, 'segment', [(1, 0)] if layer == 0 else both)]
    ppermute x5 -> x12, waiting for transfers between devices: 49.3 us -> 70.4 us  [the longest x4 35 us: two_segments(): last = lax.ppermute(factor[1], 'segment', [(1, 0)])]
    ppermute x5 -> x12, starting transfers between devices: 14.5 us -> 34.5 us  [the longest x4 18 us: two_segments(): early = [lax.ppermute(factor[0], 'segment', [(0, 1)]) for factor in factors]]
    all_to_all x15 -> x19, starting transfers between devices: 73.1 us -> 88.3 us  [exchange(): return lax.all_to_all(value, 'blk', 0, 0, tiled=True)]
    ppermute x12, waiting for transfers between devices: 76.5 us -> 67.1 us  [step(): other = lax.ppermute(leave, 'segment', [(1, 0)] if layer == 0 else both)]
    all_to_all x15 -> x19, waiting for transfers between devices: 73.7 us -> 80.5 us  [exchange(): return lax.all_to_all(value, 'blk', 0, 0, tiled=True)]
    unnamed x126 -> x178, local copies, waits for them, and re-layouts: 18.3 us -> 24.2 us
  transfers between devices with their start and end apart: 32 -> 43, of which waited for: 26 -> 41; matrix products, arithmetic and copies ran while one was open for 1% -> 2% of each run, Pallas kernels for 3% -> 3%
where the time goes in v6:
time: 518 us; the launch traced here: 515 us
  waiting for transfers between devices  218 us (42%)
  starting transfers between devices  156 us (30%)
  Pallas kernels  67.6 us (13%)
  local copies, waits for them, and re-layouts  30.2 us (6%)
  blocking collectives  29.3 us (6%)
  other arithmetic  8.56 us (2%)
    all_to_all x19, starting transfers between devices, exchange(): return lax.all_to_all(value, 'blk', 0, 0, tiled=True)  88.3 us
    all_to_all x19, waiting for transfers between devices, exchange(): return lax.all_to_all(value, 'blk', 0, 0, tiled=True)  80.5 us
    pallas_call x25, Pallas kernels, run(): pl.pallas_call(kernel, out_shape=outs, in_specs=[pl.BlockSpec(memory_spac...  67.6 us
    ppermute x12, waiting for transfers between devices, step(): other = lax.ppermute(leave, 'segment', [(1, 0)] if layer == 0 else both)  67.1 us
    ppermute x4, waiting for transfers between devices, two_segments(): last = lax.ppermute(factor[1], 'segment', [(1, 0)])  35 us
    ppermute x12, starting transfers between devices, step(): other = lax.ppermute(leave, 'segment', [(1, 0)] if layer == 0 else both)  33.7 us
    all_to_all x1, blocking collectives, exchange(): return lax.all_to_all(value, 'blk', 0, 0, tiled=True)  29.3 us
    unnamed x178, local copies, waits for them, and re-layouts  24.2 us
  transfers between devices with their start and end apart: 43, of which 41 were waited for; matrix products, arithmetic and copies ran while one was open for 2% of the time, Pallas kernels for 3%

profile of v6, /device:TPU:0, one launch (start us, length us, event | category | flops | bytes accessed | tf_op | source)
XLA Modules:
  0.0 514.7 jit_solution(4949642556556856950)
XLA Ops:
  16.1 6.0 %all-to-all-start = ((bf16[16,64,256]{2,1,0:T(8,128)(2,1)}), bf16[16,64,256]{2,1,0:T(8,128)(2,1)S(1)}, u32[]{:S(2)}, u32[]{:S(2)}) async-start(bf16[16,64,256]{2,1,0:T(8,128)(2,1)} %start_work.1), calls=%async_computation | async-start | bytes 1048576 | tf_op jit(solution)/shard_map/all_to_all | solution.py:317
  27.3 6.1 %collective-permute-done.1.refs_2_.refs_3_ = bf16[8,128,128]{2,1,0:T(8,128)(2,1)S(1)} collective-permute-done((bf16[8,128,128]{2,1,0:T(8,128)(2,1)S(1)}, bf16[8,128,128]{2,1,0:T(8,128)(2,1)S(1)}, u32[]{:S(2)}, u32[]{:S(2)}) %collective-permute-start.1) | collective-permute-done | bytes 262176 | tf_op jit(solution)/shard_map/ppermute | solution.py:321
  49.1 6.1 %collective-permute-done.2.refs_2_.refs_3_ = bf16[8,128,128]{2,1,0:T(8,128)(2,1)S(1)} collective-permute-done((bf16[8,128,128]{2,1,0:T(8,128)(2,1)S(1)}, bf16[8,128,128]{2,1,0:T(8,128)(2,1)S(1)}, u32[]{:S(2)}, u32[]{:S(2)}) %collective-permute-start.2) | collective-permute-done | bytes 262176 | tf_op jit(solution)/shard_map/ppermute | solution.py:321
  71.4 6.0 %collective-permute-done.3.refs_2_.refs_3_ = bf16[8,128,128]{2,1,0:T(8,128)(2,1)S(1)} collective-permute-done((bf16[8,128,128]{2,1,0:T(8,128)(2,1)S(1)}, bf16[8,128,128]{2,1,0:T(8,128)(2,1)S(1)}, u32[]{:S(2)}, u32[]{:S(2)}) %collective-permute-start.3) | collective-permute-done | bytes 262176 | tf_op jit(solution)/shard_map/ppermute | solution.py:321
  120.9 5.6 %collective-permute-done.7 = bf16[8,128,128]{2,1,0:T(8,128)(2,1)S(1)} collective-permute-done((bf16[8,128,128]{2,1,0:T(8,128)(2,1)S(1)}, bf16[8,128,128]{2,1,0:T(8,128)(2,1)S(1)}, u32[]{:S(2)}, u32[]{:S(2)}) %collective-permute-start.7) | collective-permute-done | bytes 262176 | tf_op jit(solution)/shard_map/ppermute | solution.py:328
  126.5 5.3 %collective-permute-done.5.refs_2_.refs_3_ = bf16[8,128,128]{2,1,0:T(8,128)(2,1)S(1)} collective-permute-done((bf16[8,128,128]{2,1,0:T(8,128)(2,1)S(1)}, bf16[8,128,128]{2,1,0:T(8,128)(2,1)S(1)}, u32[]{:S(2)}, u32[]{:S(2)}) %collective-permute-start.5) | collective-permute-done | bytes 262176 | tf_op jit(solution)/shard_map/ppermute | solution.py:327
  138.2 6.8 %all-to-all-start.5 = ((bf16[16,64,256]{2,1,0:T(8,128)(2,1)}), bf16[16,64,256]{2,1,0:T(8,128)(2,1)S(1)}, u32[]{:S(2)}, u32[]{:S(2)}) async-start(bf16[16,64,256]{2,1,0:T(8,128)(2,1)} %copy-done.35), calls=%async_computation.5 | async-start | bytes 1048576 | tf_op jit(solution)/shard_map/all_to_all | solution.py:317
  162.1 29.3 %all_to_all.100.refs_0_.refs_1_ = bf16[16,128,256]{2,1,0:T(8,128)(2,1)} all-to-all(bf16[16,128,256]{2,1,0:T(8,128)(2,1)} %gelu_work.4), channel_id=1, replica_groups=mesh['segment'=2,'blk'=16] {'blk'}, dimensions={0} | all-to-all | bytes 2097152 | tf_op jit(solution)/shard_map/all_to_all | solution.py:317
  194.4 5.1 all-to-all-start.7
  200.8 9.8 %collective-permute-done.9 = bf16[8,128,128]{2,1,0:T(8,128)(2,1)S(1)} collective-permute-done((bf16[8,128,128]{2,1,0:T(8,128)(2,1)S(1)}, bf16[8,128,128]{2,1,0:T(8,128)(2,1)S(1)}, u32[]{:S(2)}, u32[]{:S(2)}) %collective-permute-start.9) | collective-permute-done | bytes 262176 | tf_op jit(solution)/shard_map/ppermute | solution.py:328
  223.5 9.7 %collective-permute-done.10 = bf16[8,128,128]{2,1,0:T(8,128)(2,1)S(1)} collective-permute-done((bf16[8,128,128]{2,1,0:T(8,128)(2,1)S(1)}, bf16[8,128,128]{2,1,0:T(8,128)(2,1)S(1)}, u32[]{:S(2)}, u32[]{:S(2)}) %collective-permute-start.10) | collective-permute-done | bytes 262176 | tf_op jit(solution)/shard_map/ppermute | solution.py:328
  244.6 9.8 %collective-permute-done.11 = bf16[8,128,128]{2,1,0:T(8,128)(2,1)S(1)} collective-permute-done((bf16[8,128,128]{2,1,0:T(8,128)(2,1)S(1)}, bf16[8,128,128]{2,1,0:T(8,128)(2,1)S(1)}, u32[]{:S(2)}, u32[]{:S(2)}) %collective-permute-start.11) | collective-permute-done | bytes 262176 | tf_op jit(solution)/shard_map/ppermute | solution.py:328
  269.5 11.9 %all-to-all-done.10.refs_0_ = bf16[16,64,256]{2,1,0:T(8,128)(2,1)} async-done(((bf16[16,64,256]{2,1,0:T(8,128)(2,1)}), bf16[16,64,256]{2,1,0:T(8,128)(2,1)}, u32[]{:S(2)}, u32[]{:S(2)}) %all-to-all-start.10) | async-done | bytes 524320 | tf_op jit(solution)/shard_map/all_to_all | solution.py:317
  292.8 6.9 %collective-permute-done.12.refs_5_ = bf16[8,128,128]{2,1,0:T(8,128)(2,1)S(1)} collective-permute-done((bf16[8,128,128]{2,1,0:T(8,128)(2,1)S(1)}, bf16[8,128,128]{2,1,0:T(8,128)(2,1)S(1)}, u32[]{:S(2)}, u32[]{:S(2)}) %collective-permute-start.12) | collective-permute-done | bytes 262176 | tf_op jit(solution)/shard_map/ppermute | solution.py:342
  299.7 12.2 %all-to-all-done.11.refs_0_.refs_1_ = bf16[16,128,256]{2,1,0:T(8,128)(2,1)S(1)} async-done(((bf16[16,128,256]{2,1,0:T(8,128)(2,1)}), bf16[16,128,256]{2,1,0:T(8,128)(2,1)S(1)}, u32[]{:S(2)}, u32[]{:S(2)}) %all-to-all-start.11) | async-done | bytes 1048608 | tf_op jit(solution)/shard_map/all_to_all | solution.py:317
  318.2 7.0 %all-to-all-start.12 = ((bf16[16,64,256]{2,1,0:T(8,128)(2,1)}), bf16[16,64,256]{2,1,0:T(8,128)(2,1)S(1)}, u32[]{:S(2)}, u32[]{:S(2)}) async-start(bf16[16,64,256]{2,1,0:T(8,128)(2,1)} %get-tuple-element.36), calls=%async_computation.12 | async-start | bytes 1048576 | tf_op jit(solution)/shard_map/all_to_all | solution.py:317
  328.9 6.9 %collective-permute-done.13.refs_4_ = bf16[8,128,128]{2,1,0:T(8,128)(2,1)S(1)} collective-permute-done((bf16[8,128,128]{2,1,0:T(8,128)(2,1)S(1)}, bf16[8,128,128]{2,1,0:T(8,128)(2,1)S(1)}, u32[]{:S(2)}, u32[]{:S(2)}) %collective-permute-start.13) | collective-permute-done | bytes 262176 | tf_op jit(solution)/shard_map/ppermute | solution.py:342
  351.0 6.9 %collective-permute-done.14.refs_4_ = bf16[8,128,128]{2,1,0:T(8,128)(2,1)S(1)} collective-permute-done((bf16[8,128,128]{2,1,0:T(8,128)(2,1)S(1)}, bf16[8,128,128]{2,1,0:T(8,128)(2,1)S(1)}, u32[]{:S(2)}, u32[]{:S(2)}) %collective-permute-start.14) | collective-permute-done | bytes 262176 | tf_op jit(solution)/shard_map/ppermute | solution.py:342
  373.5 6.9 %collective-permute-done.15.refs_4_ = bf16[8,128,128]{2,1,0:T(8,128)(2,1)S(1)} collective-permute-done((bf16[8,128,128]{2,1,0:T(8,128)(2,1)S(1)}, bf16[8,128,128]{2,1,0:T(8,128)(2,1)S(1)}, u32[]{:S(2)}, u32[]{:S(2)}) %collective-permute-start.15) | collective-permute-done | bytes 262176 | tf_op jit(solution)/shard_map/ppermute | solution.py:342
  395.7 6.9 %collective-permute-done.16.refs_5_ = bf16[8,128,128]{2,1,0:T(8,128)(2,1)S(1)} collective-permute-done((bf16[8,128,128]{2,1,0:T(8,128)(2,1)S(1)}, bf16[8,128,128]{2,1,0:T(8,128)(2,1)S(1)}, u32[]{:S(2)}, u32[]{:S(2)}) %collective-permute-start.16) | collective-permute-done | bytes 262176 | tf_op jit(solution)/shard_map/ppermute | solution.py:342
  419.3 6.9 %collective-permute-done.17.refs_4_ = bf16[8,128,128]{2,1,0:T(8,128)(2,1)S(1)} collective-permute-done((bf16[8,128,128]{2,1,0:T(8,128)(2,1)S(1)}, bf16[8,128,128]{2,1,0:T(8,128)(2,1)S(1)}, u32[]{:S(2)}, u32[]{:S(2)}) %collective-permute-start.17) | collective-permute-done | bytes 262176 | tf_op jit(solution)/shard_map/ppermute | solution.py:342
  442.2 6.9 %collective-permute-done.18.refs_4_ = bf16[8,128,128]{2,1,0:T(8,128)(2,1)S(1)} collective-permute-done((bf16[8,128,128]{2,1,0:T(8,128)(2,1)S(1)}, bf16[8,128,128]{2,1,0:T(8,128)(2,1)S(1)}, u32[]{:S(2)}, u32[]{:S(2)}) %collective-permute-start.18) | collective-permute-done | bytes 262176 | tf_op jit(solution)/shard_map/ppermute | solution.py:342
  491.4 7.0 %collective-permute-done.22 = bf16[8,128,128]{2,1,0:T(8,128)(2,1)S(1)} collective-permute-done((bf16[8,128,128]{2,1,0:T(8,128)(2,1)}, bf16[8,128,128]{2,1,0:T(8,128)(2,1)S(1)}, u32[]{:S(2)}, u32[]{:S(2)}) %collective-permute-start.22) | collective-permute-done | bytes 262176 | tf_op jit(solution)/shard_map/ppermute | solution.py:342
  506.2 7.2 %collective-permute-done.20 = bf16[8,128,128]{2,1,0:T(8,128)(2,1)S(1)} collective-permute-done((bf16[8,128,128]{2,1,0:T(8,128)(2,1)S(1)}, bf16[8,128,128]{2,1,0:T(8,128)(2,1)S(1)}, u32[]{:S(2)}, u32[]{:S(2)}) %collective-permute-start.20) | collective-permute-done | bytes 262176 | tf_op jit(solution)/shard_map/ppermute | solution.py:342
  (290 shorter events, 311.0 us)
Async XLA Ops:
  16.1 20.5 %all-to-all-start = ((bf16[16,64,256]{2,1,0:T(8,128)(2,1)}), bf16[16,64,256]{2,1,0:T(8,128)(2,1)S(1)}, u32[]{:S(2)}, u32[]{:S(2)}) async-start(bf16[16,64,256]{2,1,0:T(8,128)(2,1)} %start_work.1), calls=%async_computation | async-start | bytes 1048576 | tf_op jit(solution)/shard_map/all_to_all | solution.py:317
  39.7 18.7 %all-to-all-start.1 = ((bf16[16,64,256]{2,1,0:T(8,128)(2,1)}), bf16[16,64,256]{2,1,0:T(8,128)(2,1)S(1)}, u32[]{:S(2)}, u32[]{:S(2)}) async-start(bf16[16,64,256]{2,1,0:T(8,128)(2,1)} %copy-done.33), calls=%async_computation.1 | async-start | bytes 1048576 | tf_op jit(solution)/shard_map/all_to_all | solution.py:317
  61.9 18.8 %all-to-all-start.2 = ((bf16[16,64,256]{2,1,0:T(8,128)(2,1)}), bf16[16,64,256]{2,1,0:T(8,128)(2,1)}, u32[]{:S(2)}, u32[]{:S(2)}) async-start(bf16[16,64,256]{2,1,0:T(8,128)(2,1)} %copy-done.34), calls=%async_computation.2 | async-start | bytes 1048576 | tf_op jit(solution)/shard_map/all_to_all | solution.py:317
  83.6 18.5 %all-to-all-start.3 = ((bf16[16,64,256]{2,1,0:T(8,128)(2,1)}), bf16[16,64,256]{2,1,0:T(8,128)(2,1)S(1)}, u32[]{:S(2)}, u32[]{:S(2)}) async-start(bf16[16,64,256]{2,1,0:T(8,128)(2,1)} %copy-done.32), calls=%async_computation.3 | async-start | bytes 1048576 | tf_op jit(solution)/shard_map/all_to_all | solution.py:317
  105.4 27.1 %all-to-all-start.4 = ((bf16[16,128,256]{2,1,0:T(8,128)(2,1)}), bf16[16,128,256]{2,1,0:T(8,128)(2,1)S(1)}, u32[]{:S(2)}, u32[]{:S(2)}) async-start(bf16[16,128,256]{2,1,0:T(8,128)(2,1)} %get-tuple-element.29), calls=%async_computation.4 | async-start | bytes 2097152 | tf_op jit(solution)/shard_map/all_to_all | solution.py:317
  113.7 12.8 %collective-permute-start.7 = (bf16[8,128,128]{2,1,0:T(8,128)(2,1)S(1)}, bf16[8,128,128]{2,1,0:T(8,128)(2,1)S(1)}, u32[]{:S(2)}, u32[]{:S(2)}) collective-permute-start(bf16[8,128,128]{2,1,0:T(8,128)(2,1)S(1)} %copy-done.87), channel_id=1, source_target_pairs={{16,0},{17,1},{18,2},{19,3},{20,4},{21,5},{22,6},{23,7},{24,8},{25... | collective-permute-start | bytes 786440 | tf_op jit(solution)/shard_map/ppermute | solution.py:328
  115.0 16.8 %collective-permute-start.5 = (bf16[8,128,128]{2,1,0:T(8,128)(2,1)S(1)}, bf16[8,128,128]{2,1,0:T(8,128)(2,1)S(1)}, u32[]{:S(2)}, u32[]{:S(2)}) collective-permute-start(bf16[8,128,128]{2,1,0:T(8,128)(2,1)S(1)} %broadcast_select_fusion.6), channel_id=1, source_target_pairs={{0,16},{16,0},{1,17},{17,1},{2,18},{18,2},{3,19},{19,3},{4,20},{20... | collective-permute-start | bytes 786440 | tf_op jit(solution)/shard_map/ppermute | solution.py:327
  138.2 21.3 %all-to-all-start.5 = ((bf16[16,64,256]{2,1,0:T(8,128)(2,1)}), bf16[16,64,256]{2,1,0:T(8,128)(2,1)S(1)}, u32[]{:S(2)}, u32[]{:S(2)}) async-start(bf16[16,64,256]{2,1,0:T(8,128)(2,1)} %copy-done.35), calls=%async_computation.5 | async-start | bytes 1048576 | tf_op jit(solution)/shard_map/all_to_all | solution.py:317
  194.4 19.5 %all-to-all-start.7 = ((bf16[16,64,256]{2,1,0:T(8,128)(2,1)}), bf16[16,64,256]{2,1,0:T(8,128)(2,1)S(1)}, u32[]{:S(2)}, u32[]{:S(2)}) async-start(bf16[16,64,256]{2,1,0:T(8,128)(2,1)} %left_work.8), calls=%async_computation.7 | async-start | bytes 1048576 | tf_op jit(solution)/shard_map/all_to_all | solution.py:317
  218.0 18.7 %all-to-all-start.8 = ((bf16[16,64,256]{2,1,0:T(8,128)(2,1)}), bf16[16,64,256]{2,1,0:T(8,128)(2,1)S(1)}, u32[]{:S(2)}, u32[]{:S(2)}) async-start(bf16[16,64,256]{2,1,0:T(8,128)(2,1)} %copy-done.59), calls=%async_computation.8 | async-start | bytes 1048576 | tf_op jit(solution)/shard_map/all_to_all | solution.py:317
  239.1 18.7 %all-to-all-start.9 = ((bf16[16,64,256]{2,1,0:T(8,128)(2,1)}), bf16[16,64,256]{2,1,0:T(8,128)(2,1)S(1)}, u32[]{:S(2)}, u32[]{:S(2)}) async-start(bf16[16,64,256]{2,1,0:T(8,128)(2,1)} %copy-done.36), calls=%async_computation.9 | async-start | bytes 1048576 | tf_op jit(solution)/shard_map/all_to_all | solution.py:317
  262.6 18.8 %all-to-all-start.10 = ((bf16[16,64,256]{2,1,0:T(8,128)(2,1)}), bf16[16,64,256]{2,1,0:T(8,128)(2,1)}, u32[]{:S(2)}, u32[]{:S(2)}) async-start(bf16[16,64,256]{2,1,0:T(8,128)(2,1)} %copy-done.60), calls=%async_computation.10 | async-start | bytes 1048576 | tf_op jit(solution)/shard_map/all_to_all | solution.py:317
  284.8 27.2 %all-to-all-start.11 = ((bf16[16,128,256]{2,1,0:T(8,128)(2,1)}), bf16[16,128,256]{2,1,0:T(8,128)(2,1)S(1)}, u32[]{:S(2)}, u32[]{:S(2)}) async-start(bf16[16,128,256]{2,1,0:T(8,128)(2,1)} %get-tuple-element.33), calls=%async_computation.11 | async-start | bytes 2097152 | tf_op jit(solution)/shard_map/all_to_all | solution.py:317
  318.2 21.5 %all-to-all-start.12 = ((bf16[16,64,256]{2,1,0:T(8,128)(2,1)}), bf16[16,64,256]{2,1,0:T(8,128)(2,1)S(1)}, u32[]{:S(2)}, u32[]{:S(2)}) async-start(bf16[16,64,256]{2,1,0:T(8,128)(2,1)} %get-tuple-element.36), calls=%async_computation.12 | async-start | bytes 1048576 | tf_op jit(solution)/shard_map/all_to_all | solution.py:317
  343.2 18.6 %all-to-all-start.13 = ((bf16[16,64,256]{2,1,0:T(8,128)(2,1)}), bf16[16,64,256]{2,1,0:T(8,128)(2,1)S(1)}, u32[]{:S(2)}, u32[]{:S(2)}) async-start(bf16[16,64,256]{2,1,0:T(8,128)(2,1)} %get-tuple-element.38), calls=%async_computation.13 | async-start | bytes 1048576 | tf_op jit(solution)/shard_map/all_to_all | solution.py:317
  365.7 18.7 %all-to-all-start.14 = ((bf16[16,64,256]{2,1,0:T(8,128)(2,1)}), bf16[16,64,256]{2,1,0:T(8,128)(2,1)S(1)}, u32[]{:S(2)}, u32[]{:S(2)}) async-start(bf16[16,64,256]{2,1,0:T(8,128)(2,1)} %get-tuple-element.40), calls=%async_computation.14 | async-start | bytes 1048576 | tf_op jit(solution)/shard_map/all_to_all | solution.py:317
  388.0 18.7 %all-to-all-start.15 = ((bf16[16,64,256]{2,1,0:T(8,128)(2,1)}), bf16[16,64,256]{2,1,0:T(8,128)(2,1)S(1)}, u32[]{:S(2)}, u32[]{:S(2)}) async-start(bf16[16,64,256]{2,1,0:T(8,128)(2,1)} %get-tuple-element.42), calls=%async_computation.15 | async-start | bytes 1048576 | tf_op jit(solution)/shard_map/all_to_all | solution.py:317
  411.7 18.7 %all-to-all-start.16 = ((bf16[16,64,256]{2,1,0:T(8,128)(2,1)}), bf16[16,64,256]{2,1,0:T(8,128)(2,1)S(1)}, u32[]{:S(2)}, u32[]{:S(2)}) async-start(bf16[16,64,256]{2,1,0:T(8,128)(2,1)} %get-tuple-element.45), calls=%async_computation.16 | async-start | bytes 1048576 | tf_op jit(solution)/shard_map/all_to_all | solution.py:317
  434.6 18.6 %all-to-all-start.17 = ((bf16[16,64,256]{2,1,0:T(8,128)(2,1)}), bf16[16,64,256]{2,1,0:T(8,128)(2,1)S(1)}, u32[]{:S(2)}, u32[]{:S(2)}) async-start(bf16[16,64,256]{2,1,0:T(8,128)(2,1)} %get-tuple-element.47), calls=%async_computation.17 | async-start | bytes 1048576 | tf_op jit(solution)/shard_map/all_to_all | solution.py:317
  458.5 18.6 %all-to-all-start.18 = ((bf16[16,64,256]{2,1,0:T(8,128)(2,1)}), bf16[16,64,256]{2,1,0:T(8,128)(2,1)S(1)}, u32[]{:S(2)}, u32[]{:S(2)}) async-start(bf16[16,64,256]{2,1,0:T(8,128)(2,1)} %copy-done.58), calls=%async_computation.18 | async-start | bytes 1048576 | tf_op jit(solution)/shard_map/all_to_all | solution.py:317
  462.6 12.2 %collective-permute-start.19 = (bf16[8,128,128]{2,1,0:T(8,128)(2,1)}, bf16[8,128,128]{2,1,0:T(8,128)(2,1)S(1)}, u32[]{:S(2)}, u32[]{:S(2)}) collective-permute-start(bf16[8,128,128]{2,1,0:T(8,128)(2,1)} %copy-done.78), channel_id=1, source_target_pairs={{16,0},{17,1},{18,2},{19,3},{20,4},{21,5},{22,6},{23,7},{24,8},{25... | collective-permute-start | bytes 786440 | tf_op jit(solution)/shard_map/ppermute | solution.py:342
  466.8 20.9 %collective-permute-start.23 = (bf16[8,128,128]{2,1,0:T(8,128)(2,1)}, bf16[8,128,128]{2,1,0:T(8,128)(2,1)}, u32[]{:S(2)}, u32[]{:S(2)}) collective-permute-start(bf16[8,128,128]{2,1,0:T(8,128)(2,1)} %last_outer_work.1), channel_id=1, source_target_pairs={{0,16},{16,0},{1,17},{17,1},{2,18},{18,2},{3,19},{19,3},{4,20},{20... | collective-permute-start | bytes 786440 | tf_op jit(solution)/shard_map/ppermute | solution.py:342
  481.8 19.0 %all-to-all-start.19 = ((bf16[16,64,256]{2,1,0:T(8,128)(2,1)}), bf16[16,64,256]{2,1,0:T(8,128)(2,1)S(1)}, u32[]{:S(2)}, u32[]{:S(2)}) async-start(bf16[16,64,256]{2,1,0:T(8,128)(2,1)} %copy-done.57), calls=%async_computation.19 | async-start | bytes 1048576 | tf_op jit(solution)/shard_map/all_to_all | solution.py:317
  490.1 13.7 %collective-permute-start.21 = (bf16[8,128,128]{2,1,0:T(8,128)(2,1)}, bf16[8,128,128]{2,1,0:T(8,128)(2,1)}, u32[]{:S(2)}, u32[]{:S(2)}) collective-permute-start(bf16[8,128,128]{2,1,0:T(8,128)(2,1)} %get-tuple-element.52), channel_id=1, source_target_pairs={{16,0},{17,1},{18,2},{19,3},{20,4},{21,5},{22,6},{23,7},{24,8},{25... | collective-permute-start | bytes 786440 | tf_op jit(solution)/shard_map/ppermute | solution.py:342
  (108 other events, 865.6 us)

commit v7 on v6

--- a/solution.py
+++ b/solution.py
@@ -146,7 +146,7 @@
     ):
         plan, tokens, picks = self.plan, self.tokens, self.picks
         rows = plan.own * plan.own
-        pieces = 2
+        pieces = 1
         span = plan.own // pieces
         arrays = [value[0] if isinstance(value, tuple) else value for value in ins]
         places = [value[1] if isinstance(value, tuple) else 0 for value in ins]

time: 518 us -> 509 us (0.983)
  starting transfers between devices: 156 us -> 174 us
  waiting for transfers between devices: 218 us -> 203 us
  Pallas kernels: 67.6 us -> 56.9 us
    all_to_all x19, waiting for transfers between devices: 80.5 us -> 64.4 us  [exchange(): return lax.all_to_all(value, 'blk', 0, 0, tiled=True)]
    ppermute x12, starting transfers between devices: 33.7 us -> 48.9 us  [step(): other = lax.ppermute(leave, 'segment', [(1, 0)] if layer == 0 else both)]
    pallas_call x25, Pallas kernels: 67.6 us -> 56.9 us  [run(): pl.pallas_call(kernel, out_shape=outs, in_specs=[pl.BlockSpec(memory_spac...]
  transfers between devices with their start and end apart: 43 -> 43, of which waited for: 41 -> 40; matrix products, arithmetic and copies ran while one was open for 2% -> 2% of each run, Pallas kernels for 3% -> 2%
where the time goes in v7:
time: 509 us; the launch traced here: 507 us
  waiting for transfers between devices  203 us (40%)
  starting transfers between devices  174 us (34%)
  Pallas kernels  56.9 us (11%)
  local copies, waits for them, and re-layouts  30.2 us (6%)
  blocking collectives  29.3 us (6%)
  other arithmetic  8.56 us (2%)
    all_to_all x19, starting transfers between devices, exchange(): return lax.all_to_all(value, 'blk', 0, 0, tiled=True)  89.5 us
    ppermute x12, waiting for transfers between devices, step(): other = lax.ppermute(leave, 'segment', [(1, 0)] if layer == 0 else both)  66.6 us
    all_to_all x19, waiting for transfers between devices, exchange(): return lax.all_to_all(value, 'blk', 0, 0, tiled=True)  64.4 us
    pallas_call x25, Pallas kernels, run(): pl.pallas_call(kernel, out_shape=outs, in_specs=[pl.BlockSpec(memory_spac...  56.9 us
    ppermute x12, starting transfers between devices, step(): other = lax.ppermute(leave, 'segment', [(1, 0)] if layer == 0 else both)  48.9 us
    ppermute x4, waiting for transfers between devices, two_segments(): last = lax.ppermute(factor[1], 'segment', [(1, 0)])  36.4 us
    all_to_all x1, blocking collectives, exchange(): return lax.all_to_all(value, 'blk', 0, 0, tiled=True)  29.3 us
    unnamed x178, local copies, waits for them, and re-layouts  24.2 us
  transfers between devices with their start and end apart: 43, of which 40 were waited for; matrix products, arithmetic and copies ran while one was open for 2% of the time, Pallas kernels for 2%

profile of v7, /device:TPU:0, one launch (start us, length us, event | category | flops | bytes accessed | tf_op | source)
XLA Modules:
  0.0 506.5 jit_solution(10803585633637130050)
XLA Ops:
  15.6 6.0 %all-to-all-start = ((bf16[16,64,256]{2,1,0:T(8,128)(2,1)}), bf16[16,64,256]{2,1,0:T(8,128)(2,1)S(1)}, u32[]{:S(2)}, u32[]{:S(2)}) async-start(bf16[16,64,256]{2,1,0:T(8,128)(2,1)} %start_work.1), calls=%async_computation | async-start | bytes 1048576 | tf_op jit(solution)/shard_map/all_to_all | solution.py:317
  26.8 6.1 %collective-permute-done.1.refs_2_.refs_3_ = bf16[8,128,128]{2,1,0:T(8,128)(2,1)S(1)} collective-permute-done((bf16[8,128,128]{2,1,0:T(8,128)(2,1)S(1)}, bf16[8,128,128]{2,1,0:T(8,128)(2,1)S(1)}, u32[]{:S(2)}, u32[]{:S(2)}) %collective-permute-start.1) | collective-permute-done | bytes 262176 | tf_op jit(solution)/shard_map/ppermute | solution.py:321
  48.1 6.1 %collective-permute-done.2.refs_2_.refs_3_ = bf16[8,128,128]{2,1,0:T(8,128)(2,1)S(1)} collective-permute-done((bf16[8,128,128]{2,1,0:T(8,128)(2,1)S(1)}, bf16[8,128,128]{2,1,0:T(8,128)(2,1)S(1)}, u32[]{:S(2)}, u32[]{:S(2)}) %collective-permute-start.2) | collective-permute-done | bytes 262176 | tf_op jit(solution)/shard_map/ppermute | solution.py:321
  69.9 6.0 %collective-permute-done.3.refs_2_.refs_3_ = bf16[8,128,128]{2,1,0:T(8,128)(2,1)S(1)} collective-permute-done((bf16[8,128,128]{2,1,0:T(8,128)(2,1)S(1)}, bf16[8,128,128]{2,1,0:T(8,128)(2,1)S(1)}, u32[]{:S(2)}, u32[]{:S(2)}) %collective-permute-start.3) | collective-permute-done | bytes 262176 | tf_op jit(solution)/shard_map/ppermute | solution.py:321
  118.7 5.6 %collective-permute-done.7 = bf16[8,128,128]{2,1,0:T(8,128)(2,1)S(1)} collective-permute-done((bf16[8,128,128]{2,1,0:T(8,128)(2,1)S(1)}, bf16[8,128,128]{2,1,0:T(8,128)(2,1)S(1)}, u32[]{:S(2)}, u32[]{:S(2)}) %collective-permute-start.7) | collective-permute-done | bytes 262176 | tf_op jit(solution)/shard_map/ppermute | solution.py:328
  135.6 6.4 %all-to-all-start.5 = ((bf16[16,64,256]{2,1,0:T(8,128)(2,1)}), bf16[16,64,256]{2,1,0:T(8,128)(2,1)S(1)}, u32[]{:S(2)}, u32[]{:S(2)}) async-start(bf16[16,64,256]{2,1,0:T(8,128)(2,1)} %copy-done.35), calls=%async_computation.5 | async-start | bytes 1048576 | tf_op jit(solution)/shard_map/all_to_all | solution.py:317
  158.6 29.3 %all_to_all.100.refs_0_.refs_1_ = bf16[16,128,256]{2,1,0:T(8,128)(2,1)} all-to-all(bf16[16,128,256]{2,1,0:T(8,128)(2,1)} %gelu_work.4), channel_id=1, replica_groups=mesh['segment'=2,'blk'=16] {'blk'}, dimensions={0} | all-to-all | bytes 2097152 | tf_op jit(solution)/shard_map/all_to_all | solution.py:317
  196.8 10.2 %collective-permute-done.9 = bf16[8,128,128]{2,1,0:T(8,128)(2,1)S(1)} collective-permute-done((bf16[8,128,128]{2,1,0:T(8,128)(2,1)S(1)}, bf16[8,128,128]{2,1,0:T(8,128)(2,1)S(1)}, u32[]{:S(2)}, u32[]{:S(2)}) %collective-permute-start.9) | collective-permute-done | bytes 262176 | tf_op jit(solution)/shard_map/ppermute | solution.py:328
  219.3 10.3 %collective-permute-done.10 = bf16[8,128,128]{2,1,0:T(8,128)(2,1)S(1)} collective-permute-done((bf16[8,128,128]{2,1,0:T(8,128)(2,1)S(1)}, bf16[8,128,128]{2,1,0:T(8,128)(2,1)S(1)}, u32[]{:S(2)}, u32[]{:S(2)}) %collective-permute-start.10) | collective-permute-done | bytes 262176 | tf_op jit(solution)/shard_map/ppermute | solution.py:328
  239.9 10.3 %collective-permute-done.11 = bf16[8,128,128]{2,1,0:T(8,128)(2,1)S(1)} collective-permute-done((bf16[8,128,128]{2,1,0:T(8,128)(2,1)S(1)}, bf16[8,128,128]{2,1,0:T(8,128)(2,1)S(1)}, u32[]{:S(2)}, u32[]{:S(2)}) %collective-permute-start.11) | collective-permute-done | bytes 262176 | tf_op jit(solution)/shard_map/ppermute | solution.py:328
  263.6 12.2 %all-to-all-done.10.refs_0_ = bf16[16,64,256]{2,1,0:T(8,128)(2,1)} async-done(((bf16[16,64,256]{2,1,0:T(8,128)(2,1)}), bf16[16,64,256]{2,1,0:T(8,128)(2,1)}, u32[]{:S(2)}, u32[]{:S(2)}) %all-to-all-start.10) | async-done | bytes 524320 | tf_op jit(solution)/shard_map/all_to_all | solution.py:317
  287.9 6.9 %collective-permute-done.12.refs_5_ = bf16[8,128,128]{2,1,0:T(8,128)(2,1)S(1)} collective-permute-done((bf16[8,128,128]{2,1,0:T(8,128)(2,1)S(1)}, bf16[8,128,128]{2,1,0:T(8,128)(2,1)S(1)}, u32[]{:S(2)}, u32[]{:S(2)}) %collective-permute-start.12) | collective-permute-done | bytes 262176 | tf_op jit(solution)/shard_map/ppermute | solution.py:342
  294.8 10.8 %all-to-all-done.11.refs_0_.refs_1_ = bf16[16,128,256]{2,1,0:T(8,128)(2,1)S(1)} async-done(((bf16[16,128,256]{2,1,0:T(8,128)(2,1)}), bf16[16,128,256]{2,1,0:T(8,128)(2,1)S(1)}, u32[]{:S(2)}, u32[]{:S(2)}) %all-to-all-start.11) | async-done | bytes 1048608 | tf_op jit(solution)/shard_map/all_to_all | solution.py:317
  311.3 7.0 %all-to-all-start.12 = ((bf16[16,64,256]{2,1,0:T(8,128)(2,1)}), bf16[16,64,256]{2,1,0:T(8,128)(2,1)S(1)}, u32[]{:S(2)}, u32[]{:S(2)}) async-start(bf16[16,64,256]{2,1,0:T(8,128)(2,1)} %get-tuple-element.36), calls=%async_computation.12 | async-start | bytes 1048576 | tf_op jit(solution)/shard_map/all_to_all | solution.py:317
  323.7 6.9 %collective-permute-done.13.refs_4_ = bf16[8,128,128]{2,1,0:T(8,128)(2,1)S(1)} collective-permute-done((bf16[8,128,128]{2,1,0:T(8,128)(2,1)S(1)}, bf16[8,128,128]{2,1,0:T(8,128)(2,1)S(1)}, u32[]{:S(2)}, u32[]{:S(2)}) %collective-permute-start.13) | collective-permute-done | bytes 262176 | tf_op jit(solution)/shard_map/ppermute | solution.py:342
  345.4 6.9 %collective-permute-done.14.refs_4_ = bf16[8,128,128]{2,1,0:T(8,128)(2,1)S(1)} collective-permute-done((bf16[8,128,128]{2,1,0:T(8,128)(2,1)S(1)}, bf16[8,128,128]{2,1,0:T(8,128)(2,1)S(1)}, u32[]{:S(2)}, u32[]{:S(2)}) %collective-permute-start.14) | collective-permute-done | bytes 262176 | tf_op jit(solution)/shard_map/ppermute | solution.py:342
  367.6 6.9 %collective-permute-done.15.refs_4_ = bf16[8,128,128]{2,1,0:T(8,128)(2,1)S(1)} collective-permute-done((bf16[8,128,128]{2,1,0:T(8,128)(2,1)S(1)}, bf16[8,128,128]{2,1,0:T(8,128)(2,1)S(1)}, u32[]{:S(2)}, u32[]{:S(2)}) %collective-permute-start.15) | collective-permute-done | bytes 262176 | tf_op jit(solution)/shard_map/ppermute | solution.py:342
  389.5 6.9 %collective-permute-done.16.refs_5_ = bf16[8,128,128]{2,1,0:T(8,128)(2,1)S(1)} collective-permute-done((bf16[8,128,128]{2,1,0:T(8,128)(2,1)S(1)}, bf16[8,128,128]{2,1,0:T(8,128)(2,1)S(1)}, u32[]{:S(2)}, u32[]{:S(2)}) %collective-permute-start.16) | collective-permute-done | bytes 262176 | tf_op jit(solution)/shard_map/ppermute | solution.py:342
  407.3 5.6 %collective-permute-start.17 = (bf16[8,128,128]{2,1,0:T(8,128)(2,1)S(1)}, bf16[8,128,128]{2,1,0:T(8,128)(2,1)S(1)}, u32[]{:S(2)}, u32[]{:S(2)}) collective-permute-start(bf16[8,128,128]{2,1,0:T(8,128)(2,1)S(1)} %get-tuple-element.46), channel_id=1, source_target_pairs={{0,16},{16,0},{1,17},{17,1},{2,18},{18,2},{3,19},{19,3},{4,20},{20... | collective-permute-start | bytes 786440 | tf_op jit(solution)/shard_map/ppermute | solution.py:342
  412.9 6.9 %collective-permute-done.17.refs_4_ = bf16[8,128,128]{2,1,0:T(8,128)(2,1)S(1)} collective-permute-done((bf16[8,128,128]{2,1,0:T(8,128)(2,1)S(1)}, bf16[8,128,128]{2,1,0:T(8,128)(2,1)S(1)}, u32[]{:S(2)}, u32[]{:S(2)}) %collective-permute-start.17) | collective-permute-done | bytes 262176 | tf_op jit(solution)/shard_map/ppermute | solution.py:342
  435.2 6.9 %collective-permute-done.18.refs_4_ = bf16[8,128,128]{2,1,0:T(8,128)(2,1)S(1)} collective-permute-done((bf16[8,128,128]{2,1,0:T(8,128)(2,1)S(1)}, bf16[8,128,128]{2,1,0:T(8,128)(2,1)S(1)}, u32[]{:S(2)}, u32[]{:S(2)}) %collective-permute-start.18) | collective-permute-done | bytes 262176 | tf_op jit(solution)/shard_map/ppermute | solution.py:342
  472.9 6.1 %all-to-all-start.19 = ((bf16[16,64,256]{2,1,0:T(8,128)(2,1)}), bf16[16,64,256]{2,1,0:T(8,128)(2,1)S(1)}, u32[]{:S(2)}, u32[]{:S(2)}) async-start(bf16[16,64,256]{2,1,0:T(8,128)(2,1)} %copy-done.57), calls=%async_computation.19 | async-start | bytes 1048576 | tf_op jit(solution)/shard_map/all_to_all | solution.py:317
  484.0 6.7 %collective-permute-done.22 = bf16[8,128,128]{2,1,0:T(8,128)(2,1)S(1)} collective-permute-done((bf16[8,128,128]{2,1,0:T(8,128)(2,1)}, bf16[8,128,128]{2,1,0:T(8,128)(2,1)S(1)}, u32[]{:S(2)}, u32[]{:S(2)}) %collective-permute-start.22) | collective-permute-done | bytes 262176 | tf_op jit(solution)/shard_map/ppermute | solution.py:342
  498.5 6.7 %collective-permute-done.20 = bf16[8,128,128]{2,1,0:T(8,128)(2,1)S(1)} collective-permute-done((bf16[8,128,128]{2,1,0:T(8,128)(2,1)S(1)}, bf16[8,128,128]{2,1,0:T(8,128)(2,1)S(1)}, u32[]{:S(2)}, u32[]{:S(2)}) %collective-permute-start.20) | collective-permute-done | bytes 262176 | tf_op jit(solution)/shard_map/ppermute | solution.py:342
  (290 shorter events, 302.4 us)
Async XLA Ops:
  15.6 20.5 %all-to-all-start = ((bf16[16,64,256]{2,1,0:T(8,128)(2,1)}), bf16[16,64,256]{2,1,0:T(8,128)(2,1)S(1)}, u32[]{:S(2)}, u32[]{:S(2)}) async-start(bf16[16,64,256]{2,1,0:T(8,128)(2,1)} %start_work.1), calls=%async_computation | async-start | bytes 1048576 | tf_op jit(solution)/shard_map/all_to_all | solution.py:317
  38.7 18.7 %all-to-all-start.1 = ((bf16[16,64,256]{2,1,0:T(8,128)(2,1)}), bf16[16,64,256]{2,1,0:T(8,128)(2,1)S(1)}, u32[]{:S(2)}, u32[]{:S(2)}) async-start(bf16[16,64,256]{2,1,0:T(8,128)(2,1)} %copy-done.33), calls=%async_computation.1 | async-start | bytes 1048576 | tf_op jit(solution)/shard_map/all_to_all | solution.py:317
  60.4 18.8 %all-to-all-start.2 = ((bf16[16,64,256]{2,1,0:T(8,128)(2,1)}), bf16[16,64,256]{2,1,0:T(8,128)(2,1)}, u32[]{:S(2)}, u32[]{:S(2)}) async-start(bf16[16,64,256]{2,1,0:T(8,128)(2,1)} %copy-done.34), calls=%async_computation.2 | async-start | bytes 1048576 | tf_op jit(solution)/shard_map/all_to_all | solution.py:317
  81.6 18.5 %all-to-all-start.3 = ((bf16[16,64,256]{2,1,0:T(8,128)(2,1)}), bf16[16,64,256]{2,1,0:T(8,128)(2,1)S(1)}, u32[]{:S(2)}, u32[]{:S(2)}) async-start(bf16[16,64,256]{2,1,0:T(8,128)(2,1)} %copy-done.32), calls=%async_computation.3 | async-start | bytes 1048576 | tf_op jit(solution)/shard_map/all_to_all | solution.py:317
  102.9 27.5 %all-to-all-start.4 = ((bf16[16,128,256]{2,1,0:T(8,128)(2,1)}), bf16[16,128,256]{2,1,0:T(8,128)(2,1)S(1)}, u32[]{:S(2)}, u32[]{:S(2)}) async-start(bf16[16,128,256]{2,1,0:T(8,128)(2,1)} %get-tuple-element.29), calls=%async_computation.4 | async-start | bytes 2097152 | tf_op jit(solution)/shard_map/all_to_all | solution.py:317
  111.6 12.8 %collective-permute-start.7 = (bf16[8,128,128]{2,1,0:T(8,128)(2,1)S(1)}, bf16[8,128,128]{2,1,0:T(8,128)(2,1)S(1)}, u32[]{:S(2)}, u32[]{:S(2)}) collective-permute-start(bf16[8,128,128]{2,1,0:T(8,128)(2,1)S(1)} %copy-done.87), channel_id=1, source_target_pairs={{16,0},{17,1},{18,2},{19,3},{20,4},{21,5},{22,6},{23,7},{24,8},{25... | collective-permute-start | bytes 786440 | tf_op jit(solution)/shard_map/ppermute | solution.py:328
  112.9 16.8 %collective-permute-start.5 = (bf16[8,128,128]{2,1,0:T(8,128)(2,1)S(1)}, bf16[8,128,128]{2,1,0:T(8,128)(2,1)S(1)}, u32[]{:S(2)}, u32[]{:S(2)}) collective-permute-start(bf16[8,128,128]{2,1,0:T(8,128)(2,1)S(1)} %broadcast_select_fusion.6), channel_id=1, source_target_pairs={{0,16},{16,0},{1,17},{17,1},{2,18},{18,2},{3,19},{19,3},{4,20},{20... | collective-permute-start | bytes 786440 | tf_op jit(solution)/shard_map/ppermute | solution.py:327
  135.6 20.9 %all-to-all-start.5 = ((bf16[16,64,256]{2,1,0:T(8,128)(2,1)}), bf16[16,64,256]{2,1,0:T(8,128)(2,1)S(1)}, u32[]{:S(2)}, u32[]{:S(2)}) async-start(bf16[16,64,256]{2,1,0:T(8,128)(2,1)} %copy-done.35), calls=%async_computation.5 | async-start | bytes 1048576 | tf_op jit(solution)/shard_map/all_to_all | solution.py:317
  190.5 19.5 %all-to-all-start.7 = ((bf16[16,64,256]{2,1,0:T(8,128)(2,1)}), bf16[16,64,256]{2,1,0:T(8,128)(2,1)S(1)}, u32[]{:S(2)}, u32[]{:S(2)}) async-start(bf16[16,64,256]{2,1,0:T(8,128)(2,1)} %left_work.8), calls=%async_computation.7 | async-start | bytes 1048576 | tf_op jit(solution)/shard_map/all_to_all | solution.py:317
  213.8 18.7 %all-to-all-start.8 = ((bf16[16,64,256]{2,1,0:T(8,128)(2,1)}), bf16[16,64,256]{2,1,0:T(8,128)(2,1)S(1)}, u32[]{:S(2)}, u32[]{:S(2)}) async-start(bf16[16,64,256]{2,1,0:T(8,128)(2,1)} %copy-done.59), calls=%async_computation.8 | async-start | bytes 1048576 | tf_op jit(solution)/shard_map/all_to_all | solution.py:317
  234.4 18.7 %all-to-all-start.9 = ((bf16[16,64,256]{2,1,0:T(8,128)(2,1)}), bf16[16,64,256]{2,1,0:T(8,128)(2,1)S(1)}, u32[]{:S(2)}, u32[]{:S(2)}) async-start(bf16[16,64,256]{2,1,0:T(8,128)(2,1)} %copy-done.36), calls=%async_computation.9 | async-start | bytes 1048576 | tf_op jit(solution)/shard_map/all_to_all | solution.py:317
  257.0 18.8 %all-to-all-start.10 = ((bf16[16,64,256]{2,1,0:T(8,128)(2,1)}), bf16[16,64,256]{2,1,0:T(8,128)(2,1)}, u32[]{:S(2)}, u32[]{:S(2)}) async-start(bf16[16,64,256]{2,1,0:T(8,128)(2,1)} %copy-done.60), calls=%async_computation.10 | async-start | bytes 1048576 | tf_op jit(solution)/shard_map/all_to_all | solution.py:317
  278.4 27.2 %all-to-all-start.11 = ((bf16[16,128,256]{2,1,0:T(8,128)(2,1)}), bf16[16,128,256]{2,1,0:T(8,128)(2,1)S(1)}, u32[]{:S(2)}, u32[]{:S(2)}) async-start(bf16[16,128,256]{2,1,0:T(8,128)(2,1)} %get-tuple-element.33), calls=%async_computation.11 | async-start | bytes 2097152 | tf_op jit(solution)/shard_map/all_to_all | solution.py:317
  311.3 21.5 %all-to-all-start.12 = ((bf16[16,64,256]{2,1,0:T(8,128)(2,1)}), bf16[16,64,256]{2,1,0:T(8,128)(2,1)S(1)}, u32[]{:S(2)}, u32[]{:S(2)}) async-start(bf16[16,64,256]{2,1,0:T(8,128)(2,1)} %get-tuple-element.36), calls=%async_computation.12 | async-start | bytes 1048576 | tf_op jit(solution)/shard_map/all_to_all | solution.py:317
  335.8 18.6 %all-to-all-start.13 = ((bf16[16,64,256]{2,1,0:T(8,128)(2,1)}), bf16[16,64,256]{2,1,0:T(8,128)(2,1)S(1)}, u32[]{:S(2)}, u32[]{:S(2)}) async-start(bf16[16,64,256]{2,1,0:T(8,128)(2,1)} %get-tuple-element.38), calls=%async_computation.13 | async-start | bytes 1048576 | tf_op jit(solution)/shard_map/all_to_all | solution.py:317
  357.9 18.7 %all-to-all-start.14 = ((bf16[16,64,256]{2,1,0:T(8,128)(2,1)}), bf16[16,64,256]{2,1,0:T(8,128)(2,1)S(1)}, u32[]{:S(2)}, u32[]{:S(2)}) async-start(bf16[16,64,256]{2,1,0:T(8,128)(2,1)} %get-tuple-element.40), calls=%async_computation.14 | async-start | bytes 1048576 | tf_op jit(solution)/shard_map/all_to_all | solution.py:317
  379.7 18.7 %all-to-all-start.15 = ((bf16[16,64,256]{2,1,0:T(8,128)(2,1)}), bf16[16,64,256]{2,1,0:T(8,128)(2,1)S(1)}, u32[]{:S(2)}, u32[]{:S(2)}) async-start(bf16[16,64,256]{2,1,0:T(8,128)(2,1)} %get-tuple-element.42), calls=%async_computation.15 | async-start | bytes 1048576 | tf_op jit(solution)/shard_map/all_to_all | solution.py:317
  403.1 18.7 %all-to-all-start.16 = ((bf16[16,64,256]{2,1,0:T(8,128)(2,1)}), bf16[16,64,256]{2,1,0:T(8,128)(2,1)S(1)}, u32[]{:S(2)}, u32[]{:S(2)}) async-start(bf16[16,64,256]{2,1,0:T(8,128)(2,1)} %get-tuple-element.45), calls=%async_computation.16 | async-start | bytes 1048576 | tf_op jit(solution)/shard_map/all_to_all | solution.py:317
  425.6 18.6 %all-to-all-start.17 = ((bf16[16,64,256]{2,1,0:T(8,128)(2,1)}), bf16[16,64,256]{2,1,0:T(8,128)(2,1)S(1)}, u32[]{:S(2)}, u32[]{:S(2)}) async-start(bf16[16,64,256]{2,1,0:T(8,128)(2,1)} %get-tuple-element.47), calls=%async_computation.17 | async-start | bytes 1048576 | tf_op jit(solution)/shard_map/all_to_all | solution.py:317
  449.2 19.0 %all-to-all-start.18 = ((bf16[16,64,256]{2,1,0:T(8,128)(2,1)}), bf16[16,64,256]{2,1,0:T(8,128)(2,1)S(1)}, u32[]{:S(2)}, u32[]{:S(2)}) async-start(bf16[16,64,256]{2,1,0:T(8,128)(2,1)} %copy-done.58), calls=%async_computation.18 | async-start | bytes 1048576 | tf_op jit(solution)/shard_map/all_to_all | solution.py:317
  453.3 14.2 %collective-permute-start.19 = (bf16[8,128,128]{2,1,0:T(8,128)(2,1)}, bf16[8,128,128]{2,1,0:T(8,128)(2,1)S(1)}, u32[]{:S(2)}, u32[]{:S(2)}) collective-permute-start(bf16[8,128,128]{2,1,0:T(8,128)(2,1)} %copy-done.78), channel_id=1, source_target_pairs={{16,0},{17,1},{18,2},{19,3},{20,4},{21,5},{22,6},{23,7},{24,8},{25... | collective-permute-start | bytes 786440 | tf_op jit(solution)/shard_map/ppermute | solution.py:342
  457.4 22.9 %collective-permute-start.23 = (bf16[8,128,128]{2,1,0:T(8,128)(2,1)}, bf16[8,128,128]{2,1,0:T(8,128)(2,1)}, u32[]{:S(2)}, u32[]{:S(2)}) collective-permute-start(bf16[8,128,128]{2,1,0:T(8,128)(2,1)} %last_outer_work.1), channel_id=1, source_target_pairs={{0,16},{16,0},{1,17},{17,1},{2,18},{18,2},{3,19},{19,3},{4,20},{20... | collective-permute-start | bytes 786440 | tf_op jit(solution)/shard_map/ppermute | solution.py:342
  472.9 20.6 %all-to-all-start.19 = ((bf16[16,64,256]{2,1,0:T(8,128)(2,1)}), bf16[16,64,256]{2,1,0:T(8,128)(2,1)S(1)}, u32[]{:S(2)}, u32[]{:S(2)}) async-start(bf16[16,64,256]{2,1,0:T(8,128)(2,1)} %copy-done.57), calls=%async_computation.19 | async-start | bytes 1048576 | tf_op jit(solution)/shard_map/all_to_all | solution.py:317
  482.7 13.4 %collective-permute-start.21 = (bf16[8,128,128]{2,1,0:T(8,128)(2,1)}, bf16[8,128,128]{2,1,0:T(8,128)(2,1)}, u32[]{:S(2)}, u32[]{:S(2)}) collective-permute-start(bf16[8,128,128]{2,1,0:T(8,128)(2,1)} %get-tuple-element.52), channel_id=1, source_target_pairs={{16,0},{17,1},{18,2},{19,3},{20,4},{21,5},{22,6},{23,7},{24,8},{25... | collective-permute-start | bytes 786440 | tf_op jit(solution)/shard_map/ppermute | solution.py:342
  (108 other events, 871.5 us)
